TPU v7x, 32 devices: a whole 2x2x4 slice. The times are simulated.
32 devices in a mesh: gx: 4 (over y, core), gy: 4 (over z), gz: 2 (over x).
Axes of the slice: x: 2, y: 2, z: 4, core: 2. Of those that a mesh axis runs over, the one named last changes fastest.
Arguments:
- positions: float32 [3, 4096], P(None, ('gx', 'gy', 'gz')), may hold values from -8 to 8
- atom_features: float32 [4096, 128], P(('gx', 'gy', 'gz')), may hold values from -6 to 6
- send_face: int32 [32, 6, 32], P(('gx', 'gy', 'gz')), may hold values from 0 to 127
- send_edge: int32 [32, 12, 8], P(('gx', 'gy', 'gz')), may hold values from 0 to 127
- send_corner: int32 [32, 8, 2], P(('gx', 'gy', 'gz')), may hold values from 0 to 127
- centre: int32 [196608], P(('gx', 'gy', 'gz')), may hold values from 0 to 127
- other: int32 [196608], P(('gx', 'gy', 'gz')), may hold values from 0 to 431
- edge_count: int32 [32], P(('gx', 'gy', 'gz')), may hold values from 1536 to 6144, as said below
- w_proj_a: float32 [128, 128], replicated, may hold values from -0.5 to 0.5
- w_proj_b: float32 [128, 128], replicated, may hold values from -0.5 to 0.5
- w_radial: float32 [8, 128], replicated, may hold values from -2 to 2
- w_first: bfloat16 [128, 128], replicated, may hold values from -0.5 to 0.5
- w_env: bfloat16 [128, 128], replicated, may hold values from -0.5 to 0.5
- w_value: bfloat16 [128, 128], replicated, may hold values from -0.5 to 0.5
- w_second: bfloat16 [256, 128], replicated, may hold values from -0.375 to 0.375
- w_out: bfloat16 [128], replicated, may hold values from -0.5 to 0.5
Outputs:
- forces: float32 [3, 4096], P(None, ('gx', 'gy', 'gz'))
- atom_energy: float32 [4096], P(('gx', 'gy', 'gz'))
- feature_grad: float32 [4096, 128], P(('gx', 'gy', 'gz'))
Inputs may be any that keep to these rules, and one draw needn't show every extreme that they name: `edge_count`: some domain has exactly 6144 live edges in every draw.
All inputs are finite; a program needn't handle non-finite values.
Results may differ from a plain program's by a relative error of at most 0.035.
Values sent between devices are 32-bit elements; how exact they have to be, the bound alone decides.
No kernel may reach another device: no remote copies, remote signals or barrier semaphores. Data moves between devices by JAX's collectives and lax.ppermute only.
A program may use at most 192 MiB of HBM per device.

v0:
```python
import math

import jax
import jax.numpy as jnp
from jax import lax
from jax.experimental import pallas as pl
from jax.experimental.pallas import tpu as pltpu
from jax.sharding import PartitionSpec as P

F32 = jnp.float32
BF16 = jnp.bfloat16
HIGH = lax.Precision.HIGHEST
AXES = ("gx", "gy", "gz")
CHUNK = 2048
SUB = 256
WIN = 16
OTHER_BITS = 9
OTHER_MASK = (1 << OTHER_BITS) - 1
LANES = 128
ROOT3 = 1.732


VMEM = pl.BlockSpec(memory_space=pltpu.VMEM)
SMEM = pl.BlockSpec(memory_space=pltpu.SMEM)
PARAMS = pltpu.CompilerParams(vmem_limit_bytes=52 * 2**20)


def shape(*dims, dtype=F32):
    return jax.ShapeDtypeStruct(dims, dtype)


def dot_nn(a, b, precision=None):
    return lax.dot_general(
        a, b, (((1,), (0,)), ((), ())), preferred_element_type=F32, precision=precision
    )


def dot_nt(a, b, precision=None):
    return lax.dot_general(
        a, b, (((1,), (1,)), ((), ())), preferred_element_type=F32, precision=precision
    )


def dot_tn(a, b, precision=None):
    return lax.dot_general(
        a, b, (((0,), (0,)), ((), ())), preferred_element_type=F32, precision=precision
    )


def offset_classes():
    classes = [[], [], []]
    for a in (-1, 0, 1):
        for b in (-1, 0, 1):
            for c in (-1, 0, 1):
                if (a, b, c) != (0, 0, 0):
                    classes[abs(a) + abs(b) + abs(c) - 1].append((a, b, c))
    return classes


CLASSES = offset_classes()


OFFSETS = [off for group in CLASSES for off in group]


def kind(off):
    return abs(off[0]) + abs(off[1]) + abs(off[2]) - 1


class Plan:
    def __init__(self, widths, sizes):
        self.widths = widths
        self.sizes = sizes
        self.groups = [self.group(a) for a in range(3)]
        self.own_rest = [off for off in OFFSETS if off[2] == 0]
        self.held_rest = [off for off in OFFSETS if off[0] == 0]

    def group(self, a):
        groups = {}
        for off in OFFSETS:
            if off[a] != 0:
                groups.setdefault(off[a] % self.sizes[a], []).append(off)
        return list(groups.values())

    def live(self, off):
        return self.widths[kind(off)]

    def rows(self, off):
        return self.live(off) + 1

    def total(self, blocks):
        return sum(self.rows(off) for off in blocks)

    def spans(self, blocks):
        at = 0
        for off in blocks:
            yield off, at
            at += self.rows(off)

    def place(self, a, off):
        for g, blocks in enumerate(self.groups[a]):
            if off in blocks:
                return g, dict(self.spans(blocks))[off]
        raise KeyError(off)

    def find(self, came, axes, rest_ref, rest, off):
        for a in axes:
            if off[a] != 0:
                g, begin = self.place(a, off)
                return came[a][g], begin
        return rest_ref, dict(self.spans(rest))[off]

    def cut(self, refs, *axes):
        came = {}
        for a in axes:
            n = len(self.groups[a])
            came[a], refs = refs[:n], refs[n:]
        return came, refs

    def shapes(self, a, chans):
        return [shape(self.total(blocks), chans) for blocks in self.groups[a]]

    def send(self, a, messages, back=False):
        n = self.sizes[a]
        got = []
        for blocks, message in zip(self.groups[a], messages):
            step = -blocks[0][a] if back else blocks[0][a]
            got.append(lax.ppermute(message, AXES[a], [(i, (i + step) % n) for i in range(n)]))
        return got


GROUP = 32


def group_rows(count):
    row = lax.broadcasted_iota(jnp.int32, (count, LANES), 0)
    group = lax.broadcasted_iota(jnp.int32, (count, LANES), 1) // GROUP
    return (row == group).astype(F32) * (group < 3).astype(F32)


def diagonal(x):
    row = lax.broadcasted_iota(jnp.int32, x.shape, 0)
    lane = lax.broadcasted_iota(jnp.int32, x.shape, 1)
    return jnp.where((lane & (GROUP - 1)) == row, x, 0.0)


def spread(row, live):
    return diagonal(jnp.broadcast_to(row, (live, LANES)))


def split(x):
    high = x.astype(BF16).astype(F32)
    return high, x - high


def dot_exact(hot, x, dims):
    high, low = split(x)
    both = jnp.concatenate([high, low], axis=1).astype(BF16)
    out = lax.dot_general(hot, both, (dims, ((), ())), preferred_element_type=F32)
    return out[:, 0 : x.shape[1]] + out[:, x.shape[1] :]


def prep_kernel(plan, rows_ref, list_ref, *outs):
    n_z = len(plan.groups[2])
    sends, rest_ref, sel_ref, turn_ref = outs[:n_z], outs[n_z], outs[n_z + 1], outs[n_z + 2]
    own = sel_ref.shape[1]
    lane = lax.broadcasted_iota(jnp.int32, (1, own), 1)
    turn_ref[...] = jnp.zeros_like(turn_ref)
    turn_ref[0 : list_ref.shape[0], 0 : list_ref.shape[1]] = list_ref[...]
    columns = turn_ref[...].T
    sel_ref[...] = jnp.zeros_like(sel_ref)
    messages = plan.groups[2] + [plan.own_rest]
    at = 0
    for blocks in messages:
        for off, begin in plan.spans(blocks):
            key = OFFSETS.index(off)
            live = plan.live(off)
            column = columns[0:live, key : key + 1]
            sel_ref[at + begin : at + begin + live, :] = (column == lane).astype(F32)
        at += plan.total(blocks)
    pos = dot_tn(rows_ref[own : own + 3, :], group_rows(3), HIGH)
    sel = sel_ref[...]
    rows = dot_nn(sel, rows_ref[0:own, :], HIGH)
    places = dot_nn(sel, pos, HIGH)
    at = 0
    for blocks, send in zip(messages, tuple(sends) + (rest_ref,)):
        count = plan.total(blocks)
        send[...] = rows[at : at + count, :]
        for off, begin in plan.spans(blocks):
            live = plan.live(off)
            block = places[at + begin : at + begin + live, :]
            send[begin + live : begin + live + 1, :] = jnp.sum(
                diagonal(block), axis=0, keepdims=True
            )
        at += count


def glue_kernel(plan, a, axes, rest, *refs):
    rest_ref = refs[0]
    came, outs = plan.cut(refs[1:], *axes)
    for blocks, out in zip(plan.groups[a], outs):
        for off, row in plan.spans(blocks):
            src, begin = plan.find(came, axes, rest_ref, rest, off)
            out[row : row + plan.rows(off), :] = src[begin : begin + plan.rows(off), :]


def glue(plan, a, axes, rest, rest_rows, came):
    given = [rest_rows] + [message for axis in axes for message in came[axis]]
    outs = plan.shapes(a, rest_rows.shape[1])
    return pl.pallas_call(
        lambda *refs: glue_kernel(plan, a, axes, rest, *refs),
        out_shape=outs,
        in_specs=[VMEM] * len(given),
        out_specs=[VMEM] * len(outs),
        compiler_params=PARAMS,
    )(*given)


def sort_kernel(dead, count_ref, centre_ref, other_ref, key_ref, bound_ref, turn_ref):
    rows = centre_ref.shape[0]
    regs = turn_ref.shape[0] // 16
    group = regs * 8
    row = lax.broadcasted_iota(jnp.int32, (rows, LANES), 0)
    lane = lax.broadcasted_iota(jnp.int32, (rows, LANES), 1)
    key = jnp.where(
        row * LANES + lane < count_ref[0], (centre_ref[...] << OTHER_BITS) + other_ref[...], dead
    ).astype(F32)
    x = [key[8 * v : 8 * v + 8, :] for v in range(rows // 8)]
    x += [jnp.full((8, LANES), float(dead), F32)] * (regs - len(x))
    s = lax.broadcasted_iota(jnp.int32, (8, LANES), 0)
    ln = lax.broadcasted_iota(jnp.int32, (8, LANES), 1)
    base = ln * group + s * regs

    def sign(k, v):
        return jnp.where(((base + v) & k) == 0, 1.0, -1.0).astype(F32)

    last = [jnp.ones((8, LANES), F32)] * regs
    total = group * LANES
    k = 2
    while k <= total:
        signs = [sign(k, v) for v in range(regs)] if k < total else [1.0] * regs
        x = [x[v] * (last[v] * signs[v]) for v in range(regs)]
        last = signs
        j = k // 2
        while j >= 1:
            if j < regs:
                for v in range(regs):
                    if v & j == 0:
                        a, b = x[v], x[v | j]
                        x[v], x[v | j] = jnp.minimum(a, b), jnp.maximum(a, b)
            else:
                axis, step, size, ids = (
                    (0, j // regs, 8, s) if j < group else (1, j // group, LANES, ln)
                )
                low = (ids & step) == 0
                for v in range(regs):
                    up = pltpu.roll(x[v], size - step, axis)
                    if 2 * step == size:
                        mate = up
                    else:
                        mate = jnp.where(low, up, pltpu.roll(x[v], step, axis))
                    x[v] = jnp.where(low, jnp.minimum(x[v], mate), jnp.maximum(x[v], mate))
            j //= 2
        k *= 2
    least = x[0]
    most = jnp.where(x[0] == float(dead), -1.0, x[0])
    for v in range(1, regs):
        least = jnp.minimum(least, x[v])
        most = jnp.maximum(most, jnp.where(x[v] == float(dead), -1.0, x[v]))
    bound_ref[0:1, :] = jnp.min(least, axis=0, keepdims=True).astype(jnp.int32) >> OTHER_BITS
    bound_ref[1:2, :] = jnp.max(most, axis=0, keepdims=True).astype(jnp.int32) >> OTHER_BITS
    turned = jnp.concatenate(x + [jnp.zeros((LANES - group, LANES), F32)], axis=0).T
    turn_ref[...] = turned
    ratio = LANES // group
    parts = [
        turn_ref[pl.ds(i, rows, stride=ratio), 0:group] for i in range(ratio)
    ]
    done = jnp.concatenate(parts, axis=1).astype(jnp.int32)
    per = key_ref.shape[1]
    for c in range(key_ref.shape[0]):
        key_ref[c] = done[c * per : (c + 1) * per, :]


def weight_kernel(
    rows_ref,
    wide_ref,
    half_ref,
    tab_ref,
    w1t_ref,
    wevt_ref,
    w2t_ref,
    w1_ref,
    wev_ref,
    w2_ref,
    wradb_ref,
    wcol_ref,
):
    chans = wide_ref.shape[1]
    own = rows_ref.shape[0] - 3
    wa, wb, rad = wide_ref[0:chans, :], wide_ref[chans : 2 * chans, :], wide_ref[2 * chans :, :]
    w1, wenv, wval = [half_ref[i * chans : (i + 1) * chans, :] for i in range(3)]
    w2 = half_ref[3 * chans : 5 * chans, :]

    def flip(w):
        return w.astype(F32).T.astype(BF16)

    w1_ref[...] = w1
    w2_ref[...] = w2
    w1t_ref[...] = flip(w1)
    wevt_ref[0:chans, :] = flip(wenv)
    wevt_ref[chans:, :] = flip(wval)
    w2t_ref[:, 0:chans] = flip(w2[0:chans, :])
    w2t_ref[:, chans:] = flip(w2[chans:, :])
    wev_ref[:, 0:chans] = wenv
    wev_ref[:, chans:] = wval
    wradb_ref[...] = jnp.concatenate([rad, jnp.zeros_like(rad)], axis=0).astype(BF16)
    wout = half_ref[5 * chans : 5 * chans + 1, :].astype(F32)
    wcol_ref[...] = jnp.broadcast_to(wout, (LANES, chans)).T
    feat = rows_ref[0:own, :]
    tab_ref[0:own, :] = dot_nn(feat, wa, HIGH)
    tab_ref[own : 2 * own, :] = dot_nn(feat, wb, HIGH)
    rad_hi, rad_lo = split(rad)
    tab_ref[2 * own :, :] = jnp.concatenate([rad_hi, rad_hi, rad_lo, jnp.zeros_like(rad)], axis=0)


def harmonics(ux, uy, uz):
    return [
        ux,
        uy,
        uz,
        ROOT3 * ux * uy,
        ROOT3 * uy * uz,
        ROOT3 * ux * uz,
        0.866 * (ux * ux - uy * uy),
        0.5 * (3.0 * uz * uz - 1.0),
    ]


def trig(half):
    turns = jnp.round(half)
    x = math.pi * (half - turns)
    odd = turns - 2.0 * jnp.floor(0.5 * turns)
    sign = 1.0 - 2.0 * odd
    x2 = x * x
    s = jnp.full_like(x, -1.0 / 39916800)
    for coef in (1.0 / 362880, -1.0 / 5040, 1.0 / 120, -1.0 / 6, 1.0):
        s = s * x2 + coef
    c = jnp.full_like(x, 1.0 / 479001600)
    for coef in (-1.0 / 3628800, 1.0 / 40320, -1.0 / 720, 1.0 / 24, -0.5, 1.0):
        c = c * x2 + coef
    return sign * x * s, sign * c


def waves(half, count):
    s1, c1 = trig(half)
    sins, coss = [s1], [c1]
    s0, c0 = jnp.zeros_like(s1), jnp.ones_like(c1)
    for _ in range(count - 1):
        sn = 2.0 * c1 * sins[-1] - s0
        cn = 2.0 * c1 * coss[-1] - c0
        s0, c0 = sins[-1], coss[-1]
        sins.append(sn)
        coss.append(cn)
    return sins, coss


def look_up(table_row, index):
    low = index & (LANES - 1)
    high = index >> 7
    result = jnp.zeros(index.shape, F32)
    for block in range(table_row.shape[1] // LANES):
        part = jnp.broadcast_to(table_row[:, block * LANES : (block + 1) * LANES], index.shape)
        got = jnp.take_along_axis(part, low, axis=1)
        result = jnp.where(high == block, got, result)
    return result


def in_lanes(tile):
    return jnp.concatenate([tile[r : r + 1, :] for r in range(tile.shape[0])], axis=1)


def one_hot(row, base, count):
    near = jnp.clip(row - base, -1, LANES).astype(BF16)
    iota = lax.broadcasted_iota(jnp.int32, (count, row.shape[1]), 0).astype(BF16)
    return jnp.where(iota == near, jnp.ones((), BF16), jnp.zeros((), BF16))


def sorted_size(edges):
    return 1 << (edges - 1).bit_length()


def main_kernel(plan, *refs):
    count_ref, bound_ref, key_ref, pos_ref, wb_ref = refs[:5]
    came, refs = plan.cut(refs[5:], 0, 1, 2)
    half_ref, w1t_ref, wevt_ref, w2t_ref, w1_ref, wev_ref, w2_ref, wradb_ref, wcol_ref = refs[:9]
    ae_ref, own_ref = refs[9:11]
    n_x = len(plan.groups[0])
    back_refs, rest_ref = refs[11 : 11 + n_x], refs[11 + n_x]
    (
        tab_ref,
        ghost_ref,
        place_ref,
        table_ref,
        y_ref,
        basis_ref,
        geo_ref,
        first_ref,
        dsilu_ref,
        ew_ref,
        val_ref,
        a_ref,
        env_ref,
        denv_ref,
        big_ref,
        dt_ref,
        dv_ref,
        dfa_ref,
        live_ref,
        dy_ref,
        db_ref,
        dr_ref,
        acc_ref,
    ) = refs[12 + n_x :]
    own = pos_ref.shape[1]
    chans = w1_ref.shape[0]
    n_basis = wradb_ref.shape[0] // 2
    rows_all = key_ref.shape[0] * key_ref.shape[1]
    per = CHUNK // LANES
    subs = CHUNK // SUB
    sub_rows = SUB // LANES
    n_ghost = sum(len(c) * w for c, w in zip(CLASSES, plan.widths))
    n_tab = own + n_ghost
    n_sel = own + n_tab

    place_ref[...] = jnp.zeros_like(place_ref)
    at = 0
    for off in OFFSETS:
        live = plan.live(off)
        message, begin = plan.find(came, (0, 1, 2), None, [], off)
        ghost_ref[at : at + live, :] = message[begin : begin + live, :]
        place_ref[at : at + live, :] = spread(message[begin + live : begin + live + 1, :], live)
        at += live
    ghost_pos = dot_nt(group_rows(8), place_ref[...], HIGH)
    pos_t = jnp.concatenate([pos_ref[...], ghost_pos[0:3, :]], axis=1)
    f_hi, f_lo = split(ghost_ref[...])
    w_hi, w_lo = split(wb_ref[...])
    tab_ref[0 : 2 * own, :] = half_ref[0 : 2 * own, :]
    tab_ref[2 * own : n_sel, :] = dot_nn(
        jnp.concatenate([f_hi, f_lo, f_hi], axis=1).astype(BF16),
        jnp.concatenate([w_hi, w_hi, w_lo], axis=0).astype(BF16),
    )
    tab_ref[n_sel:, :] = half_ref[2 * own :, :]
    table_ref[...] = tab_ref[...].T.astype(BF16)

    keys = key_ref[...].reshape(rows_all, LANES)
    centre = keys >> OTHER_BITS
    other = keys & OTHER_MASK
    valid = (keys != (own - 1) * (OTHER_MASK + 1) + OTHER_MASK).astype(F32)
    r = [
        look_up(pos_t[a : a + 1, :], other) - look_up(pos_t[a : a + 1, 0:LANES], centre)
        for a in range(3)
    ]
    d2 = r[0] * r[0] + r[1] * r[1] + r[2] * r[2] + 0.01
    dist = jnp.sqrt(d2)
    inv = 1.0 / dist
    q = 1.0 / (1.0 + 0.25 * d2)
    envelope = q * q
    unit = [x * inv for x in r]
    for m, comp in enumerate(harmonics(*unit)):
        y_ref[pl.ds(m, rows_all, stride=8), :] = comp
    sins, _ = waves(0.5 * dist, n_basis)
    scale = envelope * inv
    for n in range(n_basis):
        basis_ref[pl.ds(n, rows_all, stride=n_basis), :] = sins[n] * scale
    for i, plane in enumerate((unit[0], unit[1], unit[2], dist, inv, q, envelope * valid, valid)):
        geo_ref[i] = plane.reshape(geo_ref.shape[1:])

    env_ref[...] = jnp.zeros_like(env_ref)
    denv_ref[...] = jnp.zeros_like(denv_ref)
    ae_ref[...] = jnp.zeros_like(ae_ref)
    acc_ref[...] = jnp.zeros_like(acc_ref)
    dr_ref[...] = jnp.zeros_like(dr_ref)

    bound_total = sorted_size(rows_all * LANES)
    n_chunks = lax.div(count_ref[0] + (CHUNK - 1), jnp.int32(CHUNK))

    def window(k, s):
        groups = bound_ref.shape[1] * SUB // bound_total
        first = (k * subs + s) * groups
        low = bound_ref[0, first]
        high = low
        for g in range(groups):
            high = jnp.maximum(high, bound_ref[1, first + g])
        start = pl.multiple_of((low >> 3) << 3, 8)
        more = lax.div(high - start, jnp.int32(WIN))
        return start, more

    def any_more(k):
        most = window(k, 0)[1]
        for s in range(1, subs):
            most = jnp.maximum(most, window(k, s)[1])
        return most > 0

    def window_hot(k, s, start):
        rows = key_ref[k, s * sub_rows : (s + 1) * sub_rows, :]
        crow = in_lanes(rows >> OTHER_BITS) - start
        return lax.broadcasted_iota(jnp.int32, (WIN, SUB), 0) == crow

    def select(k, s, start):
        row = k * per + s * sub_rows
        hot = window_hot(k, s, start)
        tiles = [
            y_ref[pl.ds(pl.multiple_of((row + j) * 8, 8), 8), :] for j in range(sub_rows)
        ]
        ys = jnp.concatenate(tiles, axis=1)
        parts = [hot.astype(F32)]
        for m in range(8):
            parts.append(jnp.where(hot, ys[m : m + 1, :], 0.0))
        return jnp.concatenate(parts, axis=0).astype(BF16)

    def load_window(ref, start):
        return jnp.concatenate(
            [ref[m, pl.ds(start, WIN), :] for m in range(9)], axis=0
        ).astype(BF16)

    def add_window(ref, start, rows):
        for m in range(9):
            ref[m, pl.ds(start, WIN), :] += rows[m * WIN : (m + 1) * WIN, :]

    def sub_lanes(s):
        return slice(s * SUB, (s + 1) * SUB)

    def more_windows(k, body):
        @pl.when(any_more(k))
        def _():
            for s in range(subs):
                start, more = window(k, s)

                def step(t, carry, s=s, start=start):
                    body(s, pl.multiple_of(start + t * WIN, 8))
                    return carry

                lax.fori_loop(1, more + 1, step, 0)

    def row_of(plane, k):
        return in_lanes(geo_ref[plane, k])

    def phase_a(k, carry):
        kt = key_ref[k]
        crow = in_lanes(kt >> OTHER_BITS)
        orow = in_lanes(kt & OTHER_MASK)
        hots = [one_hot(crow, 0, own)]
        for base in range(0, n_tab, LANES):
            hots.append(one_hot(orow, base, min(LANES, n_tab - base)))
        tiles = [
            basis_ref[pl.ds(pl.multiple_of((k * per + j) * n_basis, 8), n_basis), :]
            for j in range(per)
        ]
        basis = jnp.concatenate(tiles, axis=1)
        b_hi, b_lo = split(basis)
        hots.append(jnp.concatenate([b_hi, b_lo], axis=0).astype(BF16))
        hots.append(jnp.concatenate([b_hi, jnp.zeros_like(b_hi)], axis=0).astype(BF16))
        mixed = dot_nn(table_ref[...], jnp.concatenate(hots, axis=0)).astype(BF16)
        z1 = dot_nn(w1t_ref[...], mixed)
        sg = 0.5 + 0.5 * jnp.tanh(0.5 * z1)
        first = z1 * sg
        dsilu_ref[k] = (sg + first * (1.0 - sg)).astype(BF16)
        first = first.astype(BF16)
        first_ref[k] = first
        both = dot_nn(wevt_ref[...], first)
        ew = (both[0:chans] * row_of(6, k)).astype(BF16)
        ew_ref[k] = ew
        val_ref[k] = both[chans:].astype(BF16)
        for s in range(subs):
            start, _ = window(k, s)
            a = select(k, s, start)
            a_ref[k * subs + s] = a
            add_window(env_ref, start, dot_nt(a, ew[:, sub_lanes(s)]))

        def again(s, start):
            a = select(k, s, start)
            add_window(env_ref, start, dot_nt(a, ew_ref[k, :, sub_lanes(s)]))

        more_windows(k, again)
        return carry

    lax.fori_loop(0, n_chunks, phase_a, 0)

    def phase_b(k, carry):
        for s in range(subs):
            start, _ = window(k, s)
            big_ref[:, sub_lanes(s)] = dot_tn(load_window(env_ref, start), a_ref[k * subs + s])

        def again_total(s, start):
            big_ref[:, sub_lanes(s)] += dot_tn(load_window(env_ref, start), select(k, s, start))

        more_windows(k, again_total)
        total = 0.2 * big_ref[...]
        value = val_ref[k].astype(F32)
        scalar = (value * total).astype(BF16)
        z2 = dot_nn(w2t_ref[...], jnp.concatenate([first_ref[k], scalar], axis=0))
        sg = 0.5 + 0.5 * jnp.tanh(0.5 * z2)
        second = z2 * sg
        wcol = jnp.concatenate([wcol_ref[...]] * per, axis=1)
        ee = jnp.sum(second.astype(BF16).astype(F32) * wcol, axis=0, keepdims=True)
        envv = row_of(6, k)
        dy_ref[9, :, :] = jnp.zeros((per, LANES), F32)
        live = ee * row_of(7, k)
        for j in range(per):
            live_ref[k, j : j + 1, :] = live[:, j * LANES : (j + 1) * LANES]
        energy = ee * envv
        dz2 = ((wcol * envv) * (sg + second * (1.0 - sg))).astype(BF16)
        dj = dot_nn(w2_ref[...], dz2)
        dfa_ref[k] = dj[0:chans].astype(BF16)
        dscalar = dj[chans:]
        dt = (0.2 * value * dscalar).astype(BF16)
        dt_ref[k] = dt
        dv_ref[k] = (total * dscalar).astype(BF16)

        def add_energy(s, start):
            hot = window_hot(k, s, start)
            part = jnp.where(hot, energy[:, sub_lanes(s)], 0.0)
            half = part[:, 0:LANES]
            for j in range(1, sub_rows):
                half = half + part[:, j * LANES : (j + 1) * LANES]
            ae_ref[pl.ds(start, WIN), :] += half

        for s in range(subs):
            start, _ = window(k, s)
            add_window(denv_ref, start, dot_nt(a_ref[k * subs + s], dt[:, sub_lanes(s)]))
            add_energy(s, start)

        def again(s, start):
            add_window(
                denv_ref, start, dot_nt(select(k, s, start), dt_ref[k, :, sub_lanes(s)])
            )
            add_energy(s, start)

        more_windows(k, again)
        return carry

    lax.fori_loop(0, n_chunks, phase_b, 0)

    def phase_c(k, carry):
        def env_terms(s, start, a, fresh):
            e_win = load_window(env_ref, start)
            d_win = load_window(denv_ref, start)
            dew = dot_tn(d_win, a)
            pair = jnp.concatenate(
                [dt_ref[k, :, sub_lanes(s)], ew_ref[k, :, sub_lanes(s)]], axis=0
            )
            prods = dot_nn(jnp.concatenate([e_win, d_win], axis=1), pair)
            hot = a[0:WIN].astype(F32)
            if fresh:
                big_ref[:, sub_lanes(s)] = dew
            else:
                big_ref[:, sub_lanes(s)] += dew
            for m in range(1, 9):
                row = jnp.sum(prods[m * WIN : (m + 1) * WIN] * hot, axis=0, keepdims=True)
                for j in range(sub_rows):
                    at = s * sub_rows + j
                    piece = row[:, j * LANES : (j + 1) * LANES]
                    if fresh:
                        dy_ref[m, at : at + 1, :] = piece
                    else:
                        dy_ref[m, at : at + 1, :] += piece

        for s in range(subs):
            start, _ = window(k, s)
            env_terms(s, start, a_ref[k * subs + s], True)
        more_windows(k, lambda s, start: env_terms(s, start, select(k, s, start), False))
        dew = big_ref[...]
        dpre = (dew * row_of(6, k)).astype(BF16)
        denv_row = jnp.sum(dew * ew_ref[k].astype(F32), axis=0, keepdims=True)
        for j in range(per):
            dy_ref[0, j : j + 1, :] = denv_row[:, j * LANES : (j + 1) * LANES]
        dfirst = dfa_ref[k].astype(F32) + dot_nn(
            wev_ref[...], jnp.concatenate([dpre, dv_ref[k]], axis=0)
        )
        dz1 = (dfirst * dsilu_ref[k].astype(F32)).astype(BF16)
        dmixed = dot_nn(w1_ref[...], dz1).astype(BF16)
        dbasis = dot_nn(wradb_ref[...], dmixed)
        for j in range(per):
            db_ref[j * n_basis : (j + 1) * n_basis, :] = dbasis[
                0:n_basis, j * LANES : (j + 1) * LANES
            ]
        ux, uy, uz, dist, inv, q = [geo_ref[i, k] for i in range(6)]
        envelope = q * q
        g = envelope * inv
        denvelope = -(q * envelope) * dist
        dg = (denvelope - g) * inv
        sins, coss = waves(0.5 * dist, n_basis)
        denv_direct = live_ref[k] + dy_ref[0] / envelope
        ddist = denv_direct * denvelope
        for n in range(n_basis):
            db = db_ref[pl.ds(n, per, stride=n_basis), :]
            ddist = ddist + db * (coss[n] * ((n + 1) * math.pi / 2.0) * g + sins[n] * dg)
        y = [dy_ref[m] for m in range(9)]
        gx = y[1] + ROOT3 * (uy * y[4] + uz * y[6]) + (2.0 * 0.866) * ux * y[7]
        gy = y[2] + ROOT3 * (ux * y[4] + uz * y[5]) - (2.0 * 0.866) * uy * y[7]
        gz = y[3] + ROOT3 * (uy * y[5] + ux * y[6]) + 3.0 * uz * y[8]
        along = ddist - inv * (gx * ux + gy * uy + gz * uz)
        for i, (gu, u) in enumerate(((gx, ux), (gy, uy), (gz, uz))):
            hi, lo = split(inv * gu + along * u)
            dr_ref[pl.ds(i, per, stride=16), :] = hi
            dr_ref[pl.ds(3 + i, per, stride=16), :] = lo
        dr = jnp.concatenate([dr_ref[j * 16 : (j + 1) * 16, :] for j in range(per)], axis=1)
        kt = key_ref[k]
        crow = in_lanes(kt >> OTHER_BITS)
        orow = in_lanes(kt & OTHER_MASK)
        hots = [one_hot(crow, 0, own)]
        for base in range(0, n_tab, LANES):
            hots.append(one_hot(orow, base, min(LANES, n_tab - base)))
        sums = dot_nt(
            jnp.concatenate(hots, axis=0),
            jnp.concatenate([dmixed, dr.astype(BF16)], axis=0),
        )
        acc_ref[:, 0:chans] += sums[:, 0:chans]
        acc_ref[:, chans : chans + 16] += sums[:, chans:]
        return carry

    lax.fori_loop(0, n_chunks, phase_c, 0)

    own_ref[...] = acc_ref[0 : 2 * own, :]
    row = lax.broadcasted_iota(jnp.int32, (LANES, LANES), 0)
    group = lax.broadcasted_iota(jnp.int32, (LANES, LANES), 1) // GROUP
    both = ((group < 3) & ((row == group) | (row == group + 3))).astype(F32)
    places = dot_nn(acc_ref[2 * own :, LANES:], both, HIGH)
    found = {}
    at = 2 * own
    for off in OFFSETS:
        found[off] = at
        at += plan.live(off)
    for blocks, ref in zip(
        plan.groups[0] + [plan.held_rest], tuple(back_refs) + (rest_ref,)
    ):
        for off, row in plan.spans(blocks):
            live = plan.live(off)
            at = found[off]
            ref[row : row + live, :] = acc_ref[at : at + live, 0:chans]
            block = places[at - 2 * own : at - 2 * own + live, :]
            ref[row + live : row + live + 1, :] = jnp.sum(diagonal(block), axis=0, keepdims=True)


def own_kernel(ae_ref, own_ref, wa_ref, wb_ref, energy_ref, fg_ref, force_ref):
    chans = wa_ref.shape[1]
    own = force_ref.shape[1]
    energy_ref[...] = jnp.sum(ae_ref[0:own, :].T, axis=0, keepdims=True)
    fg_ref[...] = dot_nt(own_ref[0:own, 0:chans], wa_ref[...], HIGH) + dot_nt(
        own_ref[own:, 0:chans], wb_ref[...], HIGH
    )
    force = (own_ref[own:, LANES:] - own_ref[0:own, LANES:]).T
    force_ref[...] = force[0:3, :] + force[3:6, :]


def last_kernel(plan, sel_ref, fg_ref, force_ref, wb_ref, *refs):
    came, refs = plan.cut(refs, 0, 1, 2)
    out_force_ref, out_fg_ref, both_ref = refs
    both_ref[...] = jnp.zeros_like(both_ref)
    chans = fg_ref.shape[1]
    at = 0
    for blocks in plan.groups[2] + [plan.own_rest]:
        for off, row in plan.spans(blocks):
            live = plan.live(off)
            src, begin = plan.find(came, (2, 1, 0), None, [], off)
            here = slice(at + row, at + row + live)
            both_ref[here, 0:chans] = src[begin : begin + live, :]
            both_ref[here, chans:] = spread(src[begin + live : begin + live + 1, :], live)
        at += plan.total(blocks)
    sums = dot_exact(sel_ref[...].astype(BF16), both_ref[...], ((0,), (0,)))
    out_fg_ref[...] = fg_ref[...] + dot_nt(sums[:, 0:chans], wb_ref[...], HIGH)
    total = dot_nt(group_rows(8), sums[:, chans:], HIGH)
    out_force_ref[...] = -(force_ref[...] + total[0:3, :])


def local(
    positions,
    atom_features,
    send_face,
    send_edge,
    send_corner,
    centre,
    other,
    edge_count,
    w_proj_a,
    w_proj_b,
    w_radial,
    w_first,
    w_env,
    w_value,
    w_second,
    w_out,
):
    own, chans = atom_features.shape
    edges = centre.shape[0]
    n_basis = w_radial.shape[0]
    plan = Plan(
        [send_face.shape[2], send_edge.shape[2], send_corner.shape[2]],
        [lax.axis_size(axis) for axis in AXES],
    )
    n_ghost = sum(len(c) * w for c, w in zip(CLASSES, plan.widths))
    n_sel = 2 * own + n_ghost
    n_send = sum(plan.total(blocks) for blocks in plan.groups[2]) + plan.total(plan.own_rest)
    n_table = n_sel + 4 * n_basis
    edges_up = -(-edges // CHUNK) * CHUNK
    n_rows = edges_up // LANES
    n_chunks = edges_up // CHUNK

    with jax.named_scope("prep"):
        rows = jnp.concatenate([atom_features, positions], axis=0)
        widest = max(plan.widths)
        lists = jnp.concatenate(
            [
                jnp.pad(x[0], ((0, 0), (0, widest - x.shape[2])))
                for x in (send_face, send_edge, send_corner)
            ],
            axis=0,
        )
        *sends, own_rows, sel = pl.pallas_call(
            lambda *refs: prep_kernel(plan, *refs),
            out_shape=plan.shapes(2, chans)
            + [shape(plan.total(plan.own_rest), chans), shape(n_send, own)],
            in_specs=[VMEM] * 2,
            out_specs=[VMEM] * (len(plan.groups[2]) + 2),
            scratch_shapes=[pltpu.VMEM((LANES, LANES), jnp.int32)],
            compiler_params=PARAMS,
        )(rows, lists)

    came = {}
    with jax.named_scope("halo_z"):
        came[2] = plan.send(2, sends)

    with jax.named_scope("group_edges"):
        dead = (own - 1) * (OTHER_MASK + 1) + OTHER_MASK
        pad = [(0, edges_up - edges)]
        regs = max(sorted_size(edges_up) // (8 * LANES), 1)
        key, bounds = pl.pallas_call(
            lambda *refs: sort_kernel(dead, *refs),
            out_shape=[
                shape(n_chunks, CHUNK // LANES, LANES, dtype=jnp.int32),
                shape(2, LANES, dtype=jnp.int32),
            ],
            in_specs=[SMEM, VMEM, VMEM],
            out_specs=[VMEM] * 2,
            scratch_shapes=[pltpu.VMEM((16 * regs, LANES), F32)],
            compiler_params=PARAMS,
        )(
            edge_count,
            jnp.pad(centre, pad).reshape(n_rows, LANES),
            jnp.pad(other, pad).reshape(n_rows, LANES),
        )

    with jax.named_scope("halo_y"):
        came[2], key, bounds = lax.optimization_barrier((came[2], key, bounds))
        came[1] = plan.send(1, glue(plan, 1, (2,), plan.own_rest, own_rows, came))

    with jax.named_scope("weights"):
        wide = jnp.concatenate([w_proj_a, w_proj_b, w_radial], axis=0)
        narrow = jnp.concatenate([w_first, w_env, w_value, w_second, w_out[None, :]], axis=0)
        half, *weights = pl.pallas_call(
            weight_kernel,
            out_shape=[
                shape(2 * own + 4 * n_basis, chans),
                shape(chans, chans, dtype=BF16),
                shape(2 * chans, chans, dtype=BF16),
                shape(chans, 2 * chans, dtype=BF16),
                shape(chans, chans, dtype=BF16),
                shape(chans, 2 * chans, dtype=BF16),
                shape(2 * chans, chans, dtype=BF16),
                shape(2 * n_basis, chans, dtype=BF16),
                shape(chans, LANES),
            ],
            in_specs=[VMEM] * 3,
            out_specs=[VMEM] * 9,
            compiler_params=PARAMS,
        )(rows, wide, narrow)

    with jax.named_scope("halo_x"):
        came[1], half, weights = lax.optimization_barrier((came[1], half, weights))
        came[0] = plan.send(0, glue(plan, 0, (1, 2), plan.own_rest, own_rows, came))

    planes = (n_chunks, chans, CHUNK)
    scratch = [
        pltpu.VMEM((n_table, chans), F32),
        pltpu.VMEM((n_ghost, chans), F32),
        pltpu.VMEM((-(-n_ghost // LANES) * LANES, LANES), F32),
        pltpu.VMEM((chans, n_table), BF16),
        pltpu.VMEM((n_rows * 8, LANES), F32),
        pltpu.VMEM((n_rows * n_basis, LANES), F32),
        pltpu.VMEM((8, n_chunks, CHUNK // LANES, LANES), F32),
        pltpu.VMEM(planes, BF16),
        pltpu.VMEM(planes, BF16),
        pltpu.VMEM(planes, BF16),
        pltpu.VMEM(planes, BF16),
        pltpu.VMEM((edges_up // SUB, 9 * WIN, SUB), BF16),
        pltpu.VMEM((9, own + WIN, chans), F32),
        pltpu.VMEM((9, own + WIN, chans), F32),
        pltpu.VMEM((chans, CHUNK), F32),
        pltpu.VMEM(planes, BF16),
        pltpu.VMEM(planes, BF16),
        pltpu.VMEM(planes, BF16),
        pltpu.VMEM((n_chunks, CHUNK // LANES, LANES), F32),
        pltpu.VMEM((10, CHUNK // LANES, LANES), F32),
        pltpu.VMEM((CHUNK // LANES * n_basis, LANES), F32),
        pltpu.VMEM((CHUNK // LANES * 16, LANES), F32),
        pltpu.VMEM((n_sel, 2 * LANES), F32),
    ]
    with jax.named_scope("layer"):
        given = [edge_count, bounds, key, positions, w_proj_b]
        given += [*came[0], *came[1], *came[2], half, *weights]
        atom_sums, own_sums, *back, held = pl.pallas_call(
            lambda *refs: main_kernel(plan, *refs),
            out_shape=[shape(own + WIN, LANES), shape(2 * own, 2 * LANES)]
            + plan.shapes(0, chans)
            + [shape(plan.total(plan.held_rest), chans)],
            in_specs=[SMEM, SMEM] + [VMEM] * (len(given) - 2),
            out_specs=[VMEM] * (3 + len(plan.groups[0])),
            scratch_shapes=scratch,
            compiler_params=PARAMS,
        )(*given)

    with jax.named_scope("halo_back"):
        home = {0: plan.send(0, back, back=True)}
        home[1] = plan.send(1, glue(plan, 1, (0,), plan.held_rest, held, home), back=True)
        home[2] = plan.send(2, glue(plan, 2, (1, 0), plan.held_rest, held, home), back=True)

    with jax.named_scope("own_part"):
        energy, fg, force = pl.pallas_call(
            own_kernel,
            out_shape=[shape(1, own), shape(own, chans), shape(3, own)],
            in_specs=[VMEM] * 4,
            out_specs=[VMEM] * 3,
            compiler_params=PARAMS,
        )(atom_sums, own_sums, w_proj_a, w_proj_b)

    with jax.named_scope("owner_sums"):
        given = [sel, fg, force, w_proj_b, *home[0], *home[1], *home[2]]
        forces, feature_grad = pl.pallas_call(
            lambda *refs: last_kernel(plan, *refs),
            out_shape=[shape(3, own), shape(own, chans)],
            in_specs=[VMEM] * len(given),
            out_specs=[VMEM] * 2,
            scratch_shapes=[pltpu.VMEM((n_send, chans + LANES), F32)],
            compiler_params=PARAMS,
        )(*given)
    return forces, energy.reshape(own), feature_grad


def solution(mesh):
    shard = P(AXES)
    return jax.shard_map(
        local,
        mesh=mesh,
        in_specs=(
            P(None, AXES),
            P(AXES, None),
            P(AXES, None, None),
            P(AXES, None, None),
            P(AXES, None, None),
            shard,
            shard,
            shard,
        )
        + (P(),) * 8,
        out_specs=(P(None, AXES), shard, P(AXES, None)),
        check_vma=False,
    )
```

profile of v0, /device:TPU:0, one launch (start us, length us, event | category | flops | bytes accessed | tf_op | source)
XLA Modules:
  0.0 57.6 jit_solution(15525373884399762999)
XLA Ops:
  0.6 0.0 copy-start.11
  0.6 0.7 %copy.23 = s32[1,6,32]{2,1,0:T(8,128)S(1)} copy(s32[1,6,32]{2,0,1:T(1,128)} %param.18) | data formatting | bytes 1536
  1.3 0.0 copy-done.11
  1.3 0.1 copy.20
  1.4 0.6 %copy-done.10 = s32[1,12,8]{1,2,0:T(8,128)S(1)} copy-done((s32[1,12,8]{1,2,0:T(8,128)S(1)}, s32[1,12,8]{1,2,0:T(8,128)}, u32[]{:S(2)}) %copy-start.10) | copy-done | bytes 408
  2.0 0.1 copy.19
  2.1 0.9 %constant_dynamic-update-slice_fusion.1 = f32[131,128]{1,0:T(8,128)S(1)} fusion(f32[128,128]{1,0:T(8,128)} %param.17), kind=kLoop, calls=%fused_computation.4 | loop fusion | bytes 131072
  3.0 0.0 copy-done.4
  3.0 0.0 copy-start.6
  3.0 0.7 %prep.1 = (f32[162,128]{1,0:T(8,128)S(1)}, f32[168,128]{1,0:T(8,128)S(1)}, f32[330,128]{1,0:T(8,128)S(1)}) custom-call(f32[131,128]{1,0:T(8,128)S(1)} %constant_dynamic-update-slice_fusion.refs_0_.rows_ref, s32[26,32]{1,0:T(8,128)S(1)} %pad_add_fusion.refs_1_), custom_call_target="tpu_custom_call" | custom-call | tf_op jit(solution)/shard_map/prep/pallas_call | solution.py:819
  3.7 0.0 copy-start.7
  3.7 3.0 %collective-permute-start = (f32[162,128]{1,0:T(8,128)S(1)}, f32[162,128]{1,0:T(8,128)S(1)}, u32[]{:S(2)}, u32[]{:S(2)}) collective-permute-start(f32[162,128]{1,0:T(8,128)S(1)} %get-tuple-element.48), channel_id=1, source_target_pairs={{0,1},{1,0},{2,3},{3,2},{4,5},{5,4},{6,7},{7,6},{8,9},{9,8},{10,11... | collective-permute-start | bytes 248840 | tf_op jit(solution)/shard_map/halo_z/ppermute | solution.py:128
  6.7 0.0 copy-done.6
  6.7 0.0 copy-done.7
  6.7 0.0 copy-start.5
  6.8 0.7 %copy-done.8 = bf16[128,128]{1,0:T(8,128)(2,1)S(1)} copy-done((bf16[128,128]{1,0:T(8,128)(2,1)S(1)}, bf16[128,128]{1,0:T(8,128)(2,1)}, u32[]{:S(2)}) %copy-start.8) | copy-done | bytes 32792
  7.5 0.1 copy-done.5
  7.6 0.6 %copy-done.12 = bf16[128]{0:T(256)(128)(2,1)S(1)} copy-done((bf16[128]{0:T(256)(128)(2,1)S(1)}, bf16[128]{0:T(256)(128)(2,1)}, u32[]{:S(2)}) %copy-start.12) | copy-done | bytes 280
  8.9 0.0 copy-done.2
  8.9 0.0 copy-done.3
  8.9 2.4 %group_edges.1 = (s32[3,16,128]{2,1,0:T(8,128)S(1)}, s32[2,128]{1,0:T(2,128)S(1)}) custom-call(s32[1]{0:T(128)S(6)} %copy.29.refs_0_, s32[48,128]{1,0:T(8,128)S(1)} %bitcast.10, s32[48,128]{1,0:T(8,128)S(1)} %bitcast.11), custom_call_target="tpu_custom_call" | custom-call | tf_op jit(solution)/shard_map/group_edges/pallas_call | solution.py:837
  11.3 0.0 collective-permute-done.refs_1_.refs_3_.refs_9_
  11.3 0.0 copy-start
  11.4 0.0 copy-start.1
  11.4 0.0 copy-start.9
  11.4 3.7 %collective-permute-start.1 = (f32[81,128]{1,0:T(8,128)S(1)}, f32[81,128]{1,0:T(8,128)S(1)}, u32[]{:S(2)}, u32[]{:S(2)}) collective-permute-start(f32[81,128]{1,0:T(8,128)S(1)} %get-tuple-element.55), channel_id=1, source_target_pairs={{0,6},{2,0},{4,2},{6,4},{1,7},{3,1},{5,3},{7,5},{8,14},{10,8},{12,... | collective-permute-start | bytes 124424 | tf_op jit(solution)/shard_map/halo_y/ppermute | solution.py:128
  15.1 0.0 collective-permute-start.2
  15.1 0.0 copy-done.1
  15.1 0.3 weights.1
  15.4 1.4 %collective-permute-done.1.refs_1_.refs_7_ = f32[81,128]{1,0:T(8,128)S(1)} collective-permute-done((f32[81,128]{1,0:T(8,128)S(1)}, f32[81,128]{1,0:T(8,128)S(1)}, u32[]{:S(2)}, u32[]{:S(2)}) %collective-permute-start.1) | collective-permute-done | bytes 41504 | tf_op jit(solution)/shard_map/halo_y/ppermute | solution.py:128
  16.8 4.1 %collective-permute-done.2.refs_2_.refs_8_ = f32[81,128]{1,0:T(8,128)S(1)} collective-permute-done((f32[81,128]{1,0:T(8,128)S(1)}, f32[81,128]{1,0:T(8,128)S(1)}, u32[]{:S(2)}, u32[]{:S(2)}) %collective-permute-start.2) | collective-permute-done | bytes 41504 | tf_op jit(solution)/shard_map/halo_y/ppermute | solution.py:128
  20.9 0.1 collective-permute-start.3
  21.0 0.5 collective-permute-start.4
  21.5 1.2 %collective-permute-done.3.refs_5_ = f32[81,128]{1,0:T(8,128)S(1)} collective-permute-done((f32[81,128]{1,0:T(8,128)S(1)}, f32[81,128]{1,0:T(8,128)S(1)}, u32[]{:S(2)}, u32[]{:S(2)}) %collective-permute-start.3) | collective-permute-done | bytes 41504 | tf_op jit(solution)/shard_map/halo_x/ppermute | solution.py:128
  22.7 2.3 %collective-permute-done.4.refs_6_ = f32[81,128]{1,0:T(8,128)S(1)} collective-permute-done((f32[81,128]{1,0:T(8,128)S(1)}, f32[81,128]{1,0:T(8,128)S(1)}, u32[]{:S(2)}, u32[]{:S(2)}) %collective-permute-start.4) | collective-permute-done | bytes 41504 | tf_op jit(solution)/shard_map/halo_x/ppermute | solution.py:128
  25.0 17.0 %layer.1 = (f32[144,128]{1,0:T(8,128)S(1)}, f32[256,256]{1,0:T(8,128)S(1)}, f32[81,128]{1,0:T(8,128)S(1)}, f32[81,128]{1,0:T(8,128)S(1)}, f32[168,128]{1,0:T(8,128)S(1)}) custom-call(s32[1]{0:T(128)S(6)} %copy.29.refs_0_, s32[2,128]{1,0:T(2,128)S(1)} %get-tuple-element.51.refs_1_, s32[3,16,128]{2,1,0:T(8,128)S(1)} %get-tuple-element.52.refs_2_, ...), custom_call_target="tpu_custom_call" | custom-call | tf_op jit(solution)/shard_map/layer/pallas_call | solution.py:911
  42.0 0.1 collective-permute-start.5
  42.1 1.7 %collective-permute-start.6 = (f32[81,128]{1,0:T(8,128)S(1)}, f32[81,128]{1,0:T(8,128)S(1)}, u32[]{:S(2)}, u32[]{:S(2)}) collective-permute-start(f32[81,128]{1,0:T(8,128)S(1)} %get-tuple-element.84), channel_id=1, source_target_pairs={{0,24},{8,0},{16,8},{24,16},{1,25},{9,1},{17,9},{25,17},{2,26},{10... | collective-permute-start | bytes 124424 | tf_op jit(solution)/shard_map/halo_back/ppermute | solution.py:128
  43.8 2.1 %collective-permute-done.5.refs_1_.refs_3_.refs_4_ = f32[81,128]{1,0:T(8,128)S(1)} collective-permute-done((f32[81,128]{1,0:T(8,128)S(1)}, f32[81,128]{1,0:T(8,128)S(1)}, u32[]{:S(2)}, u32[]{:S(2)}) %collective-permute-start.5) | collective-permute-done | bytes 41504 | tf_op jit(solution)/shard_map/halo_back/ppermute | solution.py:128
  45.9 0.0 collective-permute-done.6.refs_2_.refs_4_.refs_5_
  45.9 0.1 collective-permute-start.7
  45.9 3.8 %collective-permute-start.8 = (f32[81,128]{1,0:T(8,128)S(1)}, f32[81,128]{1,0:T(8,128)S(1)}, u32[]{:S(2)}, u32[]{:S(2)}) collective-permute-start(f32[81,128]{1,0:T(8,128)S(1)} %get-tuple-element.87), channel_id=1, source_target_pairs={{0,6},{2,0},{4,2},{6,4},{1,7},{3,1},{5,3},{7,5},{8,14},{10,8},{12,... | collective-permute-start | bytes 124424 | tf_op jit(solution)/shard_map/halo_back/ppermute | solution.py:128
  49.8 2.0 %collective-permute-done.7.refs_1_.refs_6_ = f32[81,128]{1,0:T(8,128)S(1)} collective-permute-done((f32[81,128]{1,0:T(8,128)S(1)}, f32[81,128]{1,0:T(8,128)S(1)}, u32[]{:S(2)}, u32[]{:S(2)}) %collective-permute-start.7) | collective-permute-done | bytes 41504 | tf_op jit(solution)/shard_map/halo_back/ppermute | solution.py:128
  51.8 0.0 collective-permute-done.8.refs_2_.refs_7_
  51.8 0.7 %collective-permute-start.9 = (f32[162,128]{1,0:T(8,128)S(1)}, f32[162,128]{1,0:T(8,128)S(1)}, u32[]{:S(2)}, u32[]{:S(2)}) collective-permute-start(f32[162,128]{1,0:T(8,128)S(1)} %halo_back.3), channel_id=1, source_target_pairs={{0,1},{1,0},{2,3},{3,2},{4,5},{5,4},{6,7},{7,6},{8,9},{9,8},{10,11... | collective-permute-start | bytes 248840 | tf_op jit(solution)/shard_map/halo_back/ppermute | solution.py:128
  52.5 0.8 %own_part.1 = (f32[1,128]{1,0:T(1,128)}, f32[128,128]{1,0:T(8,128)S(1)}, f32[3,128]{1,0:T(4,128)S(1)}) custom-call(f32[144,128]{1,0:T(8,128)S(1)} %get-tuple-element.79.ae_ref, f32[256,256]{1,0:T(8,128)S(1)} %get-tuple-element.80.own_ref, f32[128,128]{1,0:T(8,128)S(1)} %copy-done.1, f32[128,128]{1,0:T(8,128)S(1)} %copy-done), custom_call_target="tpu_custom_call" | custom-call | tf_op jit(solution)/shard_map/own_part/pallas_call | solution.py:928
  53.4 3.0 %collective-permute-done.9.refs_8_ = f32[162,128]{1,0:T(8,128)S(1)} collective-permute-done((f32[162,128]{1,0:T(8,128)S(1)}, f32[162,128]{1,0:T(8,128)S(1)}, u32[]{:S(2)}, u32[]{:S(2)}) %collective-permute-start.9) | collective-permute-done | bytes 82976 | tf_op jit(solution)/shard_map/halo_back/ppermute | solution.py:128
  56.3 1.2 %owner_sums.1 = (f32[3,128]{1,0:T(4,128)}, f32[128,128]{1,0:T(8,128)}) custom-call(f32[330,128]{1,0:T(8,128)S(1)} %get-tuple-element.47.refs_0_, f32[128,128]{1,0:T(8,128)S(1)} %get-tuple-element.81.refs_1_, f32[3,128]{1,0:T(4,128)S(1)} %get-tuple-element.82.refs_2_, f32[128,128]{1,0:T(8,128)S(1)} %copy-done, ...), custom_call_target="tpu_custom_call" | custom-call | tf_op jit(solution)/shard_map/owner_sums/pallas_call | solution.py:938
  (20 shorter events, 0.1 us)
Async XLA Ops:
  0.6 0.7 %copy-start.11 = (s32[1,8,2]{1,2,0:T(2,128)S(1)}, s32[1,8,2]{1,2,0:T(2,128)}, u32[]{:S(2)}) copy-start(s32[1,8,2]{1,2,0:T(2,128)} %param.20) | copy-start | bytes 196
  1.3 0.7 %copy-start.10 = (s32[1,12,8]{1,2,0:T(8,128)S(1)}, s32[1,12,8]{1,2,0:T(8,128)}, u32[]{:S(2)}) copy-start(s32[1,12,8]{1,2,0:T(8,128)} %param.19) | copy-start | bytes 1156
  2.1 0.9 %copy-start.4 = (f32[3,128]{1,0:T(4,128)S(1)}, f32[3,128]{1,0:T(4,128)}, u32[]{:S(2)}) copy-start(f32[3,128]{1,0:T(4,128)} %refs_3_.2) | copy-start | bytes 4612
  3.0 3.7 %copy-start.6 = (bf16[128,128]{1,0:T(8,128)(2,1)S(1)}, bf16[128,128]{1,0:T(8,128)(2,1)}, u32[]{:S(2)}) copy-start(bf16[128,128]{1,0:T(8,128)(2,1)} %param.27) | copy-start | bytes 98308
  3.7 3.0 %copy-start.7 = (bf16[128,128]{1,0:T(8,128)(2,1)S(1)}, bf16[128,128]{1,0:T(8,128)(2,1)}, u32[]{:S(2)}) copy-start(bf16[128,128]{1,0:T(8,128)(2,1)} %param.28) | copy-start | bytes 98308
  3.7 7.6 %collective-permute-start = (f32[162,128]{1,0:T(8,128)S(1)}, f32[162,128]{1,0:T(8,128)S(1)}, u32[]{:S(2)}, u32[]{:S(2)}) collective-permute-start(f32[162,128]{1,0:T(8,128)S(1)} %get-tuple-element.48), channel_id=1, source_target_pairs={{0,1},{1,0},{2,3},{3,2},{4,5},{5,4},{6,7},{7,6},{8,9},{9,8},{10,11... | collective-permute-start | bytes 248840 | tf_op jit(solution)/shard_map/halo_z/ppermute | solution.py:128
  6.7 0.8 %copy-start.8 = (bf16[128,128]{1,0:T(8,128)(2,1)S(1)}, bf16[128,128]{1,0:T(8,128)(2,1)}, u32[]{:S(2)}) copy-start(bf16[128,128]{1,0:T(8,128)(2,1)} %param.29) | copy-start | bytes 98308
  6.7 0.8 %copy-start.5 = (bf16[256,128]{1,0:T(8,128)(2,1)S(1)}, bf16[256,128]{1,0:T(8,128)(2,1)}, u32[]{:S(2)}) copy-start(bf16[256,128]{1,0:T(8,128)(2,1)} %param.30) | copy-start | bytes 196612
  7.6 0.7 %copy-start.12 = (bf16[128]{0:T(256)(128)(2,1)S(1)}, bf16[128]{0:T(256)(128)(2,1)}, u32[]{:S(2)}) copy-start(bf16[128]{0:T(256)(128)(2,1)} %param.31) | copy-start | bytes 772
  7.6 1.3 %copy-start.2 = (s32[6144]{0:T(1024)S(1)}, s32[6144]{0:T(1024)}, u32[]{:S(2)}) copy-start(s32[6144]{0:T(1024)} %param.21) | copy-start | bytes 73732
  7.6 1.3 %copy-start.3 = (s32[6144]{0:T(1024)S(1)}, s32[6144]{0:T(1024)}, u32[]{:S(2)}) copy-start(s32[6144]{0:T(1024)} %param.22) | copy-start | bytes 73732
  11.3 3.7 %copy-start = (f32[128,128]{1,0:T(8,128)S(1)}, f32[128,128]{1,0:T(8,128)}, u32[]{:S(2)}) copy-start(f32[128,128]{1,0:T(8,128)} %refs_3_.3) | copy-start | bytes 196612
  11.4 3.7 %copy-start.1 = (f32[128,128]{1,0:T(8,128)S(1)}, f32[128,128]{1,0:T(8,128)}, u32[]{:S(2)}) copy-start(f32[128,128]{1,0:T(8,128)} %wa_ref.1) | copy-start | bytes 196612
  11.4 3.7 %copy-start.9 = (f32[8,128]{1,0:T(8,128)S(1)}, f32[8,128]{1,0:T(8,128)}, u32[]{:S(2)}) copy-start(f32[8,128]{1,0:T(8,128)} %param.26) | copy-start | bytes 12292
  11.4 5.4 %collective-permute-start.1 = (f32[81,128]{1,0:T(8,128)S(1)}, f32[81,128]{1,0:T(8,128)S(1)}, u32[]{:S(2)}, u32[]{:S(2)}) collective-permute-start(f32[81,128]{1,0:T(8,128)S(1)} %get-tuple-element.55), channel_id=1, source_target_pairs={{0,6},{2,0},{4,2},{6,4},{1,7},{3,1},{5,3},{7,5},{8,14},{10,8},{12,... | collective-permute-start | bytes 124424 | tf_op jit(solution)/shard_map/halo_y/ppermute | solution.py:128
  15.1 5.8 %collective-permute-start.2 = (f32[81,128]{1,0:T(8,128)S(1)}, f32[81,128]{1,0:T(8,128)S(1)}, u32[]{:S(2)}, u32[]{:S(2)}) collective-permute-start(f32[81,128]{1,0:T(8,128)S(1)} %get-tuple-element.56), channel_id=1, source_target_pairs={{0,2},{2,4},{4,6},{6,0},{1,3},{3,5},{5,7},{7,1},{8,10},{10,12},{12... | collective-permute-start | bytes 124424 | tf_op jit(solution)/shard_map/halo_y/ppermute | solution.py:128
  20.9 1.8 %collective-permute-start.3 = (f32[81,128]{1,0:T(8,128)S(1)}, f32[81,128]{1,0:T(8,128)S(1)}, u32[]{:S(2)}, u32[]{:S(2)}) collective-permute-start(f32[81,128]{1,0:T(8,128)S(1)} %get-tuple-element.68), channel_id=1, source_target_pairs={{0,24},{8,0},{16,8},{24,16},{1,25},{9,1},{17,9},{25,17},{2,26},{10... | collective-permute-start | bytes 124424 | tf_op jit(solution)/shard_map/halo_x/ppermute | solution.py:128
  21.0 4.0 %collective-permute-start.4 = (f32[81,128]{1,0:T(8,128)S(1)}, f32[81,128]{1,0:T(8,128)S(1)}, u32[]{:S(2)}, u32[]{:S(2)}) collective-permute-start(f32[81,128]{1,0:T(8,128)S(1)} %get-tuple-element.69), channel_id=1, source_target_pairs={{0,8},{8,16},{16,24},{24,0},{1,9},{9,17},{17,25},{25,1},{2,10},{10... | collective-permute-start | bytes 124424 | tf_op jit(solution)/shard_map/halo_x/ppermute | solution.py:128
  42.0 3.9 %collective-permute-start.5 = (f32[81,128]{1,0:T(8,128)S(1)}, f32[81,128]{1,0:T(8,128)S(1)}, u32[]{:S(2)}, u32[]{:S(2)}) collective-permute-start(f32[81,128]{1,0:T(8,128)S(1)} %get-tuple-element.83), channel_id=1, source_target_pairs={{0,8},{8,16},{16,24},{24,0},{1,9},{9,17},{17,25},{25,1},{2,10},{10... | collective-permute-start | bytes 124424 | tf_op jit(solution)/shard_map/halo_back/ppermute | solution.py:128
  42.1 3.8 %collective-permute-start.6 = (f32[81,128]{1,0:T(8,128)S(1)}, f32[81,128]{1,0:T(8,128)S(1)}, u32[]{:S(2)}, u32[]{:S(2)}) collective-permute-start(f32[81,128]{1,0:T(8,128)S(1)} %get-tuple-element.84), channel_id=1, source_target_pairs={{0,24},{8,0},{16,8},{24,16},{1,25},{9,1},{17,9},{25,17},{2,26},{10... | collective-permute-start | bytes 124424 | tf_op jit(solution)/shard_map/halo_back/ppermute | solution.py:128
  45.9 5.9 %collective-permute-start.7 = (f32[81,128]{1,0:T(8,128)S(1)}, f32[81,128]{1,0:T(8,128)S(1)}, u32[]{:S(2)}, u32[]{:S(2)}) collective-permute-start(f32[81,128]{1,0:T(8,128)S(1)} %get-tuple-element.86), channel_id=1, source_target_pairs={{0,2},{2,4},{4,6},{6,0},{1,3},{3,5},{5,7},{7,1},{8,10},{10,12},{12... | collective-permute-start | bytes 124424 | tf_op jit(solution)/shard_map/halo_back/ppermute | solution.py:128
  45.9 5.8 %collective-permute-start.8 = (f32[81,128]{1,0:T(8,128)S(1)}, f32[81,128]{1,0:T(8,128)S(1)}, u32[]{:S(2)}, u32[]{:S(2)}) collective-permute-start(f32[81,128]{1,0:T(8,128)S(1)} %get-tuple-element.87), channel_id=1, source_target_pairs={{0,6},{2,0},{4,2},{6,4},{1,7},{3,1},{5,3},{7,5},{8,14},{10,8},{12,... | collective-permute-start | bytes 124424 | tf_op jit(solution)/shard_map/halo_back/ppermute | solution.py:128
  51.8 4.6 %collective-permute-start.9 = (f32[162,128]{1,0:T(8,128)S(1)}, f32[162,128]{1,0:T(8,128)S(1)}, u32[]{:S(2)}, u32[]{:S(2)}) collective-permute-start(f32[162,128]{1,0:T(8,128)S(1)} %halo_back.3), channel_id=1, source_target_pairs={{0,1},{1,0},{2,3},{3,2},{4,5},{5,4},{6,7},{7,6},{8,9},{9,8},{10,11... | collective-permute-start | bytes 248840 | tf_op jit(solution)/shard_map/halo_back/ppermute | solution.py:128
where the time goes:
time: 58 us; the launch traced here: 57.6 us
  Pallas kernels  22.5 us (39%)
  waiting for transfers between devices  16.1 us (28%)
  starting transfers between devices  13.6 us (23%)
  local copies, waits for them, and re-layouts  3.87 us (7%)
  between operations  1.49 us (3%)
    pallas_call x1, Pallas kernels, local(): pl.pallas_call(lambda *refs: main_kernel(plan, *refs), out_shape=[shape(o...  17 us
    ppermute x10, waiting for transfers between devices, send(): lax.ppermute(message, AXES[a], [(i, (i + step) % n) for i in range(n)])  16.1 us
    ppermute x10, starting transfers between devices, send(): lax.ppermute(message, AXES[a], [(i, (i + step) % n) for i in range(n)])  13.6 us
    unnamed x32, local copies, waits for them, and re-layouts  3.69 us
    pallas_call x1, Pallas kernels, local(): pl.pallas_call(lambda *refs: sort_kernel(dead, *refs), out_shape=[shape(n...  2.41 us
    pallas_call x1, Pallas kernels, local(): pl.pallas_call(lambda *refs: last_kernel(plan, *refs), out_shape=[shape(3...  1.23 us
  transfers between devices with their start and end apart: 10, of which 7 were waited for; matrix products, arithmetic and copies ran while one was open for 0% of the time, Pallas kernels for 6%

commit v1 on v0

--- a/solution.py
+++ b/solution.py
@@ -11,7 +11,7 @@
 BF16 = jnp.bfloat16
 HIGH = lax.Precision.HIGHEST
 AXES = ("gx", "gy", "gz")
-CHUNK = 2048
+CHUNK = 6144
 SUB = 256
 WIN = 16
 OTHER_BITS = 9
@@ -160,22 +160,27 @@
     return out[:, 0 : x.shape[1]] + out[:, x.shape[1] :]
 
 
-def prep_kernel(plan, rows_ref, list_ref, *outs):
+def prep_kernel(plan, rows_ref, *outs):
     n_z = len(plan.groups[2])
     sends, rest_ref, sel_ref, turn_ref = outs[:n_z], outs[n_z], outs[n_z + 1], outs[n_z + 2]
     own = sel_ref.shape[1]
-    lane = lax.broadcasted_iota(jnp.int32, (1, own), 1)
+    lane = lax.broadcasted_iota(jnp.int32, (1, own), 1).astype(F32)
+    n_faces = len(CLASSES[0])
     turn_ref[...] = jnp.zeros_like(turn_ref)
-    turn_ref[0 : list_ref.shape[0], 0 : list_ref.shape[1]] = list_ref[...]
-    columns = turn_ref[...].T
+    turn_ref[0:n_faces, :] = rows_ref[own + 8 : own + 8 + n_faces, :]
+    columns = [turn_ref[...].T]
+    at = own + 16
+    for width in plan.widths[1:]:
+        columns.append(rows_ref[at : at + width, :])
+        at += -(-width // 8) * 8
     sel_ref[...] = jnp.zeros_like(sel_ref)
     messages = plan.groups[2] + [plan.own_rest]
     at = 0
     for blocks in messages:
         for off, begin in plan.spans(blocks):
-            key = OFFSETS.index(off)
+            key = CLASSES[kind(off)].index(off)
             live = plan.live(off)
-            column = columns[0:live, key : key + 1]
+            column = columns[kind(off)][0:live, key : key + 1]
             sel_ref[at + begin : at + begin + live, :] = (column == lane).astype(F32)
         at += plan.total(blocks)
     pos = dot_tn(rows_ref[own : own + 3, :], group_rows(3), HIGH)
@@ -292,11 +297,11 @@
     w1_ref,
     wev_ref,
     w2_ref,
-    wradb_ref,
     wcol_ref,
 ):
     chans = wide_ref.shape[1]
-    own = rows_ref.shape[0] - 3
+    rad_rows = wide_ref.shape[0] - 2 * chans
+    own = (tab_ref.shape[0] - 4 * rad_rows) // 2
     wa, wb, rad = wide_ref[0:chans, :], wide_ref[chans : 2 * chans, :], wide_ref[2 * chans :, :]
     w1, wenv, wval = [half_ref[i * chans : (i + 1) * chans, :] for i in range(3)]
     w2 = half_ref[3 * chans : 5 * chans, :]
@@ -304,7 +309,9 @@
     def flip(w):
         return w.astype(F32).T.astype(BF16)
 
-    w1_ref[...] = w1
+    down = dot_nn(rad, w1.astype(F32), HIGH)
+    w1_ref[0:chans, :] = w1
+    w1_ref[chans:, :] = jnp.concatenate([down, jnp.zeros_like(down)], axis=0).astype(BF16)
     w2_ref[...] = w2
     w1t_ref[...] = flip(w1)
     wevt_ref[0:chans, :] = flip(wenv)
@@ -313,7 +320,6 @@
     w2t_ref[:, chans:] = flip(w2[chans:, :])
     wev_ref[:, 0:chans] = wenv
     wev_ref[:, chans:] = wval
-    wradb_ref[...] = jnp.concatenate([rad, jnp.zeros_like(rad)], axis=0).astype(BF16)
     wout = half_ref[5 * chans : 5 * chans + 1, :].astype(F32)
     wcol_ref[...] = jnp.broadcast_to(wout, (LANES, chans)).T
     feat = rows_ref[0:own, :]
@@ -392,10 +398,10 @@
 def main_kernel(plan, *refs):
     count_ref, bound_ref, key_ref, pos_ref, wb_ref = refs[:5]
     came, refs = plan.cut(refs[5:], 0, 1, 2)
-    half_ref, w1t_ref, wevt_ref, w2t_ref, w1_ref, wev_ref, w2_ref, wradb_ref, wcol_ref = refs[:9]
-    ae_ref, own_ref = refs[9:11]
+    half_ref, w1t_ref, wevt_ref, w2t_ref, w1_ref, wev_ref, w2_ref, wcol_ref = refs[:8]
+    ae_ref, own_ref = refs[8:10]
     n_x = len(plan.groups[0])
-    back_refs, rest_ref = refs[11 : 11 + n_x], refs[11 + n_x]
+    back_refs, rest_ref = refs[10 : 10 + n_x], refs[10 + n_x]
     (
         tab_ref,
         ghost_ref,
@@ -416,14 +422,15 @@
         dv_ref,
         dfa_ref,
         live_ref,
+        energy_ref,
         dy_ref,
         db_ref,
         dr_ref,
         acc_ref,
-    ) = refs[12 + n_x :]
+    ) = refs[11 + n_x :]
     own = pos_ref.shape[1]
-    chans = w1_ref.shape[0]
-    n_basis = wradb_ref.shape[0] // 2
+    chans = w1_ref.shape[1]
+    n_basis = (w1_ref.shape[0] - chans) // 2
     rows_all = key_ref.shape[0] * key_ref.shape[1]
     per = CHUNK // LANES
     subs = CHUNK // SUB
@@ -495,15 +502,13 @@
         more = lax.div(high - start, jnp.int32(WIN))
         return start, more
 
-    def any_more(k):
-        most = window(k, 0)[1]
-        for s in range(1, subs):
-            most = jnp.maximum(most, window(k, s)[1])
-        return most > 0
+    most = jnp.int32(0)
+    for s in range(rows_all // sub_rows):
+        most = jnp.maximum(most, window(s // subs, s % subs)[1])
 
     def window_hot(k, s, start):
-        rows = key_ref[k, s * sub_rows : (s + 1) * sub_rows, :]
-        crow = in_lanes(rows >> OTHER_BITS) - start
+        rows = [key_ref[k, pl.ds(s * sub_rows + j, 1), :] for j in range(sub_rows)]
+        crow = (jnp.concatenate(rows, axis=1) >> OTHER_BITS) - start
         return lax.broadcasted_iota(jnp.int32, (WIN, SUB), 0) == crow
 
     def select(k, s, start):
@@ -528,19 +533,23 @@
             ref[m, pl.ds(start, WIN), :] += rows[m * WIN : (m + 1) * WIN, :]
 
     def sub_lanes(s):
-        return slice(s * SUB, (s + 1) * SUB)
+        if isinstance(s, int):
+            return slice(s * SUB, (s + 1) * SUB)
+        return pl.ds(pl.multiple_of(s * SUB, SUB), SUB)
 
     def more_windows(k, body):
-        @pl.when(any_more(k))
+        @pl.when(most > 0)
         def _():
-            for s in range(subs):
+            def over(s, carry):
                 start, more = window(k, s)
 
-                def step(t, carry, s=s, start=start):
+                def step(t, carry):
                     body(s, pl.multiple_of(start + t * WIN, 8))
                     return carry
 
-                lax.fori_loop(1, more + 1, step, 0)
+                return lax.fori_loop(1, more + 1, step, carry)
+
+            lax.fori_loop(0, subs, over, 0)
 
     def row_of(plane, k):
         return in_lanes(geo_ref[plane, k])
@@ -604,11 +613,10 @@
         wcol = jnp.concatenate([wcol_ref[...]] * per, axis=1)
         ee = jnp.sum(second.astype(BF16).astype(F32) * wcol, axis=0, keepdims=True)
         envv = row_of(6, k)
-        dy_ref[9, :, :] = jnp.zeros((per, LANES), F32)
         live = ee * row_of(7, k)
         for j in range(per):
             live_ref[k, j : j + 1, :] = live[:, j * LANES : (j + 1) * LANES]
-        energy = ee * envv
+        energy_ref[...] = ee * envv
         dz2 = ((wcol * envv) * (sg + second * (1.0 - sg))).astype(BF16)
         dj = dot_nn(w2_ref[...], dz2)
         dfa_ref[k] = dj[0:chans].astype(BF16)
@@ -619,7 +627,7 @@
 
         def add_energy(s, start):
             hot = window_hot(k, s, start)
-            part = jnp.where(hot, energy[:, sub_lanes(s)], 0.0)
+            part = jnp.where(hot, energy_ref[:, sub_lanes(s)], 0.0)
             half = part[:, 0:LANES]
             for j in range(1, sub_rows):
                 half = half + part[:, j * LANES : (j + 1) * LANES]
@@ -661,9 +669,9 @@
                     at = s * sub_rows + j
                     piece = row[:, j * LANES : (j + 1) * LANES]
                     if fresh:
-                        dy_ref[m, at : at + 1, :] = piece
+                        dy_ref[m, pl.ds(at, 1), :] = piece
                     else:
-                        dy_ref[m, at : at + 1, :] += piece
+                        dy_ref[m, pl.ds(at, 1), :] += piece
 
         for s in range(subs):
             start, _ = window(k, s)
@@ -678,8 +686,9 @@
             wev_ref[...], jnp.concatenate([dpre, dv_ref[k]], axis=0)
         )
         dz1 = (dfirst * dsilu_ref[k].astype(F32)).astype(BF16)
-        dmixed = dot_nn(w1_ref[...], dz1).astype(BF16)
-        dbasis = dot_nn(wradb_ref[...], dmixed)
+        dboth = dot_nn(w1_ref[...], dz1)
+        dmixed = dboth[0:chans].astype(BF16)
+        dbasis = dboth[chans:]
         for j in range(per):
             db_ref[j * n_basis : (j + 1) * n_basis, :] = dbasis[
                 0:n_basis, j * LANES : (j + 1) * LANES
@@ -773,6 +782,20 @@
     out_force_ref[...] = -(force_ref[...] + total[0:3, :])
 
 
+def stack(*arrays):
+    dtype = arrays[0].dtype
+    tile = 32 // dtype.itemsize
+    starts = [0]
+    for x in arrays:
+        starts.append(starts[-1] + -(-x.shape[0] // tile) * tile)
+    total = None
+    for x, at in zip(arrays, starts):
+        below = starts[-1] - at - x.shape[0]
+        part = jnp.pad(x.astype(dtype), ((at, below), (0, LANES - x.shape[1])))
+        total = part if total is None else total + part
+    return total
+
+
 def local(
     positions,
     atom_features,
@@ -807,24 +830,22 @@
     n_chunks = edges_up // CHUNK
 
     with jax.named_scope("prep"):
-        rows = jnp.concatenate([atom_features, positions], axis=0)
-        widest = max(plan.widths)
-        lists = jnp.concatenate(
-            [
-                jnp.pad(x[0], ((0, 0), (0, widest - x.shape[2])))
-                for x in (send_face, send_edge, send_corner)
-            ],
-            axis=0,
+        rows = stack(
+            atom_features,
+            positions,
+            send_face[0],
+            jnp.transpose(send_edge[0]),
+            jnp.transpose(send_corner[0]),
         )
         *sends, own_rows, sel = pl.pallas_call(
             lambda *refs: prep_kernel(plan, *refs),
             out_shape=plan.shapes(2, chans)
             + [shape(plan.total(plan.own_rest), chans), shape(n_send, own)],
-            in_specs=[VMEM] * 2,
+            in_specs=[VMEM],
             out_specs=[VMEM] * (len(plan.groups[2]) + 2),
-            scratch_shapes=[pltpu.VMEM((LANES, LANES), jnp.int32)],
+            scratch_shapes=[pltpu.VMEM((LANES, LANES), F32)],
             compiler_params=PARAMS,
-        )(rows, lists)
+        )(rows)
 
     came = {}
     with jax.named_scope("halo_z"):
@@ -851,12 +872,14 @@
         )
 
     with jax.named_scope("halo_y"):
-        came[2], key, bounds = lax.optimization_barrier((came[2], key, bounds))
+        came[2], key, bounds, w_first, w_env, w_value, w_second, w_out = lax.optimization_barrier(
+            (came[2], key, bounds, w_first, w_env, w_value, w_second, w_out)
+        )
         came[1] = plan.send(1, glue(plan, 1, (2,), plan.own_rest, own_rows, came))
 
     with jax.named_scope("weights"):
-        wide = jnp.concatenate([w_proj_a, w_proj_b, w_radial], axis=0)
-        narrow = jnp.concatenate([w_first, w_env, w_value, w_second, w_out[None, :]], axis=0)
+        wide = stack(w_proj_a, w_proj_b, w_radial)
+        narrow = stack(w_first, w_env, w_value, w_second, w_out[None, :])
         half, *weights = pl.pallas_call(
             weight_kernel,
             out_shape=[
@@ -864,14 +887,13 @@
                 shape(chans, chans, dtype=BF16),
                 shape(2 * chans, chans, dtype=BF16),
                 shape(chans, 2 * chans, dtype=BF16),
-                shape(chans, chans, dtype=BF16),
+                shape(chans + 2 * n_basis, chans, dtype=BF16),
                 shape(chans, 2 * chans, dtype=BF16),
                 shape(2 * chans, chans, dtype=BF16),
-                shape(2 * n_basis, chans, dtype=BF16),
                 shape(chans, LANES),
             ],
             in_specs=[VMEM] * 3,
-            out_specs=[VMEM] * 9,
+            out_specs=[VMEM] * 8,
             compiler_params=PARAMS,
         )(rows, wide, narrow)
 
@@ -900,7 +922,8 @@
         pltpu.VMEM(planes, BF16),
         pltpu.VMEM(planes, BF16),
         pltpu.VMEM((n_chunks, CHUNK // LANES, LANES), F32),
-        pltpu.VMEM((10, CHUNK // LANES, LANES), F32),
+        pltpu.VMEM((1, CHUNK), F32),
+        pltpu.VMEM((9, CHUNK // LANES, LANES), F32),
         pltpu.VMEM((CHUNK // LANES * n_basis, LANES), F32),
         pltpu.VMEM((CHUNK // LANES * 16, LANES), F32),
         pltpu.VMEM((n_sel, 2 * LANES), F32),

time: 58 us -> 62 us (1.069)
  waiting for transfers between devices: 16.1 us -> 22.3 us
  local copies, waits for them, and re-layouts: 3.87 us -> 1.35 us
  other arithmetic: 0.02 us -> 2.26 us
  Pallas kernels: 22.5 us -> 20.7 us
    ppermute x10, waiting for transfers between devices: 16.1 us -> 22.3 us  [send(): lax.ppermute(message, AXES[a], [(i, (i + step) % n) for i in range(n)])]
    unnamed x32 -> x24, local copies, waits for them, and re-layouts: 3.69 us -> 1.35 us
    pallas_call x1, Pallas kernels: 17 us -> 15.2 us  [local(): pl.pallas_call(lambda *refs: main_kernel(plan, *refs), out_shape=[shape(o...]
    convert_element_type x0 -> x3, other arithmetic: none -> 1.38 us  [stack(): part = jnp.pad(x.astype(dtype), ((at, below), (0, LANES - x.shape[1])))]
    add x0 -> x3, other arithmetic: none -> 0.88 us  [stack(): total = part if total is None else total + part]
  transfers between devices with their start and end apart: 10 -> 10, of which waited for: 7 -> 8; matrix products, arithmetic and copies ran while one was open for 0% -> 0% of each run, Pallas kernels for 6% -> 6%
where the time goes in v1:
time: 62 us; the launch traced here: 61.5 us
  waiting for transfers between devices  22.3 us (36%)
  Pallas kernels  20.7 us (33%)
  starting transfers between devices  13.4 us (22%)
  other arithmetic  2.26 us (4%)
  between operations  1.48 us (2%)
  local copies, waits for them, and re-layouts  1.35 us (2%)
    ppermute x10, waiting for transfers between devices, send(): lax.ppermute(message, AXES[a], [(i, (i + step) % n) for i in range(n)])  22.3 us
    pallas_call x1, Pallas kernels, local(): pl.pallas_call(lambda *refs: main_kernel(plan, *refs), out_shape=[shape(o...  15.2 us
    ppermute x10, starting transfers between devices, send(): lax.ppermute(message, AXES[a], [(i, (i + step) % n) for i in range(n)])  13.4 us
    pallas_call x1, Pallas kernels, local(): pl.pallas_call(lambda *refs: sort_kernel(dead, *refs), out_shape=[shape(n...  2.41 us
    convert_element_type x3, other arithmetic, stack(): part = jnp.pad(x.astype(dtype), ((at, below), (0, LANES - x.shape[1])))  1.38 us
    unnamed x24, local copies, waits for them, and re-layouts  1.35 us
  transfers between devices with their start and end apart: 10, of which 8 were waited for; matrix products, arithmetic and copies ran while one was open for 0% of the time, Pallas kernels for 6%

profile of v1, /device:TPU:0, one launch (start us, length us, event | category | flops | bytes accessed | tf_op | source)
XLA Modules:
  0.0 61.5 jit_solution(8804206580416483903)
XLA Ops:
  0.6 0.7 %convert_bitcast_fusion.1 = f32[2,8]{1,0:T(2,128)S(1)} fusion(s32[1,8,2]{1,2,0:T(2,128)} %param.20), kind=kLoop, calls=%fused_computation.6 | loop fusion | flops 16 | bytes 128 | tf_op jit(solution)/shard_map/prep/convert_element_type | solution.py:794
  1.3 0.0 copy-start.10
  1.3 0.7 %fusion = f32[6,32]{1,0:T(8,128)S(1)} fusion(s32[1,6,32]{2,0,1:T(1,128)} %param.18), kind=kLoop, calls=%fused_computation.4 | loop fusion | flops 192 | bytes 1536 | tf_op jit(solution)/shard_map/prep/convert_element_type | solution.py:794
  2.0 0.0 copy-done.10
  2.0 0.7 %copy-done.4 = f32[3,128]{1,0:T(4,128)S(1)} copy-done((f32[3,128]{1,0:T(4,128)S(1)}, f32[3,128]{1,0:T(4,128)}, u32[]{:S(2)}) %copy-start.4) | copy-done | bytes 1560
  2.7 0.9 %pad_add_fusion.2.refs_0_.rows_ref = f32[160,128]{1,0:T(8,128)S(1)} fusion(f32[2,8]{1,0:T(2,128)S(1)} %convert_bitcast_fusion.1, f32[8,12]{1,0:T(8,128)S(1)} %convert_bitcast_fusion, f32[6,32]{1,0:T(8,128)S(1)} %fusion, f32[3,128]{1,0:T(4,128)S(1)} %copy-done.4, f32[128,128]{1,0:T(8,128)} %param.17), kind=kLoop, calls=%fused_computation.2 | loop fusion | flops 81920 | bytes 150208 | tf_op jit(solution)/shard_map/prep/add | solution.py:795
  3.6 0.0 copy-start.1
  3.6 0.7 %prep.1 = (f32[162,128]{1,0:T(8,128)S(1)}, f32[168,128]{1,0:T(8,128)S(1)}, f32[330,128]{1,0:T(8,128)S(1)}) custom-call(f32[160,128]{1,0:T(8,128)S(1)} %pad_add_fusion.2.refs_0_.rows_ref), custom_call_target="tpu_custom_call" | custom-call | tf_op jit(solution)/shard_map/prep/pallas_call | solution.py:840
  4.3 3.0 %collective-permute-start = (f32[162,128]{1,0:T(8,128)S(1)}, f32[162,128]{1,0:T(8,128)S(1)}, u32[]{:S(2)}, u32[]{:S(2)}) collective-permute-start(f32[162,128]{1,0:T(8,128)S(1)} %get-tuple-element.51), channel_id=1, source_target_pairs={{0,1},{1,0},{2,3},{3,2},{4,5},{5,4},{6,7},{7,6},{8,9},{9,8},{10,11... | collective-permute-start | bytes 248840 | tf_op jit(solution)/shard_map/halo_z/ppermute | solution.py:128
  7.9 0.0 copy-done.2
  7.9 0.0 copy-done.3
  7.9 0.0 copy-start.9
  7.9 2.4 %group_edges.1 = (s32[1,48,128]{2,1,0:T(8,128)S(1)}, s32[2,128]{1,0:T(2,128)S(1)}) custom-call(s32[1]{0:T(128)S(6)} %copy.23.refs_0_, s32[48,128]{1,0:T(8,128)S(1)} %bitcast.14, s32[48,128]{1,0:T(8,128)S(1)} %bitcast.15), custom_call_target="tpu_custom_call" | custom-call | tf_op jit(solution)/shard_map/group_edges/pallas_call | solution.py:858
  10.3 0.0 copy-done
  10.4 0.0 copy-done.1
  10.4 0.0 copy-done.9
  10.4 0.0 collective-permute-done.refs_1_.refs_3_.refs_9_
  10.4 0.0 copy-start.5
  10.4 0.0 copy-start.6
  10.4 0.0 copy-start.7
  10.4 0.0 copy-start.8
  10.5 3.7 %collective-permute-start.1 = (f32[81,128]{1,0:T(8,128)S(1)}, f32[81,128]{1,0:T(8,128)S(1)}, u32[]{:S(2)}, u32[]{:S(2)}) collective-permute-start(f32[81,128]{1,0:T(8,128)S(1)} %get-tuple-element.58), channel_id=1, source_target_pairs={{0,6},{2,0},{4,2},{6,4},{1,7},{3,1},{5,3},{7,5},{8,14},{10,8},{12,... | collective-permute-start | bytes 124424 | tf_op jit(solution)/shard_map/halo_y/ppermute | solution.py:128
  14.1 0.0 collective-permute-start.2
  14.1 0.0 copy-done.5
  14.1 0.0 copy-done.6
  14.1 0.0 copy-done.7
  14.2 0.0 copy-done.8
  14.2 0.6 %copy-done.11 = bf16[128]{0:T(256)(128)(2,1)S(1)} copy-done((bf16[128]{0:T(256)(128)(2,1)S(1)}, bf16[128]{0:T(256)(128)(2,1)}, u32[]{:S(2)}) %copy-start.11) | copy-done | bytes 280
  14.8 0.3 weights.1
  15.1 0.7 %collective-permute-done.1.refs_1_.refs_7_ = f32[81,128]{1,0:T(8,128)S(1)} collective-permute-done((f32[81,128]{1,0:T(8,128)S(1)}, f32[81,128]{1,0:T(8,128)S(1)}, u32[]{:S(2)}, u32[]{:S(2)}) %collective-permute-start.1) | collective-permute-done | bytes 41504 | tf_op jit(solution)/shard_map/halo_y/ppermute | solution.py:128
  15.8 4.1 %collective-permute-done.2.refs_2_.refs_8_ = f32[81,128]{1,0:T(8,128)S(1)} collective-permute-done((f32[81,128]{1,0:T(8,128)S(1)}, f32[81,128]{1,0:T(8,128)S(1)}, u32[]{:S(2)}, u32[]{:S(2)}) %collective-permute-start.2) | collective-permute-done | bytes 41504 | tf_op jit(solution)/shard_map/halo_y/ppermute | solution.py:128
  20.0 0.1 collective-permute-start.3
  20.1 0.5 collective-permute-start.4
  20.6 1.2 %collective-permute-done.3.refs_5_ = f32[81,128]{1,0:T(8,128)S(1)} collective-permute-done((f32[81,128]{1,0:T(8,128)S(1)}, f32[81,128]{1,0:T(8,128)S(1)}, u32[]{:S(2)}, u32[]{:S(2)}) %collective-permute-start.3) | collective-permute-done | bytes 41504 | tf_op jit(solution)/shard_map/halo_x/ppermute | solution.py:128
  21.8 2.3 %collective-permute-done.4.refs_6_ = f32[81,128]{1,0:T(8,128)S(1)} collective-permute-done((f32[81,128]{1,0:T(8,128)S(1)}, f32[81,128]{1,0:T(8,128)S(1)}, u32[]{:S(2)}, u32[]{:S(2)}) %collective-permute-start.4) | collective-permute-done | bytes 41504 | tf_op jit(solution)/shard_map/halo_x/ppermute | solution.py:128
  24.1 15.2 %layer.1 = (f32[144,128]{1,0:T(8,128)S(1)}, f32[256,256]{1,0:T(8,128)S(1)}, f32[81,128]{1,0:T(8,128)S(1)}, f32[81,128]{1,0:T(8,128)S(1)}, f32[168,128]{1,0:T(8,128)S(1)}) custom-call(s32[1]{0:T(128)S(6)} %copy.23.refs_0_, s32[2,128]{1,0:T(2,128)S(1)} %get-tuple-element.54.refs_1_, s32[1,48,128]{2,1,0:T(8,128)S(1)} %get-tuple-element.55.refs_2_, ...), custom_call_target="tpu_custom_call" | custom-call | tf_op jit(solution)/shard_map/layer/pallas_call | solution.py:934
  39.2 0.2 collective-permute-start.5
  39.4 1.6 %collective-permute-start.6 = (f32[81,128]{1,0:T(8,128)S(1)}, f32[81,128]{1,0:T(8,128)S(1)}, u32[]{:S(2)}, u32[]{:S(2)}) collective-permute-start(f32[81,128]{1,0:T(8,128)S(1)} %get-tuple-element.90), channel_id=1, source_target_pairs={{0,24},{8,0},{16,8},{24,16},{1,25},{9,1},{17,9},{25,17},{2,26},{10... | collective-permute-start | bytes 124424 | tf_op jit(solution)/shard_map/halo_back/ppermute | solution.py:128
  41.0 1.7 %collective-permute-done.5.refs_1_.refs_3_.refs_4_ = f32[81,128]{1,0:T(8,128)S(1)} collective-permute-done((f32[81,128]{1,0:T(8,128)S(1)}, f32[81,128]{1,0:T(8,128)S(1)}, u32[]{:S(2)}, u32[]{:S(2)}) %collective-permute-start.5) | collective-permute-done | bytes 41504 | tf_op jit(solution)/shard_map/halo_back/ppermute | solution.py:128
  42.8 6.6 %collective-permute-done.6.refs_2_.refs_4_.refs_5_ = f32[81,128]{1,0:T(8,128)S(1)} collective-permute-done((f32[81,128]{1,0:T(8,128)S(1)}, f32[81,128]{1,0:T(8,128)S(1)}, u32[]{:S(2)}, u32[]{:S(2)}) %collective-permute-start.6) | collective-permute-done | bytes 41504 | tf_op jit(solution)/shard_map/halo_back/ppermute | solution.py:128
  49.4 0.1 collective-permute-start.7
  49.4 3.8 %collective-permute-start.8 = (f32[81,128]{1,0:T(8,128)S(1)}, f32[81,128]{1,0:T(8,128)S(1)}, u32[]{:S(2)}, u32[]{:S(2)}) collective-permute-start(f32[81,128]{1,0:T(8,128)S(1)} %get-tuple-element.93), channel_id=1, source_target_pairs={{0,6},{2,0},{4,2},{6,4},{1,7},{3,1},{5,3},{7,5},{8,14},{10,8},{12,... | collective-permute-start | bytes 124424 | tf_op jit(solution)/shard_map/halo_back/ppermute | solution.py:128
  53.3 2.1 %collective-permute-done.7.refs_1_.refs_6_ = f32[81,128]{1,0:T(8,128)S(1)} collective-permute-done((f32[81,128]{1,0:T(8,128)S(1)}, f32[81,128]{1,0:T(8,128)S(1)}, u32[]{:S(2)}, u32[]{:S(2)}) %collective-permute-start.7) | collective-permute-done | bytes 41504 | tf_op jit(solution)/shard_map/halo_back/ppermute | solution.py:128
  55.3 0.0 collective-permute-done.8.refs_2_.refs_7_
  55.3 0.5 collective-permute-start.9
  55.9 0.8 %own_part.1 = (f32[1,128]{1,0:T(1,128)}, f32[128,128]{1,0:T(8,128)S(1)}, f32[3,128]{1,0:T(4,128)S(1)}) custom-call(f32[144,128]{1,0:T(8,128)S(1)} %get-tuple-element.85.ae_ref, f32[256,256]{1,0:T(8,128)S(1)} %get-tuple-element.86.own_ref, f32[128,128]{1,0:T(8,128)S(1)} %copy-done.1, f32[128,128]{1,0:T(8,128)S(1)} %copy-done), custom_call_target="tpu_custom_call" | custom-call | tf_op jit(solution)/shard_map/own_part/pallas_call | solution.py:951
  56.7 3.6 %collective-permute-done.9.refs_8_ = f32[162,128]{1,0:T(8,128)S(1)} collective-permute-done((f32[162,128]{1,0:T(8,128)S(1)}, f32[162,128]{1,0:T(8,128)S(1)}, u32[]{:S(2)}, u32[]{:S(2)}) %collective-permute-start.9) | collective-permute-done | bytes 82976 | tf_op jit(solution)/shard_map/halo_back/ppermute | solution.py:128
  60.3 1.2 %owner_sums.1 = (f32[3,128]{1,0:T(4,128)}, f32[128,128]{1,0:T(8,128)}) custom-call(f32[330,128]{1,0:T(8,128)S(1)} %get-tuple-element.50.refs_0_, f32[128,128]{1,0:T(8,128)S(1)} %get-tuple-element.87.refs_1_, f32[3,128]{1,0:T(4,128)S(1)} %get-tuple-element.88.refs_2_, f32[128,128]{1,0:T(8,128)S(1)} %copy-done, ...), custom_call_target="tpu_custom_call" | custom-call | tf_op jit(solution)/shard_map/owner_sums/pallas_call | solution.py:961
  (12 shorter events, 0.1 us)
Async XLA Ops:
  1.3 0.7 %copy-start.10 = (s32[1,12,8]{1,2,0:T(8,128)S(1)}, s32[1,12,8]{1,2,0:T(8,128)}, u32[]{:S(2)}) copy-start(s32[1,12,8]{1,2,0:T(8,128)} %param.19) | copy-start | bytes 1156
  2.0 0.7 %copy-start.4 = (f32[3,128]{1,0:T(4,128)S(1)}, f32[3,128]{1,0:T(4,128)}, u32[]{:S(2)}) copy-start(f32[3,128]{1,0:T(4,128)} %refs_3_.2) | copy-start | bytes 4612
  2.7 5.2 %copy-start.2 = (s32[6144]{0:T(1024)S(1)}, s32[6144]{0:T(1024)}, u32[]{:S(2)}) copy-start(s32[6144]{0:T(1024)} %param.21) | copy-start | bytes 73732
  2.7 5.2 %copy-start.3 = (s32[6144]{0:T(1024)S(1)}, s32[6144]{0:T(1024)}, u32[]{:S(2)}) copy-start(s32[6144]{0:T(1024)} %param.22) | copy-start | bytes 73732
  3.6 6.8 %copy-start = (f32[128,128]{1,0:T(8,128)S(1)}, f32[128,128]{1,0:T(8,128)}, u32[]{:S(2)}) copy-start(f32[128,128]{1,0:T(8,128)} %refs_3_.3) | copy-start | bytes 196612
  3.6 6.8 %copy-start.1 = (f32[128,128]{1,0:T(8,128)S(1)}, f32[128,128]{1,0:T(8,128)}, u32[]{:S(2)}) copy-start(f32[128,128]{1,0:T(8,128)} %wa_ref.1) | copy-start | bytes 196612
  4.3 6.1 %collective-permute-start = (f32[162,128]{1,0:T(8,128)S(1)}, f32[162,128]{1,0:T(8,128)S(1)}, u32[]{:S(2)}, u32[]{:S(2)}) collective-permute-start(f32[162,128]{1,0:T(8,128)S(1)} %get-tuple-element.51), channel_id=1, source_target_pairs={{0,1},{1,0},{2,3},{3,2},{4,5},{5,4},{6,7},{7,6},{8,9},{9,8},{10,11... | collective-permute-start | bytes 248840 | tf_op jit(solution)/shard_map/halo_z/ppermute | solution.py:128
  7.9 2.4 %copy-start.9 = (f32[8,128]{1,0:T(8,128)S(1)}, f32[8,128]{1,0:T(8,128)}, u32[]{:S(2)}) copy-start(f32[8,128]{1,0:T(8,128)} %param.26) | copy-start | bytes 12292
  10.4 3.7 %copy-start.5 = (bf16[256,128]{1,0:T(8,128)(2,1)S(1)}, bf16[256,128]{1,0:T(8,128)(2,1)}, u32[]{:S(2)}) copy-start(bf16[256,128]{1,0:T(8,128)(2,1)} %param.30) | copy-start | bytes 196612
  10.4 3.7 %copy-start.6 = (bf16[128,128]{1,0:T(8,128)(2,1)S(1)}, bf16[128,128]{1,0:T(8,128)(2,1)}, u32[]{:S(2)}) copy-start(bf16[128,128]{1,0:T(8,128)(2,1)} %param.29) | copy-start | bytes 98308
  10.4 3.7 %copy-start.7 = (bf16[128,128]{1,0:T(8,128)(2,1)S(1)}, bf16[128,128]{1,0:T(8,128)(2,1)}, u32[]{:S(2)}) copy-start(bf16[128,128]{1,0:T(8,128)(2,1)} %param.28) | copy-start | bytes 98308
  10.4 3.7 %copy-start.8 = (bf16[128,128]{1,0:T(8,128)(2,1)S(1)}, bf16[128,128]{1,0:T(8,128)(2,1)}, u32[]{:S(2)}) copy-start(bf16[128,128]{1,0:T(8,128)(2,1)} %param.27) | copy-start | bytes 98308
  10.5 5.4 %collective-permute-start.1 = (f32[81,128]{1,0:T(8,128)S(1)}, f32[81,128]{1,0:T(8,128)S(1)}, u32[]{:S(2)}, u32[]{:S(2)}) collective-permute-start(f32[81,128]{1,0:T(8,128)S(1)} %get-tuple-element.58), channel_id=1, source_target_pairs={{0,6},{2,0},{4,2},{6,4},{1,7},{3,1},{5,3},{7,5},{8,14},{10,8},{12,... | collective-permute-start | bytes 124424 | tf_op jit(solution)/shard_map/halo_y/ppermute | solution.py:128
  14.1 0.7 %copy-start.11 = (bf16[128]{0:T(256)(128)(2,1)S(1)}, bf16[128]{0:T(256)(128)(2,1)}, u32[]{:S(2)}) copy-start(bf16[128]{0:T(256)(128)(2,1)} %param.31) | copy-start | bytes 772
  14.1 5.8 %collective-permute-start.2 = (f32[81,128]{1,0:T(8,128)S(1)}, f32[81,128]{1,0:T(8,128)S(1)}, u32[]{:S(2)}, u32[]{:S(2)}) collective-permute-start(f32[81,128]{1,0:T(8,128)S(1)} %get-tuple-element.59), channel_id=1, source_target_pairs={{0,2},{2,4},{4,6},{6,0},{1,3},{3,5},{5,7},{7,1},{8,10},{10,12},{12... | collective-permute-start | bytes 124424 | tf_op jit(solution)/shard_map/halo_y/ppermute | solution.py:128
  20.0 1.8 %collective-permute-start.3 = (f32[81,128]{1,0:T(8,128)S(1)}, f32[81,128]{1,0:T(8,128)S(1)}, u32[]{:S(2)}, u32[]{:S(2)}) collective-permute-start(f32[81,128]{1,0:T(8,128)S(1)} %get-tuple-element.75), channel_id=1, source_target_pairs={{0,24},{8,0},{16,8},{24,16},{1,25},{9,1},{17,9},{25,17},{2,26},{10... | collective-permute-start | bytes 124424 | tf_op jit(solution)/shard_map/halo_x/ppermute | solution.py:128
  20.1 4.0 %collective-permute-start.4 = (f32[81,128]{1,0:T(8,128)S(1)}, f32[81,128]{1,0:T(8,128)S(1)}, u32[]{:S(2)}, u32[]{:S(2)}) collective-permute-start(f32[81,128]{1,0:T(8,128)S(1)} %get-tuple-element.76), channel_id=1, source_target_pairs={{0,8},{8,16},{16,24},{24,0},{1,9},{9,17},{17,25},{25,1},{2,10},{10... | collective-permute-start | bytes 124424 | tf_op jit(solution)/shard_map/halo_x/ppermute | solution.py:128
  39.2 3.5 %collective-permute-start.5 = (f32[81,128]{1,0:T(8,128)S(1)}, f32[81,128]{1,0:T(8,128)S(1)}, u32[]{:S(2)}, u32[]{:S(2)}) collective-permute-start(f32[81,128]{1,0:T(8,128)S(1)} %get-tuple-element.89), channel_id=1, source_target_pairs={{0,8},{8,16},{16,24},{24,0},{1,9},{9,17},{17,25},{25,1},{2,10},{10... | collective-permute-start | bytes 124424 | tf_op jit(solution)/shard_map/halo_back/ppermute | solution.py:128
  39.4 10.0 %collective-permute-start.6 = (f32[81,128]{1,0:T(8,128)S(1)}, f32[81,128]{1,0:T(8,128)S(1)}, u32[]{:S(2)}, u32[]{:S(2)}) collective-permute-start(f32[81,128]{1,0:T(8,128)S(1)} %get-tuple-element.90), channel_id=1, source_target_pairs={{0,24},{8,0},{16,8},{24,16},{1,25},{9,1},{17,9},{25,17},{2,26},{10... | collective-permute-start | bytes 124424 | tf_op jit(solution)/shard_map/halo_back/ppermute | solution.py:128
  49.4 5.9 %collective-permute-start.7 = (f32[81,128]{1,0:T(8,128)S(1)}, f32[81,128]{1,0:T(8,128)S(1)}, u32[]{:S(2)}, u32[]{:S(2)}) collective-permute-start(f32[81,128]{1,0:T(8,128)S(1)} %get-tuple-element.92), channel_id=1, source_target_pairs={{0,2},{2,4},{4,6},{6,0},{1,3},{3,5},{5,7},{7,1},{8,10},{10,12},{12... | collective-permute-start | bytes 124424 | tf_op jit(solution)/shard_map/halo_back/ppermute | solution.py:128
  49.4 5.9 %collective-permute-start.8 = (f32[81,128]{1,0:T(8,128)S(1)}, f32[81,128]{1,0:T(8,128)S(1)}, u32[]{:S(2)}, u32[]{:S(2)}) collective-permute-start(f32[81,128]{1,0:T(8,128)S(1)} %get-tuple-element.93), channel_id=1, source_target_pairs={{0,6},{2,0},{4,2},{6,4},{1,7},{3,1},{5,3},{7,5},{8,14},{10,8},{12,... | collective-permute-start | bytes 124424 | tf_op jit(solution)/shard_map/halo_back/ppermute | solution.py:128
  55.3 4.9 %collective-permute-start.9 = (f32[162,128]{1,0:T(8,128)S(1)}, f32[162,128]{1,0:T(8,128)S(1)}, u32[]{:S(2)}, u32[]{:S(2)}) collective-permute-start(f32[162,128]{1,0:T(8,128)S(1)} %halo_back.3), channel_id=1, source_target_pairs={{0,1},{1,0},{2,3},{3,2},{4,5},{5,4},{6,7},{7,6},{8,9},{9,8},{10,11... | collective-permute-start | bytes 248840 | tf_op jit(solution)/shard_map/halo_back/ppermute | solution.py:128

commit v2 on v1

--- a/solution.py
+++ b/solution.py
@@ -11,7 +11,7 @@
 BF16 = jnp.bfloat16
 HIGH = lax.Precision.HIGHEST
 AXES = ("gx", "gy", "gz")
-CHUNK = 6144
+CHUNK = 3072
 SUB = 256
 WIN = 16
 OTHER_BITS = 9
@@ -221,17 +221,40 @@
     )(*given)
 
 
-def sort_kernel(dead, count_ref, centre_ref, other_ref, key_ref, bound_ref, turn_ref):
+def sort_kernel(own, count_ref, centre_ref, other_ref, key_ref, bound_ref, turn_ref):
+    dead = (own - 1) * (OTHER_MASK + 1) + OTHER_MASK
     rows = centre_ref.shape[0]
     regs = turn_ref.shape[0] // 16
     group = regs * 8
     row = lax.broadcasted_iota(jnp.int32, (rows, LANES), 0)
     lane = lax.broadcasted_iota(jnp.int32, (rows, LANES), 1)
-    key = jnp.where(
-        row * LANES + lane < count_ref[0], (centre_ref[...] << OTHER_BITS) + other_ref[...], dead
-    ).astype(F32)
+    live = row * LANES + lane < count_ref[0]
+    centre = centre_ref[...]
+    key = jnp.where(live, (centre << OTHER_BITS) + other_ref[...], dead).astype(F32)
     x = [key[8 * v : 8 * v + 8, :] for v in range(rows // 8)]
     x += [jnp.full((8, LANES), float(dead), F32)] * (regs - len(x))
+    n_windows = own // WIN
+    free = regs - rows // 8
+    if n_windows * SUB <= free * 8 * LANES:
+        window = jnp.where(live, centre // WIN, -1)
+        need = []
+        used = jnp.zeros((1, 1), F32)
+        for w in range(n_windows):
+            hits = jnp.sum((window == w).astype(F32), axis=0, keepdims=True)
+            hits = jnp.sum(hits, axis=1, keepdims=True)
+            whole = jnp.floor((hits + (SUB - 1)) * (1.0 / SUB)) * SUB
+            used = used + whole
+            need.append(whole - hits)
+        fits = used <= float(rows * LANES)
+        slot = lax.broadcasted_iota(jnp.int32, (8, LANES), 0) * LANES
+        slot = slot + lax.broadcasted_iota(jnp.int32, (8, LANES), 1)
+        per_reg = 8 * LANES // SUB
+        for w in range(n_windows):
+            v = rows // 8 + w // per_reg
+            at = slot - (w % per_reg) * SUB
+            take = (at >= 0) & (at.astype(F32) < need[w]) & fits
+            mark = float((w * WIN + WIN - 1) * (OTHER_MASK + 1) + OTHER_MASK)
+            x[v] = jnp.where(take, mark, x[v])
     s = lax.broadcasted_iota(jnp.int32, (8, LANES), 0)
     ln = lax.broadcasted_iota(jnp.int32, (8, LANES), 1)
     base = ln * group + s * regs
@@ -396,8 +419,8 @@
 
 
 def main_kernel(plan, *refs):
-    count_ref, bound_ref, key_ref, pos_ref, wb_ref = refs[:5]
-    came, refs = plan.cut(refs[5:], 0, 1, 2)
+    bound_ref, key_ref, pos_ref, wb_ref = refs[:4]
+    came, refs = plan.cut(refs[4:], 0, 1, 2)
     half_ref, w1t_ref, wevt_ref, w2t_ref, w1_ref, wev_ref, w2_ref, wcol_ref = refs[:8]
     ae_ref, own_ref = refs[8:10]
     n_x = len(plan.groups[0])
@@ -422,11 +445,11 @@
         dv_ref,
         dfa_ref,
         live_ref,
-        energy_ref,
         dy_ref,
         db_ref,
         dr_ref,
         acc_ref,
+        cacc_ref,
     ) = refs[11 + n_x :]
     own = pos_ref.shape[1]
     chans = w1_ref.shape[1]
@@ -462,7 +485,7 @@
     keys = key_ref[...].reshape(rows_all, LANES)
     centre = keys >> OTHER_BITS
     other = keys & OTHER_MASK
-    valid = (keys != (own - 1) * (OTHER_MASK + 1) + OTHER_MASK).astype(F32)
+    valid = (other != OTHER_MASK).astype(F32)
     r = [
         look_up(pos_t[a : a + 1, :], other) - look_up(pos_t[a : a + 1, 0:LANES], centre)
         for a in range(3)
@@ -486,13 +509,12 @@
     denv_ref[...] = jnp.zeros_like(denv_ref)
     ae_ref[...] = jnp.zeros_like(ae_ref)
     acc_ref[...] = jnp.zeros_like(acc_ref)
+    cacc_ref[...] = jnp.zeros_like(cacc_ref)
     dr_ref[...] = jnp.zeros_like(dr_ref)
 
-    bound_total = sorted_size(rows_all * LANES)
-    n_chunks = lax.div(count_ref[0] + (CHUNK - 1), jnp.int32(CHUNK))
+    groups = bound_ref.shape[1] * SUB // sorted_size(rows_all * LANES)
 
     def window(k, s):
-        groups = bound_ref.shape[1] * SUB // bound_total
         first = (k * subs + s) * groups
         low = bound_ref[0, first]
         high = low
@@ -503,21 +525,47 @@
         return start, more
 
     most = jnp.int32(0)
+    n_chunks = jnp.int32(0)
     for s in range(rows_all // sub_rows):
         most = jnp.maximum(most, window(s // subs, s % subs)[1])
+        for g in range(groups):
+            any_live = bound_ref[1, s * groups + g] >= 0
+            n_chunks = jnp.where(any_live, s // subs + 1, n_chunks)
+
+
+    def lanes_of(s, n):
+        if isinstance(s, int):
+            return slice(s * SUB, (s + n) * SUB)
+        return pl.ds(pl.multiple_of(s * SUB, SUB), n * SUB)
+
+    def tile_of(load, s, n):
+        if isinstance(s, int):
+            return load(slice(s * sub_rows, (s + n) * sub_rows))
+        return jnp.concatenate(
+            [load(pl.ds(s * sub_rows + j, 1)) for j in range(n * sub_rows)], axis=0
+        )
+
+    def plane(i, k, s, n):
+        return tile_of(lambda rows: geo_ref[i, k, rows, :], s, n)
+
+    def keys_of(k, s, n):
+        return tile_of(lambda rows: key_ref[k, rows, :], s, n)
+
+    def stacked(ref, k, s, n, height):
+        first = (k * subs + s) * sub_rows
+        tiles = [
+            ref[pl.ds(pl.multiple_of((first + j) * height, 8), height), :]
+            for j in range(n * sub_rows)
+        ]
+        return jnp.concatenate(tiles, axis=1)
 
     def window_hot(k, s, start):
-        rows = [key_ref[k, pl.ds(s * sub_rows + j, 1), :] for j in range(sub_rows)]
-        crow = (jnp.concatenate(rows, axis=1) >> OTHER_BITS) - start
+        crow = in_lanes(keys_of(k, s, 1) >> OTHER_BITS) - start
         return lax.broadcasted_iota(jnp.int32, (WIN, SUB), 0) == crow
 
     def select(k, s, start):
-        row = k * per + s * sub_rows
         hot = window_hot(k, s, start)
-        tiles = [
-            y_ref[pl.ds(pl.multiple_of((row + j) * 8, 8), 8), :] for j in range(sub_rows)
-        ]
-        ys = jnp.concatenate(tiles, axis=1)
+        ys = stacked(y_ref, k, s, 1, 8)
         parts = [hot.astype(F32)]
         for m in range(8):
             parts.append(jnp.where(hot, ys[m : m + 1, :], 0.0))
@@ -532,40 +580,33 @@
         for m in range(9):
             ref[m, pl.ds(start, WIN), :] += rows[m * WIN : (m + 1) * WIN, :]
 
-    def sub_lanes(s):
-        if isinstance(s, int):
-            return slice(s * SUB, (s + 1) * SUB)
-        return pl.ds(pl.multiple_of(s * SUB, SUB), SUB)
-
-    def more_windows(k, body):
-        @pl.when(most > 0)
-        def _():
-            def over(s, carry):
-                start, more = window(k, s)
-
-                def step(t, carry):
-                    body(s, pl.multiple_of(start + t * WIN, 8))
+    def each_window(k, s, n, slow, body):
+        for j in range(n):
+            start, more = window(k, s + j)
+            body(s + j, j, start, True)
+            if slow:
+
+                def step(i, carry, s=s, j=j, start=start):
+                    body(s + j, j, pl.multiple_of(start + i * WIN, 8), False)
                     return carry
 
-                return lax.fori_loop(1, more + 1, step, carry)
-
-            lax.fori_loop(0, subs, over, 0)
-
-    def row_of(plane, k):
-        return in_lanes(geo_ref[plane, k])
-
-    def phase_a(k, carry):
-        kt = key_ref[k]
-        crow = in_lanes(kt >> OTHER_BITS)
-        orow = in_lanes(kt & OTHER_MASK)
-        hots = [one_hot(crow, 0, own)]
-        for base in range(0, n_tab, LANES):
-            hots.append(one_hot(orow, base, min(LANES, n_tab - base)))
-        tiles = [
-            basis_ref[pl.ds(pl.multiple_of((k * per + j) * n_basis, 8), n_basis), :]
-            for j in range(per)
-        ]
-        basis = jnp.concatenate(tiles, axis=1)
+                lax.fori_loop(1, more + 1, step, 0)
+
+    def kept(k, s, start, fresh):
+        return a_ref[k * subs + s] if fresh else select(k, s, start)
+
+    def table_hots(k, s, n):
+        row = in_lanes(keys_of(k, s, n) & OTHER_MASK)
+        return [one_hot(row, at, min(LANES, n_tab - at)) for at in range(0, n_tab, LANES)]
+
+    def part(j):
+        return slice(j * SUB, (j + 1) * SUB)
+
+    def phase_a(k, s, n, slow):
+        lanes = lanes_of(s, n)
+        crow = in_lanes(keys_of(k, s, n) >> OTHER_BITS)
+        hots = [one_hot(crow, 0, own)] + table_hots(k, s, n)
+        basis = stacked(basis_ref, k, s, n, n_basis)
         b_hi, b_lo = split(basis)
         hots.append(jnp.concatenate([b_hi, b_lo], axis=0).astype(BF16))
         hots.append(jnp.concatenate([b_hi, jnp.zeros_like(b_hi)], axis=0).astype(BF16))
@@ -573,170 +614,169 @@
         z1 = dot_nn(w1t_ref[...], mixed)
         sg = 0.5 + 0.5 * jnp.tanh(0.5 * z1)
         first = z1 * sg
-        dsilu_ref[k] = (sg + first * (1.0 - sg)).astype(BF16)
+        dsilu_ref[k, :, lanes] = (sg + first * (1.0 - sg)).astype(BF16)
         first = first.astype(BF16)
-        first_ref[k] = first
+        first_ref[k, :, lanes] = first
         both = dot_nn(wevt_ref[...], first)
-        ew = (both[0:chans] * row_of(6, k)).astype(BF16)
-        ew_ref[k] = ew
-        val_ref[k] = both[chans:].astype(BF16)
-        for s in range(subs):
-            start, _ = window(k, s)
+        ew = (both[0:chans] * in_lanes(plane(6, k, s, n))).astype(BF16)
+        ew_ref[k, :, lanes] = ew
+        val_ref[k, :, lanes] = both[chans:].astype(BF16)
+
+        def body(s, j, start, fresh):
             a = select(k, s, start)
-            a_ref[k * subs + s] = a
-            add_window(env_ref, start, dot_nt(a, ew[:, sub_lanes(s)]))
-
-        def again(s, start):
-            a = select(k, s, start)
-            add_window(env_ref, start, dot_nt(a, ew_ref[k, :, sub_lanes(s)]))
-
-        more_windows(k, again)
-        return carry
-
-    lax.fori_loop(0, n_chunks, phase_a, 0)
-
-    def phase_b(k, carry):
-        for s in range(subs):
-            start, _ = window(k, s)
-            big_ref[:, sub_lanes(s)] = dot_tn(load_window(env_ref, start), a_ref[k * subs + s])
-
-        def again_total(s, start):
-            big_ref[:, sub_lanes(s)] += dot_tn(load_window(env_ref, start), select(k, s, start))
-
-        more_windows(k, again_total)
-        total = 0.2 * big_ref[...]
-        value = val_ref[k].astype(F32)
+            if fresh:
+                a_ref[k * subs + s] = a
+            add_window(env_ref, start, dot_nt(a, ew[:, part(j)]))
+
+        each_window(k, s, n, slow, body)
+
+    def phase_b(k, s, n, slow):
+        lanes = lanes_of(s, n)
+
+        def totals(s, j, start, fresh):
+            value = dot_tn(load_window(env_ref, start), kept(k, s, start, fresh))
+            if fresh:
+                big_ref[:, part(j)] = value
+            else:
+                big_ref[:, part(j)] += value
+
+        each_window(k, s, n, slow, totals)
+        total = 0.2 * big_ref[:, 0 : n * SUB]
+        value = val_ref[k, :, lanes].astype(F32)
         scalar = (value * total).astype(BF16)
-        z2 = dot_nn(w2t_ref[...], jnp.concatenate([first_ref[k], scalar], axis=0))
+        z2 = dot_nn(w2t_ref[...], jnp.concatenate([first_ref[k, :, lanes], scalar], axis=0))
         sg = 0.5 + 0.5 * jnp.tanh(0.5 * z2)
         second = z2 * sg
-        wcol = jnp.concatenate([wcol_ref[...]] * per, axis=1)
+        wcol = jnp.concatenate([wcol_ref[...]] * (n * sub_rows), axis=1)
         ee = jnp.sum(second.astype(BF16).astype(F32) * wcol, axis=0, keepdims=True)
-        envv = row_of(6, k)
-        live = ee * row_of(7, k)
-        for j in range(per):
-            live_ref[k, j : j + 1, :] = live[:, j * LANES : (j + 1) * LANES]
-        energy_ref[...] = ee * envv
+        envv = in_lanes(plane(6, k, s, n))
+        live = ee * in_lanes(plane(7, k, s, n))
+        first_row = s * sub_rows
+        for j in range(n * sub_rows):
+            live_ref[k, pl.ds(first_row + j, 1), :] = live[:, j * LANES : (j + 1) * LANES]
+        energy = ee * envv
         dz2 = ((wcol * envv) * (sg + second * (1.0 - sg))).astype(BF16)
         dj = dot_nn(w2_ref[...], dz2)
-        dfa_ref[k] = dj[0:chans].astype(BF16)
+        dfa_ref[k, :, lanes] = dj[0:chans].astype(BF16)
         dscalar = dj[chans:]
         dt = (0.2 * value * dscalar).astype(BF16)
-        dt_ref[k] = dt
-        dv_ref[k] = (total * dscalar).astype(BF16)
-
-        def add_energy(s, start):
-            hot = window_hot(k, s, start)
-            part = jnp.where(hot, energy_ref[:, sub_lanes(s)], 0.0)
-            half = part[:, 0:LANES]
-            for j in range(1, sub_rows):
-                half = half + part[:, j * LANES : (j + 1) * LANES]
+        dt_ref[k, :, lanes] = dt
+        dv_ref[k, :, lanes] = (total * dscalar).astype(BF16)
+
+        def body(s, j, start, fresh):
+            add_window(denv_ref, start, dot_nt(kept(k, s, start, fresh), dt[:, part(j)]))
+            mine = jnp.where(window_hot(k, s, start), energy[:, part(j)], 0.0)
+            half = mine[:, 0:LANES]
+            for i in range(1, sub_rows):
+                half = half + mine[:, i * LANES : (i + 1) * LANES]
             ae_ref[pl.ds(start, WIN), :] += half
 
-        for s in range(subs):
-            start, _ = window(k, s)
-            add_window(denv_ref, start, dot_nt(a_ref[k * subs + s], dt[:, sub_lanes(s)]))
-            add_energy(s, start)
-
-        def again(s, start):
-            add_window(
-                denv_ref, start, dot_nt(select(k, s, start), dt_ref[k, :, sub_lanes(s)])
-            )
-            add_energy(s, start)
-
-        more_windows(k, again)
-        return carry
-
-    lax.fori_loop(0, n_chunks, phase_b, 0)
-
-    def phase_c(k, carry):
-        def env_terms(s, start, a, fresh):
+        each_window(k, s, n, slow, body)
+
+    def phase_c(k, s, n, slow):
+        lanes = lanes_of(s, n)
+        height = n * sub_rows
+
+        def env_terms(s, j, start, fresh):
+            a = kept(k, s, start, fresh)
             e_win = load_window(env_ref, start)
             d_win = load_window(denv_ref, start)
             dew = dot_tn(d_win, a)
-            pair = jnp.concatenate(
-                [dt_ref[k, :, sub_lanes(s)], ew_ref[k, :, sub_lanes(s)]], axis=0
-            )
+            here = lanes_of(s, 1)
+            pair = jnp.concatenate([dt_ref[k, :, here], ew_ref[k, :, here]], axis=0)
             prods = dot_nn(jnp.concatenate([e_win, d_win], axis=1), pair)
             hot = a[0:WIN].astype(F32)
             if fresh:
-                big_ref[:, sub_lanes(s)] = dew
+                big_ref[:, part(j)] = dew
             else:
-                big_ref[:, sub_lanes(s)] += dew
+                big_ref[:, part(j)] += dew
             for m in range(1, 9):
                 row = jnp.sum(prods[m * WIN : (m + 1) * WIN] * hot, axis=0, keepdims=True)
-                for j in range(sub_rows):
-                    at = s * sub_rows + j
-                    piece = row[:, j * LANES : (j + 1) * LANES]
+                for i in range(sub_rows):
+                    at = j * sub_rows + i
+                    piece = row[:, i * LANES : (i + 1) * LANES]
                     if fresh:
-                        dy_ref[m, pl.ds(at, 1), :] = piece
+                        dy_ref[m, at : at + 1, :] = piece
                     else:
-                        dy_ref[m, pl.ds(at, 1), :] += piece
-
-        for s in range(subs):
-            start, _ = window(k, s)
-            env_terms(s, start, a_ref[k * subs + s], True)
-        more_windows(k, lambda s, start: env_terms(s, start, select(k, s, start), False))
-        dew = big_ref[...]
-        dpre = (dew * row_of(6, k)).astype(BF16)
-        denv_row = jnp.sum(dew * ew_ref[k].astype(F32), axis=0, keepdims=True)
-        for j in range(per):
+                        dy_ref[m, at : at + 1, :] += piece
+
+        each_window(k, s, n, slow, env_terms)
+        dew = big_ref[:, 0 : n * SUB]
+        dpre = (dew * in_lanes(plane(6, k, s, n))).astype(BF16)
+        denv_row = jnp.sum(dew * ew_ref[k, :, lanes].astype(F32), axis=0, keepdims=True)
+        for j in range(height):
             dy_ref[0, j : j + 1, :] = denv_row[:, j * LANES : (j + 1) * LANES]
-        dfirst = dfa_ref[k].astype(F32) + dot_nn(
-            wev_ref[...], jnp.concatenate([dpre, dv_ref[k]], axis=0)
+        dfirst = dfa_ref[k, :, lanes].astype(F32) + dot_nn(
+            wev_ref[...], jnp.concatenate([dpre, dv_ref[k, :, lanes]], axis=0)
         )
-        dz1 = (dfirst * dsilu_ref[k].astype(F32)).astype(BF16)
+        dz1 = (dfirst * dsilu_ref[k, :, lanes].astype(F32)).astype(BF16)
         dboth = dot_nn(w1_ref[...], dz1)
         dmixed = dboth[0:chans].astype(BF16)
         dbasis = dboth[chans:]
-        for j in range(per):
+        for j in range(height):
             db_ref[j * n_basis : (j + 1) * n_basis, :] = dbasis[
                 0:n_basis, j * LANES : (j + 1) * LANES
             ]
-        ux, uy, uz, dist, inv, q = [geo_ref[i, k] for i in range(6)]
+        ux, uy, uz, dist, inv, q = [plane(i, k, s, n) for i in range(6)]
         envelope = q * q
         g = envelope * inv
         denvelope = -(q * envelope) * dist
         dg = (denvelope - g) * inv
         sins, coss = waves(0.5 * dist, n_basis)
-        denv_direct = live_ref[k] + dy_ref[0] / envelope
-        ddist = denv_direct * denvelope
-        for n in range(n_basis):
-            db = db_ref[pl.ds(n, per, stride=n_basis), :]
-            ddist = ddist + db * (coss[n] * ((n + 1) * math.pi / 2.0) * g + sins[n] * dg)
-        y = [dy_ref[m] for m in range(9)]
+        live = tile_of(lambda rows: live_ref[k, rows, :], s, n)
+        y = [dy_ref[m, 0:height, :] for m in range(9)]
+        ddist = (live + y[0] / envelope) * denvelope
+        for i in range(n_basis):
+            db = db_ref[pl.ds(i, height, stride=n_basis), :]
+            ddist = ddist + db * (coss[i] * ((i + 1) * math.pi / 2.0) * g + sins[i] * dg)
         gx = y[1] + ROOT3 * (uy * y[4] + uz * y[6]) + (2.0 * 0.866) * ux * y[7]
         gy = y[2] + ROOT3 * (ux * y[4] + uz * y[5]) - (2.0 * 0.866) * uy * y[7]
         gz = y[3] + ROOT3 * (uy * y[5] + ux * y[6]) + 3.0 * uz * y[8]
         along = ddist - inv * (gx * ux + gy * uy + gz * uz)
         for i, (gu, u) in enumerate(((gx, ux), (gy, uy), (gz, uz))):
             hi, lo = split(inv * gu + along * u)
-            dr_ref[pl.ds(i, per, stride=16), :] = hi
-            dr_ref[pl.ds(3 + i, per, stride=16), :] = lo
-        dr = jnp.concatenate([dr_ref[j * 16 : (j + 1) * 16, :] for j in range(per)], axis=1)
-        kt = key_ref[k]
-        crow = in_lanes(kt >> OTHER_BITS)
-        orow = in_lanes(kt & OTHER_MASK)
-        hots = [one_hot(crow, 0, own)]
-        for base in range(0, n_tab, LANES):
-            hots.append(one_hot(orow, base, min(LANES, n_tab - base)))
-        sums = dot_nt(
-            jnp.concatenate(hots, axis=0),
-            jnp.concatenate([dmixed, dr.astype(BF16)], axis=0),
-        )
+            dr_ref[pl.ds(i, height, stride=16), :] = hi
+            dr_ref[pl.ds(3 + i, height, stride=16), :] = lo
+        dr = jnp.concatenate([dr_ref[j * 16 : (j + 1) * 16, :] for j in range(height)], axis=1)
+        moved = jnp.concatenate([dmixed, dr.astype(BF16)], axis=0)
+        sums = dot_nt(jnp.concatenate(table_hots(k, s, n), axis=0), moved)
         acc_ref[:, 0:chans] += sums[:, 0:chans]
         acc_ref[:, chans : chans + 16] += sums[:, chans:]
-        return carry
-
-    lax.fori_loop(0, n_chunks, phase_c, 0)
-
-    own_ref[...] = acc_ref[0 : 2 * own, :]
+
+        def body(s, j, start, fresh):
+            hot = a_ref[k * subs + s, 0:WIN, :] if fresh else window_hot(k, s, start).astype(BF16)
+            mine = dot_nt(hot, moved[:, part(j)])
+            cacc_ref[pl.ds(start, WIN), 0:chans] += mine[:, 0:chans]
+            cacc_ref[pl.ds(start, WIN), chans : chans + 16] += mine[:, chans:]
+
+        each_window(k, s, n, slow, body)
+
+    for phase in (phase_a, phase_b, phase_c):
+
+        @pl.when(most == 0)
+        def _(phase=phase):
+            def chunk(k, carry):
+                phase(k, 0, subs, False)
+                return carry
+
+            lax.fori_loop(0, n_chunks, chunk, 0)
+
+        @pl.when(most != 0)
+        def _(phase=phase):
+            def sub(i, carry):
+                phase(lax.div(i, subs), lax.rem(i, subs), 1, True)
+                return carry
+
+            lax.fori_loop(0, n_chunks * subs, sub, 0)
+
+    own_ref[0:own, :] = cacc_ref[0:own, :]
+    own_ref[own:, :] = acc_ref[0:own, :]
     row = lax.broadcasted_iota(jnp.int32, (LANES, LANES), 0)
     group = lax.broadcasted_iota(jnp.int32, (LANES, LANES), 1) // GROUP
     both = ((group < 3) & ((row == group) | (row == group + 3))).astype(F32)
-    places = dot_nn(acc_ref[2 * own :, LANES:], both, HIGH)
+    places = dot_nn(acc_ref[own:, LANES:], both, HIGH)
     found = {}
-    at = 2 * own
+    at = own
     for off in OFFSETS:
         found[off] = at
         at += plan.live(off)
@@ -747,7 +787,7 @@
             live = plan.live(off)
             at = found[off]
             ref[row : row + live, :] = acc_ref[at : at + live, 0:chans]
-            block = places[at - 2 * own : at - 2 * own + live, :]
+            block = places[at - own : at - own + live, :]
             ref[row + live : row + live + 1, :] = jnp.sum(diagonal(block), axis=0, keepdims=True)
 
 
@@ -852,11 +892,10 @@
         came[2] = plan.send(2, sends)
 
     with jax.named_scope("group_edges"):
-        dead = (own - 1) * (OTHER_MASK + 1) + OTHER_MASK
         pad = [(0, edges_up - edges)]
         regs = max(sorted_size(edges_up) // (8 * LANES), 1)
         key, bounds = pl.pallas_call(
-            lambda *refs: sort_kernel(dead, *refs),
+            lambda *refs: sort_kernel(own, *refs),
             out_shape=[
                 shape(n_chunks, CHUNK // LANES, LANES, dtype=jnp.int32),
                 shape(2, LANES, dtype=jnp.int32),
@@ -922,21 +961,21 @@
         pltpu.VMEM(planes, BF16),
         pltpu.VMEM(planes, BF16),
         pltpu.VMEM((n_chunks, CHUNK // LANES, LANES), F32),
-        pltpu.VMEM((1, CHUNK), F32),
         pltpu.VMEM((9, CHUNK // LANES, LANES), F32),
         pltpu.VMEM((CHUNK // LANES * n_basis, LANES), F32),
         pltpu.VMEM((CHUNK // LANES * 16, LANES), F32),
-        pltpu.VMEM((n_sel, 2 * LANES), F32),
+        pltpu.VMEM((n_sel - own, 2 * LANES), F32),
+        pltpu.VMEM((own + WIN, 2 * LANES), F32),
     ]
     with jax.named_scope("layer"):
-        given = [edge_count, bounds, key, positions, w_proj_b]
+        given = [bounds, key, positions, w_proj_b]
         given += [*came[0], *came[1], *came[2], half, *weights]
         atom_sums, own_sums, *back, held = pl.pallas_call(
             lambda *refs: main_kernel(plan, *refs),
             out_shape=[shape(own + WIN, LANES), shape(2 * own, 2 * LANES)]
             + plan.shapes(0, chans)
             + [shape(plan.total(plan.held_rest), chans)],
-            in_specs=[SMEM, SMEM] + [VMEM] * (len(given) - 2),
+            in_specs=[SMEM] + [VMEM] * (len(given) - 1),
             out_specs=[VMEM] * (3 + len(plan.groups[0])),
             scratch_shapes=scratch,
             compiler_params=PARAMS,

time: 62 us -> 55.8 us (0.90)
  waiting for transfers between devices: 22.3 us -> 15 us
  starting transfers between devices: 13.4 us -> 14.1 us
    ppermute x10, waiting for transfers between devices: 22.3 us -> 15 us  [send(): lax.ppermute(message, AXES[a], [(i, (i + step) % n) for i in range(n)])]
    ppermute x10, starting transfers between devices: 13.4 us -> 14.1 us  [send(): lax.ppermute(message, AXES[a], [(i, (i + step) % n) for i in range(n)])]
  transfers between devices with their start and end apart: 10 -> 10, of which waited for: 8 -> 7; matrix products, arithmetic and copies ran while one was open for 0% -> 0% of each run, Pallas kernels for 6% -> 7%
where the time goes in v2:
time: 55.8 us; the launch traced here: 55.5 us
  Pallas kernels  21.3 us (38%)
  waiting for transfers between devices  15 us (27%)
  starting transfers between devices  14.1 us (25%)
  other arithmetic  2.26 us (4%)
  between operations  1.49 us (3%)
  local copies, waits for them, and re-layouts  1.35 us (2%)
    pallas_call x1, Pallas kernels, local(): pl.pallas_call(lambda *refs: main_kernel(plan, *refs), out_shape=[shape(o...  15.7 us
    ppermute x10, waiting for transfers between devices, send(): lax.ppermute(message, AXES[a], [(i, (i + step) % n) for i in range(n)])  15 us
    ppermute x10, starting transfers between devices, send(): lax.ppermute(message, AXES[a], [(i, (i + step) % n) for i in range(n)])  14.1 us
    pallas_call x1, Pallas kernels, local(): pl.pallas_call(lambda *refs: sort_kernel(own, *refs), out_shape=[shape(n_...  2.52 us
    convert_element_type x3, other arithmetic, stack(): part = jnp.pad(x.astype(dtype), ((at, below), (0, LANES - x.shape[1])))  1.38 us
    unnamed x24, local copies, waits for them, and re-layouts  1.35 us
    pallas_call x1, Pallas kernels, local(): pl.pallas_call(lambda *refs: last_kernel(plan, *refs), out_shape=[shape(3...  1.23 us
  transfers between devices with their start and end apart: 10, of which 7 were waited for; matrix products, arithmetic and copies ran while one was open for 0% of the time, Pallas kernels for 7%

profile of v2, /device:TPU:0, one launch (start us, length us, event | category | flops | bytes accessed | tf_op | source)
XLA Modules:
  0.0 55.5 jit_solution(2722149028332405758)
XLA Ops:
  0.6 0.7 %convert_bitcast_fusion.1 = f32[2,8]{1,0:T(2,128)S(1)} fusion(s32[1,8,2]{1,2,0:T(2,128)} %param.20), kind=kLoop, calls=%fused_computation.6 | loop fusion | flops 16 | bytes 128 | tf_op jit(solution)/shard_map/prep/convert_element_type | solution.py:834
  1.3 0.7 %fusion = f32[6,32]{1,0:T(8,128)S(1)} fusion(s32[1,6,32]{2,0,1:T(1,128)} %param.18), kind=kLoop, calls=%fused_computation.4 | loop fusion | flops 192 | bytes 1536 | tf_op jit(solution)/shard_map/prep/convert_element_type | solution.py:834
  2.0 0.0 copy-done.10
  2.0 0.0 copy-start.4
  2.0 0.7 %copy-done.4 = f32[3,128]{1,0:T(4,128)S(1)} copy-done((f32[3,128]{1,0:T(4,128)S(1)}, f32[3,128]{1,0:T(4,128)}, u32[]{:S(2)}) %copy-start.4) | copy-done | bytes 1560
  2.7 0.9 %pad_add_fusion.2.refs_0_.rows_ref = f32[160,128]{1,0:T(8,128)S(1)} fusion(f32[2,8]{1,0:T(2,128)S(1)} %convert_bitcast_fusion.1, f32[8,12]{1,0:T(8,128)S(1)} %convert_bitcast_fusion, f32[6,32]{1,0:T(8,128)S(1)} %fusion, f32[3,128]{1,0:T(4,128)S(1)} %copy-done.4, f32[128,128]{1,0:T(8,128)} %param.17), kind=kLoop, calls=%fused_computation.2 | loop fusion | flops 81920 | bytes 150208 | tf_op jit(solution)/shard_map/prep/add | solution.py:835
  3.6 0.0 copy-start.1
  3.6 0.7 %prep.1 = (f32[162,128]{1,0:T(8,128)S(1)}, f32[168,128]{1,0:T(8,128)S(1)}, f32[330,128]{1,0:T(8,128)S(1)}) custom-call(f32[160,128]{1,0:T(8,128)S(1)} %pad_add_fusion.2.refs_0_.rows_ref), custom_call_target="tpu_custom_call" | custom-call | tf_op jit(solution)/shard_map/prep/pallas_call | solution.py:880
  4.3 3.0 %collective-permute-start = (f32[162,128]{1,0:T(8,128)S(1)}, f32[162,128]{1,0:T(8,128)S(1)}, u32[]{:S(2)}, u32[]{:S(2)}) collective-permute-start(f32[162,128]{1,0:T(8,128)S(1)} %get-tuple-element.51), channel_id=1, source_target_pairs={{0,1},{1,0},{2,3},{3,2},{4,5},{5,4},{6,7},{7,6},{8,9},{9,8},{10,11... | collective-permute-start | bytes 248840 | tf_op jit(solution)/shard_map/halo_z/ppermute | solution.py:128
  7.9 0.0 copy-done.2
  7.9 0.0 copy-done.3
  7.9 0.0 copy-start.9
  7.9 2.5 %group_edges.1 = (s32[2,24,128]{2,1,0:T(8,128)S(1)}, s32[2,128]{1,0:T(2,128)S(1)}) custom-call(s32[1]{0:T(128)S(6)} %copy.23.refs_0_, s32[48,128]{1,0:T(8,128)S(1)} %bitcast.14, s32[48,128]{1,0:T(8,128)S(1)} %bitcast.15), custom_call_target="tpu_custom_call" | custom-call | tf_op jit(solution)/shard_map/group_edges/pallas_call | solution.py:897
  10.5 0.0 copy-done
  10.5 0.0 copy-done.1
  10.5 0.0 copy-done.9
  10.5 0.0 collective-permute-done.refs_1_.refs_3_.refs_8_
  10.5 0.0 copy-start.5
  10.5 0.0 copy-start.6
  10.5 0.0 copy-start.7
  10.6 0.0 copy-start.8
  10.6 3.7 %collective-permute-start.1 = (f32[81,128]{1,0:T(8,128)S(1)}, f32[81,128]{1,0:T(8,128)S(1)}, u32[]{:S(2)}, u32[]{:S(2)}) collective-permute-start(f32[81,128]{1,0:T(8,128)S(1)} %get-tuple-element.58), channel_id=1, source_target_pairs={{0,6},{2,0},{4,2},{6,4},{1,7},{3,1},{5,3},{7,5},{8,14},{10,8},{12,... | collective-permute-start | bytes 124424 | tf_op jit(solution)/shard_map/halo_y/ppermute | solution.py:128
  14.2 0.0 collective-permute-start.2
  14.2 0.0 copy-done.5
  14.3 0.0 copy-done.6
  14.3 0.0 copy-done.7
  14.3 0.0 copy-done.8
  14.3 0.6 %copy-done.11 = bf16[128]{0:T(256)(128)(2,1)S(1)} copy-done((bf16[128]{0:T(256)(128)(2,1)S(1)}, bf16[128]{0:T(256)(128)(2,1)}, u32[]{:S(2)}) %copy-start.11) | copy-done | bytes 280
  14.9 0.3 weights.1
  15.2 0.7 %collective-permute-done.1.refs_1_.refs_6_ = f32[81,128]{1,0:T(8,128)S(1)} collective-permute-done((f32[81,128]{1,0:T(8,128)S(1)}, f32[81,128]{1,0:T(8,128)S(1)}, u32[]{:S(2)}, u32[]{:S(2)}) %collective-permute-start.1) | collective-permute-done | bytes 41504 | tf_op jit(solution)/shard_map/halo_y/ppermute | solution.py:128
  16.0 4.1 %collective-permute-done.2.refs_2_.refs_7_ = f32[81,128]{1,0:T(8,128)S(1)} collective-permute-done((f32[81,128]{1,0:T(8,128)S(1)}, f32[81,128]{1,0:T(8,128)S(1)}, u32[]{:S(2)}, u32[]{:S(2)}) %collective-permute-start.2) | collective-permute-done | bytes 41504 | tf_op jit(solution)/shard_map/halo_y/ppermute | solution.py:128
  20.1 0.1 collective-permute-start.3
  20.2 0.5 collective-permute-start.4
  20.7 1.2 %collective-permute-done.3.refs_4_ = f32[81,128]{1,0:T(8,128)S(1)} collective-permute-done((f32[81,128]{1,0:T(8,128)S(1)}, f32[81,128]{1,0:T(8,128)S(1)}, u32[]{:S(2)}, u32[]{:S(2)}) %collective-permute-start.3) | collective-permute-done | bytes 41504 | tf_op jit(solution)/shard_map/halo_x/ppermute | solution.py:128
  21.9 2.3 %collective-permute-done.4.refs_5_ = f32[81,128]{1,0:T(8,128)S(1)} collective-permute-done((f32[81,128]{1,0:T(8,128)S(1)}, f32[81,128]{1,0:T(8,128)S(1)}, u32[]{:S(2)}, u32[]{:S(2)}) %collective-permute-start.4) | collective-permute-done | bytes 41504 | tf_op jit(solution)/shard_map/halo_x/ppermute | solution.py:128
  24.2 15.7 %layer.1 = (f32[144,128]{1,0:T(8,128)S(1)}, f32[256,256]{1,0:T(8,128)S(1)}, f32[81,128]{1,0:T(8,128)S(1)}, f32[81,128]{1,0:T(8,128)S(1)}, f32[168,128]{1,0:T(8,128)S(1)}) custom-call(s32[2,128]{1,0:T(2,128)S(1)} %get-tuple-element.54.refs_0_, s32[2,24,128]{2,1,0:T(8,128)S(1)} %get-tuple-element.55.refs_1_, f32[3,128]{1,0:T(4,128)S(1)} %copy-done.4, ...), custom_call_target="tpu_custom_call" | custom-call | tf_op jit(solution)/shard_map/layer/pallas_call | solution.py:973
  39.9 0.1 collective-permute-start.5
  39.9 1.7 %collective-permute-start.6 = (f32[81,128]{1,0:T(8,128)S(1)}, f32[81,128]{1,0:T(8,128)S(1)}, u32[]{:S(2)}, u32[]{:S(2)}) collective-permute-start(f32[81,128]{1,0:T(8,128)S(1)} %get-tuple-element.90), channel_id=1, source_target_pairs={{0,24},{8,0},{16,8},{24,16},{1,25},{9,1},{17,9},{25,17},{2,26},{10... | collective-permute-start | bytes 124424 | tf_op jit(solution)/shard_map/halo_back/ppermute | solution.py:128
  41.7 1.7 %collective-permute-done.5.refs_1_.refs_3_.refs_4_ = f32[81,128]{1,0:T(8,128)S(1)} collective-permute-done((f32[81,128]{1,0:T(8,128)S(1)}, f32[81,128]{1,0:T(8,128)S(1)}, u32[]{:S(2)}, u32[]{:S(2)}) %collective-permute-start.5) | collective-permute-done | bytes 41504 | tf_op jit(solution)/shard_map/halo_back/ppermute | solution.py:128
  43.4 0.0 collective-permute-done.6.refs_2_.refs_4_.refs_5_
  43.4 0.1 collective-permute-start.7
  43.5 3.8 %collective-permute-start.8 = (f32[81,128]{1,0:T(8,128)S(1)}, f32[81,128]{1,0:T(8,128)S(1)}, u32[]{:S(2)}, u32[]{:S(2)}) collective-permute-start(f32[81,128]{1,0:T(8,128)S(1)} %get-tuple-element.93), channel_id=1, source_target_pairs={{0,6},{2,0},{4,2},{6,4},{1,7},{3,1},{5,3},{7,5},{8,14},{10,8},{12,... | collective-permute-start | bytes 124424 | tf_op jit(solution)/shard_map/halo_back/ppermute | solution.py:128
  47.3 2.3 %collective-permute-done.7.refs_1_.refs_6_ = f32[81,128]{1,0:T(8,128)S(1)} collective-permute-done((f32[81,128]{1,0:T(8,128)S(1)}, f32[81,128]{1,0:T(8,128)S(1)}, u32[]{:S(2)}, u32[]{:S(2)}) %collective-permute-start.7) | collective-permute-done | bytes 41504 | tf_op jit(solution)/shard_map/halo_back/ppermute | solution.py:128
  49.6 0.0 collective-permute-done.8.refs_2_.refs_7_
  49.6 1.2 %collective-permute-start.9 = (f32[162,128]{1,0:T(8,128)S(1)}, f32[162,128]{1,0:T(8,128)S(1)}, u32[]{:S(2)}, u32[]{:S(2)}) collective-permute-start(f32[162,128]{1,0:T(8,128)S(1)} %halo_back.3), channel_id=1, source_target_pairs={{0,1},{1,0},{2,3},{3,2},{4,5},{5,4},{6,7},{7,6},{8,9},{9,8},{10,11... | collective-permute-start | bytes 248840 | tf_op jit(solution)/shard_map/halo_back/ppermute | solution.py:128
  50.9 0.8 %own_part.1 = (f32[1,128]{1,0:T(1,128)}, f32[128,128]{1,0:T(8,128)S(1)}, f32[3,128]{1,0:T(4,128)S(1)}) custom-call(f32[144,128]{1,0:T(8,128)S(1)} %get-tuple-element.85.ae_ref, f32[256,256]{1,0:T(8,128)S(1)} %get-tuple-element.86.own_ref, f32[128,128]{1,0:T(8,128)S(1)} %copy-done.1, f32[128,128]{1,0:T(8,128)S(1)} %copy-done), custom_call_target="tpu_custom_call" | custom-call | tf_op jit(solution)/shard_map/own_part/pallas_call | solution.py:990
  51.7 2.6 %collective-permute-done.9.refs_8_ = f32[162,128]{1,0:T(8,128)S(1)} collective-permute-done((f32[162,128]{1,0:T(8,128)S(1)}, f32[162,128]{1,0:T(8,128)S(1)}, u32[]{:S(2)}, u32[]{:S(2)}) %collective-permute-start.9) | collective-permute-done | bytes 82976 | tf_op jit(solution)/shard_map/halo_back/ppermute | solution.py:128
  54.3 1.2 %owner_sums.1 = (f32[3,128]{1,0:T(4,128)}, f32[128,128]{1,0:T(8,128)}) custom-call(f32[330,128]{1,0:T(8,128)S(1)} %get-tuple-element.50.refs_0_, f32[128,128]{1,0:T(8,128)S(1)} %get-tuple-element.87.refs_1_, f32[3,128]{1,0:T(4,128)S(1)} %get-tuple-element.88.refs_2_, f32[128,128]{1,0:T(8,128)S(1)} %copy-done, ...), custom_call_target="tpu_custom_call" | custom-call | tf_op jit(solution)/shard_map/owner_sums/pallas_call | solution.py:1000
  (12 shorter events, 0.1 us)
Async XLA Ops:
  1.3 0.7 %copy-start.10 = (s32[1,12,8]{1,2,0:T(8,128)S(1)}, s32[1,12,8]{1,2,0:T(8,128)}, u32[]{:S(2)}) copy-start(s32[1,12,8]{1,2,0:T(8,128)} %param.19) | copy-start | bytes 1156
  2.0 0.7 %copy-start.4 = (f32[3,128]{1,0:T(4,128)S(1)}, f32[3,128]{1,0:T(4,128)}, u32[]{:S(2)}) copy-start(f32[3,128]{1,0:T(4,128)} %refs_2_.1) | copy-start | bytes 4612
  2.7 5.2 %copy-start.2 = (s32[6144]{0:T(1024)S(1)}, s32[6144]{0:T(1024)}, u32[]{:S(2)}) copy-start(s32[6144]{0:T(1024)} %param.21) | copy-start | bytes 73732
  2.7 5.2 %copy-start.3 = (s32[6144]{0:T(1024)S(1)}, s32[6144]{0:T(1024)}, u32[]{:S(2)}) copy-start(s32[6144]{0:T(1024)} %param.22) | copy-start | bytes 73732
  3.6 6.9 %copy-start = (f32[128,128]{1,0:T(8,128)S(1)}, f32[128,128]{1,0:T(8,128)}, u32[]{:S(2)}) copy-start(f32[128,128]{1,0:T(8,128)} %refs_3_.3) | copy-start | bytes 196612
  3.6 6.9 %copy-start.1 = (f32[128,128]{1,0:T(8,128)S(1)}, f32[128,128]{1,0:T(8,128)}, u32[]{:S(2)}) copy-start(f32[128,128]{1,0:T(8,128)} %wa_ref.1) | copy-start | bytes 196612
  4.3 6.3 %collective-permute-start = (f32[162,128]{1,0:T(8,128)S(1)}, f32[162,128]{1,0:T(8,128)S(1)}, u32[]{:S(2)}, u32[]{:S(2)}) collective-permute-start(f32[162,128]{1,0:T(8,128)S(1)} %get-tuple-element.51), channel_id=1, source_target_pairs={{0,1},{1,0},{2,3},{3,2},{4,5},{5,4},{6,7},{7,6},{8,9},{9,8},{10,11... | collective-permute-start | bytes 248840 | tf_op jit(solution)/shard_map/halo_z/ppermute | solution.py:128
  7.9 2.6 %copy-start.9 = (f32[8,128]{1,0:T(8,128)S(1)}, f32[8,128]{1,0:T(8,128)}, u32[]{:S(2)}) copy-start(f32[8,128]{1,0:T(8,128)} %param.26) | copy-start | bytes 12292
  10.5 3.7 %copy-start.5 = (bf16[256,128]{1,0:T(8,128)(2,1)S(1)}, bf16[256,128]{1,0:T(8,128)(2,1)}, u32[]{:S(2)}) copy-start(bf16[256,128]{1,0:T(8,128)(2,1)} %param.30) | copy-start | bytes 196612
  10.5 3.7 %copy-start.6 = (bf16[128,128]{1,0:T(8,128)(2,1)S(1)}, bf16[128,128]{1,0:T(8,128)(2,1)}, u32[]{:S(2)}) copy-start(bf16[128,128]{1,0:T(8,128)(2,1)} %param.29) | copy-start | bytes 98308
  10.5 3.7 %copy-start.7 = (bf16[128,128]{1,0:T(8,128)(2,1)S(1)}, bf16[128,128]{1,0:T(8,128)(2,1)}, u32[]{:S(2)}) copy-start(bf16[128,128]{1,0:T(8,128)(2,1)} %param.28) | copy-start | bytes 98308
  10.6 3.7 %copy-start.8 = (bf16[128,128]{1,0:T(8,128)(2,1)S(1)}, bf16[128,128]{1,0:T(8,128)(2,1)}, u32[]{:S(2)}) copy-start(bf16[128,128]{1,0:T(8,128)(2,1)} %param.27) | copy-start | bytes 98308
  10.6 5.4 %collective-permute-start.1 = (f32[81,128]{1,0:T(8,128)S(1)}, f32[81,128]{1,0:T(8,128)S(1)}, u32[]{:S(2)}, u32[]{:S(2)}) collective-permute-start(f32[81,128]{1,0:T(8,128)S(1)} %get-tuple-element.58), channel_id=1, source_target_pairs={{0,6},{2,0},{4,2},{6,4},{1,7},{3,1},{5,3},{7,5},{8,14},{10,8},{12,... | collective-permute-start | bytes 124424 | tf_op jit(solution)/shard_map/halo_y/ppermute | solution.py:128
  14.2 0.7 %copy-start.11 = (bf16[128]{0:T(256)(128)(2,1)S(1)}, bf16[128]{0:T(256)(128)(2,1)}, u32[]{:S(2)}) copy-start(bf16[128]{0:T(256)(128)(2,1)} %param.31) | copy-start | bytes 772
  14.2 5.8 %collective-permute-start.2 = (f32[81,128]{1,0:T(8,128)S(1)}, f32[81,128]{1,0:T(8,128)S(1)}, u32[]{:S(2)}, u32[]{:S(2)}) collective-permute-start(f32[81,128]{1,0:T(8,128)S(1)} %get-tuple-element.59), channel_id=1, source_target_pairs={{0,2},{2,4},{4,6},{6,0},{1,3},{3,5},{5,7},{7,1},{8,10},{10,12},{12... | collective-permute-start | bytes 124424 | tf_op jit(solution)/shard_map/halo_y/ppermute | solution.py:128
  20.1 1.8 %collective-permute-start.3 = (f32[81,128]{1,0:T(8,128)S(1)}, f32[81,128]{1,0:T(8,128)S(1)}, u32[]{:S(2)}, u32[]{:S(2)}) collective-permute-start(f32[81,128]{1,0:T(8,128)S(1)} %get-tuple-element.75), channel_id=1, source_target_pairs={{0,24},{8,0},{16,8},{24,16},{1,25},{9,1},{17,9},{25,17},{2,26},{10... | collective-permute-start | bytes 124424 | tf_op jit(solution)/shard_map/halo_x/ppermute | solution.py:128
  20.2 4.0 %collective-permute-start.4 = (f32[81,128]{1,0:T(8,128)S(1)}, f32[81,128]{1,0:T(8,128)S(1)}, u32[]{:S(2)}, u32[]{:S(2)}) collective-permute-start(f32[81,128]{1,0:T(8,128)S(1)} %get-tuple-element.76), channel_id=1, source_target_pairs={{0,8},{8,16},{16,24},{24,0},{1,9},{9,17},{17,25},{25,1},{2,10},{10... | collective-permute-start | bytes 124424 | tf_op jit(solution)/shard_map/halo_x/ppermute | solution.py:128
  39.9 3.5 %collective-permute-start.5 = (f32[81,128]{1,0:T(8,128)S(1)}, f32[81,128]{1,0:T(8,128)S(1)}, u32[]{:S(2)}, u32[]{:S(2)}) collective-permute-start(f32[81,128]{1,0:T(8,128)S(1)} %get-tuple-element.89), channel_id=1, source_target_pairs={{0,8},{8,16},{16,24},{24,0},{1,9},{9,17},{17,25},{25,1},{2,10},{10... | collective-permute-start | bytes 124424 | tf_op jit(solution)/shard_map/halo_back/ppermute | solution.py:128
  39.9 3.5 %collective-permute-start.6 = (f32[81,128]{1,0:T(8,128)S(1)}, f32[81,128]{1,0:T(8,128)S(1)}, u32[]{:S(2)}, u32[]{:S(2)}) collective-permute-start(f32[81,128]{1,0:T(8,128)S(1)} %get-tuple-element.90), channel_id=1, source_target_pairs={{0,24},{8,0},{16,8},{24,16},{1,25},{9,1},{17,9},{25,17},{2,26},{10... | collective-permute-start | bytes 124424 | tf_op jit(solution)/shard_map/halo_back/ppermute | solution.py:128
  43.4 6.2 %collective-permute-start.7 = (f32[81,128]{1,0:T(8,128)S(1)}, f32[81,128]{1,0:T(8,128)S(1)}, u32[]{:S(2)}, u32[]{:S(2)}) collective-permute-start(f32[81,128]{1,0:T(8,128)S(1)} %get-tuple-element.92), channel_id=1, source_target_pairs={{0,2},{2,4},{4,6},{6,0},{1,3},{3,5},{5,7},{7,1},{8,10},{10,12},{12... | collective-permute-start | bytes 124424 | tf_op jit(solution)/shard_map/halo_back/ppermute | solution.py:128
  43.5 6.1 %collective-permute-start.8 = (f32[81,128]{1,0:T(8,128)S(1)}, f32[81,128]{1,0:T(8,128)S(1)}, u32[]{:S(2)}, u32[]{:S(2)}) collective-permute-start(f32[81,128]{1,0:T(8,128)S(1)} %get-tuple-element.93), channel_id=1, source_target_pairs={{0,6},{2,0},{4,2},{6,4},{1,7},{3,1},{5,3},{7,5},{8,14},{10,8},{12,... | collective-permute-start | bytes 124424 | tf_op jit(solution)/shard_map/halo_back/ppermute | solution.py:128
  49.6 4.7 %collective-permute-start.9 = (f32[162,128]{1,0:T(8,128)S(1)}, f32[162,128]{1,0:T(8,128)S(1)}, u32[]{:S(2)}, u32[]{:S(2)}) collective-permute-start(f32[162,128]{1,0:T(8,128)S(1)} %halo_back.3), channel_id=1, source_target_pairs={{0,1},{1,0},{2,3},{3,2},{4,5},{5,4},{6,7},{7,6},{8,9},{9,8},{10,11... | collective-permute-start | bytes 248840 | tf_op jit(solution)/shard_map/halo_back/ppermute | solution.py:128

commit v3 on v2

--- a/solution.py
+++ b/solution.py
@@ -11,7 +11,7 @@
 BF16 = jnp.bfloat16
 HIGH = lax.Precision.HIGHEST
 AXES = ("gx", "gy", "gz")
-CHUNK = 3072
+CHUNK = 512
 SUB = 256
 WIN = 16
 OTHER_BITS = 9
@@ -228,7 +228,7 @@
     group = regs * 8
     row = lax.broadcasted_iota(jnp.int32, (rows, LANES), 0)
     lane = lax.broadcasted_iota(jnp.int32, (rows, LANES), 1)
-    live = row * LANES + lane < count_ref[0]
+    live = row * LANES + lane < count_ref[...]
     centre = centre_ref[...]
     key = jnp.where(live, (centre << OTHER_BITS) + other_ref[...], dead).astype(F32)
     x = [key[8 * v : 8 * v + 8, :] for v in range(rows // 8)]
@@ -305,8 +305,9 @@
     ]
     done = jnp.concatenate(parts, axis=1).astype(jnp.int32)
     per = key_ref.shape[1]
-    for c in range(key_ref.shape[0]):
+    for c in range(key_ref.shape[0] - 1):
         key_ref[c] = done[c * per : (c + 1) * per, :]
+    key_ref[key_ref.shape[0] - 1] = jnp.full((per, LANES), dead, jnp.int32)
 
 
 def weight_kernel(
@@ -441,9 +442,16 @@
         env_ref,
         denv_ref,
         big_ref,
+        mix_ref,
+        scal_ref,
+        dz2_ref,
+        dpre_ref,
+        dz1_ref,
         dt_ref,
         dv_ref,
         dfa_ref,
+        tot_ref,
+        dmix_ref,
         live_ref,
         dy_ref,
         db_ref,
@@ -512,10 +520,10 @@
     cacc_ref[...] = jnp.zeros_like(cacc_ref)
     dr_ref[...] = jnp.zeros_like(dr_ref)
 
-    groups = bound_ref.shape[1] * SUB // sorted_size(rows_all * LANES)
+    groups = bound_ref.shape[1] * SUB // sorted_size((rows_all - per) * LANES)
 
     def window(k, s):
-        first = (k * subs + s) * groups
+        first = jnp.minimum((k * subs + s) * groups, bound_ref.shape[1] - groups)
         low = bound_ref[0, first]
         high = low
         for g in range(groups):
@@ -526,7 +534,7 @@
 
     most = jnp.int32(0)
     n_chunks = jnp.int32(0)
-    for s in range(rows_all // sub_rows):
+    for s in range((rows_all - per) // sub_rows):
         most = jnp.maximum(most, window(s // subs, s % subs)[1])
         for g in range(groups):
             any_live = bound_ref[1, s * groups + g] >= 0
@@ -550,6 +558,11 @@
 
     def keys_of(k, s, n):
         return tile_of(lambda rows: key_ref[k, rows, :], s, n)
+
+    def put_row(ref, index, s, row):
+        for j in range(row.shape[1] // LANES):
+            at = pl.ds(s * sub_rows + j, 1)
+            ref[index + (at, slice(None))] = row[:, j * LANES : (j + 1) * LANES]
 
     def stacked(ref, k, s, n, height):
         first = (k * subs + s) * sub_rows
@@ -592,6 +605,19 @@
 
                 lax.fori_loop(1, more + 1, step, 0)
 
+    def sum_windows(k, s, n, slow, value):
+        if not slow:
+            return jnp.concatenate([value(s + j, window(k, s + j)[0], True) for j in range(n)], axis=1)
+
+        def body(s, j, start, fresh):
+            if fresh:
+                big_ref[:, part(j)] = value(s, start, fresh)
+            else:
+                big_ref[:, part(j)] += value(s, start, fresh)
+
+        each_window(k, s, n, slow, body)
+        return big_ref[:, 0 : n * SUB]
+
     def kept(k, s, start, fresh):
         return a_ref[k * subs + s] if fresh else select(k, s, start)
 
@@ -602,69 +628,66 @@
     def part(j):
         return slice(j * SUB, (j + 1) * SUB)
 
-    def phase_a(k, s, n, slow):
-        lanes = lanes_of(s, n)
+    def width(n):
+        return slice(0, n * SUB)
+
+    def mix(k, s, n, slow):
         crow = in_lanes(keys_of(k, s, n) >> OTHER_BITS)
         hots = [one_hot(crow, 0, own)] + table_hots(k, s, n)
         basis = stacked(basis_ref, k, s, n, n_basis)
         b_hi, b_lo = split(basis)
         hots.append(jnp.concatenate([b_hi, b_lo], axis=0).astype(BF16))
         hots.append(jnp.concatenate([b_hi, jnp.zeros_like(b_hi)], axis=0).astype(BF16))
-        mixed = dot_nn(table_ref[...], jnp.concatenate(hots, axis=0)).astype(BF16)
-        z1 = dot_nn(w1t_ref[...], mixed)
+        mixed = dot_nn(table_ref[...], jnp.concatenate(hots, axis=0))
+        mix_ref[:, width(n)] = mixed.astype(BF16)
+
+    def first_layer(k, s, n, slow):
+        lanes = lanes_of(s, n)
+        z1 = dot_nn(w1t_ref[...], mix_ref[:, width(n)])
         sg = 0.5 + 0.5 * jnp.tanh(0.5 * z1)
         first = z1 * sg
         dsilu_ref[k, :, lanes] = (sg + first * (1.0 - sg)).astype(BF16)
-        first = first.astype(BF16)
-        first_ref[k, :, lanes] = first
-        both = dot_nn(wevt_ref[...], first)
-        ew = (both[0:chans] * in_lanes(plane(6, k, s, n))).astype(BF16)
-        ew_ref[k, :, lanes] = ew
+        first_ref[k, :, lanes] = first.astype(BF16)
+
+    def tracks(k, s, n, slow):
+        lanes = lanes_of(s, n)
+        both = dot_nn(wevt_ref[...], first_ref[k, :, lanes])
+        ew_ref[k, :, lanes] = (both[0:chans] * in_lanes(plane(6, k, s, n))).astype(BF16)
         val_ref[k, :, lanes] = both[chans:].astype(BF16)
 
+    def env_sums(k, s, n, slow):
         def body(s, j, start, fresh):
             a = select(k, s, start)
             if fresh:
                 a_ref[k * subs + s] = a
-            add_window(env_ref, start, dot_nt(a, ew[:, part(j)]))
+            add_window(env_ref, start, dot_nt(a, ew_ref[k, :, lanes_of(s, 1)]))
 
         each_window(k, s, n, slow, body)
 
-    def phase_b(k, s, n, slow):
+    def tensor(k, s, n, slow):
         lanes = lanes_of(s, n)
 
-        def totals(s, j, start, fresh):
-            value = dot_tn(load_window(env_ref, start), kept(k, s, start, fresh))
-            if fresh:
-                big_ref[:, part(j)] = value
-            else:
-                big_ref[:, part(j)] += value
-
-        each_window(k, s, n, slow, totals)
-        total = 0.2 * big_ref[:, 0 : n * SUB]
-        value = val_ref[k, :, lanes].astype(F32)
-        scalar = (value * total).astype(BF16)
-        z2 = dot_nn(w2t_ref[...], jnp.concatenate([first_ref[k, :, lanes], scalar], axis=0))
+        def value(s, start, fresh):
+            return dot_tn(load_window(env_ref, start), kept(k, s, start, fresh))
+
+        total = 0.2 * sum_windows(k, s, n, slow, value)
+        tot_ref[k, :, lanes] = total
+        scal_ref[:, width(n)] = (val_ref[k, :, lanes].astype(F32) * total).astype(BF16)
+
+    def second_layer(k, s, n, slow):
+        lanes = lanes_of(s, n)
+        joined = jnp.concatenate([first_ref[k, :, lanes], scal_ref[:, width(n)]], axis=0)
+        z2 = dot_nn(w2t_ref[...], joined)
         sg = 0.5 + 0.5 * jnp.tanh(0.5 * z2)
         second = z2 * sg
         wcol = jnp.concatenate([wcol_ref[...]] * (n * sub_rows), axis=1)
         ee = jnp.sum(second.astype(BF16).astype(F32) * wcol, axis=0, keepdims=True)
         envv = in_lanes(plane(6, k, s, n))
-        live = ee * in_lanes(plane(7, k, s, n))
-        first_row = s * sub_rows
-        for j in range(n * sub_rows):
-            live_ref[k, pl.ds(first_row + j, 1), :] = live[:, j * LANES : (j + 1) * LANES]
+        put_row(live_ref, (k,), s, ee * in_lanes(plane(7, k, s, n)))
         energy = ee * envv
-        dz2 = ((wcol * envv) * (sg + second * (1.0 - sg))).astype(BF16)
-        dj = dot_nn(w2_ref[...], dz2)
-        dfa_ref[k, :, lanes] = dj[0:chans].astype(BF16)
-        dscalar = dj[chans:]
-        dt = (0.2 * value * dscalar).astype(BF16)
-        dt_ref[k, :, lanes] = dt
-        dv_ref[k, :, lanes] = (total * dscalar).astype(BF16)
+        dz2_ref[:, width(n)] = ((wcol * envv) * (sg + second * (1.0 - sg))).astype(BF16)
 
         def body(s, j, start, fresh):
-            add_window(denv_ref, start, dot_nt(kept(k, s, start, fresh), dt[:, part(j)]))
             mine = jnp.where(window_hot(k, s, start), energy[:, part(j)], 0.0)
             half = mine[:, 0:LANES]
             for i in range(1, sub_rows):
@@ -673,50 +696,60 @@
 
         each_window(k, s, n, slow, body)
 
-    def phase_c(k, s, n, slow):
+    def second_back(k, s, n, slow):
         lanes = lanes_of(s, n)
-        height = n * sub_rows
-
-        def env_terms(s, j, start, fresh):
+        dj = dot_nn(w2_ref[...], dz2_ref[:, width(n)])
+        dfa_ref[k, :, lanes] = dj[0:chans].astype(BF16)
+        dscalar = dj[chans:]
+        dt_ref[k, :, lanes] = (0.2 * val_ref[k, :, lanes].astype(F32) * dscalar).astype(BF16)
+        dv_ref[k, :, lanes] = (tot_ref[k, :, lanes] * dscalar).astype(BF16)
+
+    def env_back(k, s, n, slow):
+        def body(s, j, start, fresh):
+            a = kept(k, s, start, fresh)
+            add_window(denv_ref, start, dot_nt(a, dt_ref[k, :, lanes_of(s, 1)]))
+
+        each_window(k, s, n, slow, body)
+
+    def track_back(k, s, n, slow):
+        lanes = lanes_of(s, n)
+
+        def value(s, start, fresh):
             a = kept(k, s, start, fresh)
             e_win = load_window(env_ref, start)
             d_win = load_window(denv_ref, start)
-            dew = dot_tn(d_win, a)
             here = lanes_of(s, 1)
             pair = jnp.concatenate([dt_ref[k, :, here], ew_ref[k, :, here]], axis=0)
             prods = dot_nn(jnp.concatenate([e_win, d_win], axis=1), pair)
             hot = a[0:WIN].astype(F32)
-            if fresh:
-                big_ref[:, part(j)] = dew
-            else:
-                big_ref[:, part(j)] += dew
             for m in range(1, 9):
                 row = jnp.sum(prods[m * WIN : (m + 1) * WIN] * hot, axis=0, keepdims=True)
-                for i in range(sub_rows):
-                    at = j * sub_rows + i
-                    piece = row[:, i * LANES : (i + 1) * LANES]
-                    if fresh:
-                        dy_ref[m, at : at + 1, :] = piece
-                    else:
-                        dy_ref[m, at : at + 1, :] += piece
-
-        each_window(k, s, n, slow, env_terms)
-        dew = big_ref[:, 0 : n * SUB]
-        dpre = (dew * in_lanes(plane(6, k, s, n))).astype(BF16)
+                if not fresh:
+                    row = row + in_lanes(tile_of(lambda rows: dy_ref[k, m, rows, :], s, 1))
+                put_row(dy_ref, (k, m), s, row)
+            return dot_tn(d_win, a)
+
+        dew = sum_windows(k, s, n, slow, value)
+        dpre_ref[:, width(n)] = (dew * in_lanes(plane(6, k, s, n))).astype(BF16)
         denv_row = jnp.sum(dew * ew_ref[k, :, lanes].astype(F32), axis=0, keepdims=True)
-        for j in range(height):
-            dy_ref[0, j : j + 1, :] = denv_row[:, j * LANES : (j + 1) * LANES]
-        dfirst = dfa_ref[k, :, lanes].astype(F32) + dot_nn(
-            wev_ref[...], jnp.concatenate([dpre, dv_ref[k, :, lanes]], axis=0)
-        )
-        dz1 = (dfirst * dsilu_ref[k, :, lanes].astype(F32)).astype(BF16)
-        dboth = dot_nn(w1_ref[...], dz1)
-        dmixed = dboth[0:chans].astype(BF16)
-        dbasis = dboth[chans:]
-        for j in range(height):
-            db_ref[j * n_basis : (j + 1) * n_basis, :] = dbasis[
-                0:n_basis, j * LANES : (j + 1) * LANES
+        put_row(dy_ref, (k, 0), s, denv_row)
+
+    def first_back(k, s, n, slow):
+        lanes = lanes_of(s, n)
+        joined = jnp.concatenate([dpre_ref[:, width(n)], dv_ref[k, :, lanes]], axis=0)
+        dfirst = dfa_ref[k, :, lanes].astype(F32) + dot_nn(wev_ref[...], joined)
+        dz1_ref[:, width(n)] = (dfirst * dsilu_ref[k, :, lanes].astype(F32)).astype(BF16)
+
+    def mix_back(k, s, n, slow):
+        dboth = dot_nn(w1_ref[...], dz1_ref[:, width(n)])
+        dmix_ref[k, :, lanes_of(s, n)] = dboth[0:chans].astype(BF16)
+        for j in range(n * sub_rows):
+            db_ref[j * n_basis : (j + 1) * n_basis, :] = dboth[
+                chans : chans + n_basis, j * LANES : (j + 1) * LANES
             ]
+
+    def geometry_back(k, s, n, slow):
+        height = n * sub_rows
         ux, uy, uz, dist, inv, q = [plane(i, k, s, n) for i in range(6)]
         envelope = q * q
         g = envelope * inv
@@ -724,7 +757,7 @@
         dg = (denvelope - g) * inv
         sins, coss = waves(0.5 * dist, n_basis)
         live = tile_of(lambda rows: live_ref[k, rows, :], s, n)
-        y = [dy_ref[m, 0:height, :] for m in range(9)]
+        y = [tile_of(lambda rows, m=m: dy_ref[k, m, rows, :], s, n) for m in range(9)]
         ddist = (live + y[0] / envelope) * denvelope
         for i in range(n_basis):
             db = db_ref[pl.ds(i, height, stride=n_basis), :]
@@ -737,8 +770,12 @@
             hi, lo = split(inv * gu + along * u)
             dr_ref[pl.ds(i, height, stride=16), :] = hi
             dr_ref[pl.ds(3 + i, height, stride=16), :] = lo
-        dr = jnp.concatenate([dr_ref[j * 16 : (j + 1) * 16, :] for j in range(height)], axis=1)
-        moved = jnp.concatenate([dmixed, dr.astype(BF16)], axis=0)
+
+    def scatter(k, s, n, slow):
+        dr = jnp.concatenate(
+            [dr_ref[j * 16 : (j + 1) * 16, :] for j in range(n * sub_rows)], axis=1
+        )
+        moved = jnp.concatenate([dmix_ref[k, :, lanes_of(s, n)], dr.astype(BF16)], axis=0)
         sums = dot_nt(jnp.concatenate(table_hots(k, s, n), axis=0), moved)
         acc_ref[:, 0:chans] += sums[:, 0:chans]
         acc_ref[:, chans : chans + 16] += sums[:, chans:]
@@ -751,20 +788,38 @@
 
         each_window(k, s, n, slow, body)
 
-    for phase in (phase_a, phase_b, phase_c):
+    phases = (
+        (mix, first_layer, tracks, env_sums),
+        (tensor, second_layer, second_back, env_back),
+        (track_back, first_back, mix_back, geometry_back, scatter),
+    )
+    dummy = key_ref.shape[0] - 1
+    for ref in (mix_ref, scal_ref, dz2_ref, dpre_ref, dz1_ref, db_ref, dr_ref):
+        ref[...] = jnp.zeros_like(ref)
+    for ref in (first_ref, dsilu_ref, ew_ref, val_ref, dt_ref, dv_ref, dfa_ref, tot_ref):
+        ref[dummy] = jnp.zeros(ref.shape[1:], ref.dtype)
+    for ref in (dmix_ref, live_ref, dy_ref):
+        ref[dummy] = jnp.zeros(ref.shape[1:], ref.dtype)
+    for s in range(subs):
+        a_ref[dummy * subs + s] = jnp.zeros(a_ref.shape[1:], BF16)
+    for stages in phases:
 
         @pl.when(most == 0)
-        def _(phase=phase):
-            def chunk(k, carry):
-                phase(k, 0, subs, False)
+        def _(stages=stages):
+            def step(i, carry):
+                for j in reversed(range(len(stages))):
+                    k = i - j
+                    k = jnp.where((k >= 0) & (k < n_chunks), k, dummy)
+                    stages[j](k, 0, subs, False)
                 return carry
 
-            lax.fori_loop(0, n_chunks, chunk, 0)
+            lax.fori_loop(0, n_chunks + (len(stages) - 1), step, 0)
 
         @pl.when(most != 0)
-        def _(phase=phase):
+        def _(stages=stages):
             def sub(i, carry):
-                phase(lax.div(i, subs), lax.rem(i, subs), 1, True)
+                for stage in stages:
+                    stage(lax.div(i, subs), lax.rem(i, subs), 1, True)
                 return carry
 
             lax.fori_loop(0, n_chunks * subs, sub, 0)
@@ -897,15 +952,15 @@
         key, bounds = pl.pallas_call(
             lambda *refs: sort_kernel(own, *refs),
             out_shape=[
-                shape(n_chunks, CHUNK // LANES, LANES, dtype=jnp.int32),
+                shape(n_chunks + 1, CHUNK // LANES, LANES, dtype=jnp.int32),
                 shape(2, LANES, dtype=jnp.int32),
             ],
-            in_specs=[SMEM, VMEM, VMEM],
+            in_specs=[VMEM] * 3,
             out_specs=[VMEM] * 2,
             scratch_shapes=[pltpu.VMEM((16 * regs, LANES), F32)],
             compiler_params=PARAMS,
         )(
-            edge_count,
+            edge_count.reshape(1, 1),
             jnp.pad(centre, pad).reshape(n_rows, LANES),
             jnp.pad(other, pad).reshape(n_rows, LANES),
         )
@@ -940,30 +995,41 @@
         came[1], half, weights = lax.optimization_barrier((came[1], half, weights))
         came[0] = plan.send(0, glue(plan, 0, (1, 2), plan.own_rest, own_rows, came))
 
-    planes = (n_chunks, chans, CHUNK)
+    blocks = n_chunks + 1
+    per = CHUNK // LANES
+    planes = pltpu.VMEM((blocks, chans, CHUNK), BF16)
+    buffer = pltpu.VMEM((chans, CHUNK), BF16)
+    env = pltpu.VMEM((9, own + WIN, chans), F32)
     scratch = [
         pltpu.VMEM((n_table, chans), F32),
         pltpu.VMEM((n_ghost, chans), F32),
         pltpu.VMEM((-(-n_ghost // LANES) * LANES, LANES), F32),
         pltpu.VMEM((chans, n_table), BF16),
-        pltpu.VMEM((n_rows * 8, LANES), F32),
-        pltpu.VMEM((n_rows * n_basis, LANES), F32),
-        pltpu.VMEM((8, n_chunks, CHUNK // LANES, LANES), F32),
-        pltpu.VMEM(planes, BF16),
-        pltpu.VMEM(planes, BF16),
-        pltpu.VMEM(planes, BF16),
-        pltpu.VMEM(planes, BF16),
-        pltpu.VMEM((edges_up // SUB, 9 * WIN, SUB), BF16),
-        pltpu.VMEM((9, own + WIN, chans), F32),
-        pltpu.VMEM((9, own + WIN, chans), F32),
-        pltpu.VMEM((chans, CHUNK), F32),
-        pltpu.VMEM(planes, BF16),
-        pltpu.VMEM(planes, BF16),
-        pltpu.VMEM(planes, BF16),
-        pltpu.VMEM((n_chunks, CHUNK // LANES, LANES), F32),
-        pltpu.VMEM((9, CHUNK // LANES, LANES), F32),
-        pltpu.VMEM((CHUNK // LANES * n_basis, LANES), F32),
-        pltpu.VMEM((CHUNK // LANES * 16, LANES), F32),
+        pltpu.VMEM((blocks * per * 8, LANES), F32),
+        pltpu.VMEM((blocks * per * n_basis, LANES), F32),
+        pltpu.VMEM((8, blocks, per, LANES), F32),
+        planes,
+        planes,
+        planes,
+        planes,
+        pltpu.VMEM((blocks * CHUNK // SUB, 9 * WIN, SUB), BF16),
+        env,
+        env,
+        pltpu.VMEM((chans, SUB), F32),
+        buffer,
+        buffer,
+        buffer,
+        buffer,
+        buffer,
+        planes,
+        planes,
+        planes,
+        pltpu.VMEM((blocks, chans, CHUNK), F32),
+        planes,
+        pltpu.VMEM((blocks, per, LANES), F32),
+        pltpu.VMEM((blocks, 9, per, LANES), F32),
+        pltpu.VMEM((per * n_basis, LANES), F32),
+        pltpu.VMEM((per * 16, LANES), F32),
         pltpu.VMEM((n_sel - own, 2 * LANES), F32),
         pltpu.VMEM((own + WIN, 2 * LANES), F32),
     ]

time: 55.8 us -> 62.3 us (1.12); the launches traced: 55.5 us -> 61.4 us
  starting transfers between devices: 14.1 us -> 18 us
  Pallas kernels: 21.3 us -> 23 us
    ppermute x10, starting transfers between devices: 14.1 us -> 18 us  [send(): lax.ppermute(message, AXES[a], [(i, (i + step) % n) for i in range(n)])]
    pallas_call x1, Pallas kernels: 15.7 us -> 17.3 us  [local(): pl.pallas_call(lambda *refs: main_kernel(plan, *refs), out_shape=[shape(o...]
  transfers between devices with their start and end apart: 10 -> 10, of which waited for: 7 -> 8; matrix products, arithmetic and copies ran while one was open for 0% -> 0% of each run, Pallas kernels for 7% -> 6%
where the time goes in v3:
time: 62.3 us; the launch traced here: 61.4 us
  Pallas kernels  23 us (37%)
  starting transfers between devices  18 us (29%)
  waiting for transfers between devices  15.4 us (25%)
  other arithmetic  2.27 us (4%)
  between operations  1.47 us (2%)
  local copies, waits for them, and re-layouts  1.35 us (2%)
    ppermute x10, starting transfers between devices, send(): lax.ppermute(message, AXES[a], [(i, (i + step) % n) for i in range(n)])  18 us
    pallas_call x1, Pallas kernels, local(): pl.pallas_call(lambda *refs: main_kernel(plan, *refs), out_shape=[shape(o...  17.3 us
    ppermute x10, waiting for transfers between devices, send(): lax.ppermute(message, AXES[a], [(i, (i + step) % n) for i in range(n)])  15.4 us
    pallas_call x1, Pallas kernels, local(): pl.pallas_call(lambda *refs: sort_kernel(own, *refs), out_shape=[shape(n_...  2.58 us
    convert_element_type x3, other arithmetic, stack(): part = jnp.pad(x.astype(dtype), ((at, below), (0, LANES - x.shape[1])))  1.38 us
    unnamed x24, local copies, waits for them, and re-layouts  1.35 us
  transfers between devices with their start and end apart: 10, of which 8 were waited for; matrix products, arithmetic and copies ran while one was open for 0% of the time, Pallas kernels for 6%

profile of v3, /device:TPU:0, one launch (start us, length us, event | category | flops | bytes accessed | tf_op | source)
XLA Modules:
  0.0 61.4 jit_solution(6466920096338326200)
XLA Ops:
  0.6 0.7 %convert_bitcast_fusion.1 = f32[2,8]{1,0:T(2,128)S(1)} fusion(s32[1,8,2]{1,2,0:T(2,128)} %param.20), kind=kLoop, calls=%fused_computation.6 | loop fusion | flops 16 | bytes 128 | tf_op jit(solution)/shard_map/prep/convert_element_type | solution.py:889
  1.3 0.0 copy-start.10
  1.3 0.7 %fusion = f32[6,32]{1,0:T(8,128)S(1)} fusion(s32[1,6,32]{2,0,1:T(1,128)} %param.18), kind=kLoop, calls=%fused_computation.4 | loop fusion | flops 192 | bytes 1536 | tf_op jit(solution)/shard_map/prep/convert_element_type | solution.py:889
  2.0 0.0 copy-done.10
  2.0 0.7 %copy-done.4 = f32[3,128]{1,0:T(4,128)S(1)} copy-done((f32[3,128]{1,0:T(4,128)S(1)}, f32[3,128]{1,0:T(4,128)}, u32[]{:S(2)}) %copy-start.4) | copy-done | bytes 1560
  2.7 0.9 %pad_add_fusion.2.refs_0_.rows_ref = f32[160,128]{1,0:T(8,128)S(1)} fusion(f32[2,8]{1,0:T(2,128)S(1)} %convert_bitcast_fusion.1, f32[8,12]{1,0:T(8,128)S(1)} %convert_bitcast_fusion, f32[6,32]{1,0:T(8,128)S(1)} %fusion, f32[3,128]{1,0:T(4,128)S(1)} %copy-done.4, f32[128,128]{1,0:T(8,128)} %param.17), kind=kLoop, calls=%fused_computation.2 | loop fusion | flops 81920 | bytes 150208 | tf_op jit(solution)/shard_map/prep/add | solution.py:890
  3.6 0.0 copy-start.1
  3.6 0.7 %prep.1 = (f32[162,128]{1,0:T(8,128)S(1)}, f32[168,128]{1,0:T(8,128)S(1)}, f32[330,128]{1,0:T(8,128)S(1)}) custom-call(f32[160,128]{1,0:T(8,128)S(1)} %pad_add_fusion.2.refs_0_.rows_ref), custom_call_target="tpu_custom_call" | custom-call | tf_op jit(solution)/shard_map/prep/pallas_call | solution.py:935
  4.3 3.0 %collective-permute-start = (f32[162,128]{1,0:T(8,128)S(1)}, f32[162,128]{1,0:T(8,128)S(1)}, u32[]{:S(2)}, u32[]{:S(2)}) collective-permute-start(f32[162,128]{1,0:T(8,128)S(1)} %get-tuple-element.51), channel_id=1, source_target_pairs={{0,1},{1,0},{2,3},{3,2},{4,5},{5,4},{6,7},{7,6},{8,9},{9,8},{10,11... | collective-permute-start | bytes 248840 | tf_op jit(solution)/shard_map/halo_z/ppermute | solution.py:128
  7.9 0.0 copy-done.2
  7.9 0.0 copy-done.3
  7.9 0.0 copy-start.9
  7.9 2.6 %group_edges.1 = (s32[13,4,128]{2,1,0:T(4,128)S(1)}, s32[2,128]{1,0:T(2,128)S(1)}) custom-call(s32[1,1]{1,0:T(1,128)} %bitcast.15.refs_0_, s32[48,128]{1,0:T(8,128)S(1)} %bitcast.16, s32[48,128]{1,0:T(8,128)S(1)} %bitcast.17), custom_call_target="tpu_custom_call" | custom-call | tf_op jit(solution)/shard_map/group_edges/pallas_call | solution.py:952
  10.5 0.0 copy-done
  10.5 0.0 copy-done.1
  10.5 0.0 copy-done.9
  10.6 0.0 collective-permute-done.refs_1_.refs_3_.refs_8_
  10.6 0.0 copy-start.5
  10.6 0.0 copy-start.6
  10.6 0.0 copy-start.7
  10.6 0.0 copy-start.8
  10.6 3.7 %collective-permute-start.1 = (f32[81,128]{1,0:T(8,128)S(1)}, f32[81,128]{1,0:T(8,128)S(1)}, u32[]{:S(2)}, u32[]{:S(2)}) collective-permute-start(f32[81,128]{1,0:T(8,128)S(1)} %get-tuple-element.58), channel_id=1, source_target_pairs={{0,6},{2,0},{4,2},{6,4},{1,7},{3,1},{5,3},{7,5},{8,14},{10,8},{12,... | collective-permute-start | bytes 124424 | tf_op jit(solution)/shard_map/halo_y/ppermute | solution.py:128
  14.3 0.0 collective-permute-start.2
  14.3 0.0 copy-done.5
  14.3 0.0 copy-done.6
  14.3 0.0 copy-done.7
  14.3 0.0 copy-done.8
  14.3 0.6 %copy-done.11 = bf16[128]{0:T(256)(128)(2,1)S(1)} copy-done((bf16[128]{0:T(256)(128)(2,1)S(1)}, bf16[128]{0:T(256)(128)(2,1)}, u32[]{:S(2)}) %copy-start.11) | copy-done | bytes 280
  15.0 0.3 weights.1
  15.3 0.7 %collective-permute-done.1.refs_1_.refs_6_ = f32[81,128]{1,0:T(8,128)S(1)} collective-permute-done((f32[81,128]{1,0:T(8,128)S(1)}, f32[81,128]{1,0:T(8,128)S(1)}, u32[]{:S(2)}, u32[]{:S(2)}) %collective-permute-start.1) | collective-permute-done | bytes 41504 | tf_op jit(solution)/shard_map/halo_y/ppermute | solution.py:128
  16.0 4.1 %collective-permute-done.2.refs_2_.refs_7_ = f32[81,128]{1,0:T(8,128)S(1)} collective-permute-done((f32[81,128]{1,0:T(8,128)S(1)}, f32[81,128]{1,0:T(8,128)S(1)}, u32[]{:S(2)}, u32[]{:S(2)}) %collective-permute-start.2) | collective-permute-done | bytes 41504 | tf_op jit(solution)/shard_map/halo_y/ppermute | solution.py:128
  20.2 0.1 collective-permute-start.3
  20.2 0.5 collective-permute-start.4
  20.7 1.2 %collective-permute-done.3.refs_4_ = f32[81,128]{1,0:T(8,128)S(1)} collective-permute-done((f32[81,128]{1,0:T(8,128)S(1)}, f32[81,128]{1,0:T(8,128)S(1)}, u32[]{:S(2)}, u32[]{:S(2)}) %collective-permute-start.3) | collective-permute-done | bytes 41504 | tf_op jit(solution)/shard_map/halo_x/ppermute | solution.py:128
  21.9 2.3 %collective-permute-done.4.refs_5_ = f32[81,128]{1,0:T(8,128)S(1)} collective-permute-done((f32[81,128]{1,0:T(8,128)S(1)}, f32[81,128]{1,0:T(8,128)S(1)}, u32[]{:S(2)}, u32[]{:S(2)}) %collective-permute-start.4) | collective-permute-done | bytes 41504 | tf_op jit(solution)/shard_map/halo_x/ppermute | solution.py:128
  24.2 17.3 %layer.1 = (f32[144,128]{1,0:T(8,128)S(1)}, f32[256,256]{1,0:T(8,128)S(1)}, f32[81,128]{1,0:T(8,128)S(1)}, f32[81,128]{1,0:T(8,128)S(1)}, f32[168,128]{1,0:T(8,128)S(1)}) custom-call(s32[2,128]{1,0:T(2,128)S(1)} %get-tuple-element.54.refs_0_, s32[13,4,128]{2,1,0:T(4,128)S(1)} %get-tuple-element.55.refs_1_, f32[3,128]{1,0:T(4,128)S(1)} %copy-done.4, ...), custom_call_target="tpu_custom_call" | custom-call | tf_op jit(solution)/shard_map/layer/pallas_call | solution.py:1039
  41.5 5.6 %collective-permute-start.5 = (f32[81,128]{1,0:T(8,128)S(1)}, f32[81,128]{1,0:T(8,128)S(1)}, u32[]{:S(2)}, u32[]{:S(2)}) collective-permute-start(f32[81,128]{1,0:T(8,128)S(1)} %get-tuple-element.89), channel_id=1, source_target_pairs={{0,8},{8,16},{16,24},{24,0},{1,9},{9,17},{17,25},{25,1},{2,10},{10... | collective-permute-start | bytes 124424 | tf_op jit(solution)/shard_map/halo_back/ppermute | solution.py:128
  47.1 0.0 collective-permute-start.6
  47.1 0.9 %collective-permute-done.5.refs_1_.refs_3_.refs_4_ = f32[81,128]{1,0:T(8,128)S(1)} collective-permute-done((f32[81,128]{1,0:T(8,128)S(1)}, f32[81,128]{1,0:T(8,128)S(1)}, u32[]{:S(2)}, u32[]{:S(2)}) %collective-permute-start.5) | collective-permute-done | bytes 41504 | tf_op jit(solution)/shard_map/halo_back/ppermute | solution.py:128
  48.0 0.8 %collective-permute-done.6.refs_2_.refs_4_.refs_5_ = f32[81,128]{1,0:T(8,128)S(1)} collective-permute-done((f32[81,128]{1,0:T(8,128)S(1)}, f32[81,128]{1,0:T(8,128)S(1)}, u32[]{:S(2)}, u32[]{:S(2)}) %collective-permute-start.6) | collective-permute-done | bytes 41504 | tf_op jit(solution)/shard_map/halo_back/ppermute | solution.py:128
  48.9 0.4 collective-permute-start.7
  49.2 3.5 %collective-permute-start.8 = (f32[81,128]{1,0:T(8,128)S(1)}, f32[81,128]{1,0:T(8,128)S(1)}, u32[]{:S(2)}, u32[]{:S(2)}) collective-permute-start(f32[81,128]{1,0:T(8,128)S(1)} %get-tuple-element.93), channel_id=1, source_target_pairs={{0,6},{2,0},{4,2},{6,4},{1,7},{3,1},{5,3},{7,5},{8,14},{10,8},{12,... | collective-permute-start | bytes 124424 | tf_op jit(solution)/shard_map/halo_back/ppermute | solution.py:128
  52.7 2.0 %collective-permute-done.7.refs_1_.refs_6_ = f32[81,128]{1,0:T(8,128)S(1)} collective-permute-done((f32[81,128]{1,0:T(8,128)S(1)}, f32[81,128]{1,0:T(8,128)S(1)}, u32[]{:S(2)}, u32[]{:S(2)}) %collective-permute-start.7) | collective-permute-done | bytes 41504 | tf_op jit(solution)/shard_map/halo_back/ppermute | solution.py:128
  54.8 0.0 collective-permute-done.8.refs_2_.refs_7_
  54.8 1.3 %collective-permute-start.9 = (f32[162,128]{1,0:T(8,128)S(1)}, f32[162,128]{1,0:T(8,128)S(1)}, u32[]{:S(2)}, u32[]{:S(2)}) collective-permute-start(f32[162,128]{1,0:T(8,128)S(1)} %halo_back.3), channel_id=1, source_target_pairs={{0,1},{1,0},{2,3},{3,2},{4,5},{5,4},{6,7},{7,6},{8,9},{9,8},{10,11... | collective-permute-start | bytes 248840 | tf_op jit(solution)/shard_map/halo_back/ppermute | solution.py:128
  56.1 0.8 %own_part.1 = (f32[1,128]{1,0:T(1,128)}, f32[128,128]{1,0:T(8,128)S(1)}, f32[3,128]{1,0:T(4,128)S(1)}) custom-call(f32[144,128]{1,0:T(8,128)S(1)} %get-tuple-element.85.ae_ref, f32[256,256]{1,0:T(8,128)S(1)} %get-tuple-element.86.own_ref, f32[128,128]{1,0:T(8,128)S(1)} %copy-done.1, f32[128,128]{1,0:T(8,128)S(1)} %copy-done), custom_call_target="tpu_custom_call" | custom-call | tf_op jit(solution)/shard_map/own_part/pallas_call | solution.py:1056
  56.9 3.3 %collective-permute-done.9.refs_8_ = f32[162,128]{1,0:T(8,128)S(1)} collective-permute-done((f32[162,128]{1,0:T(8,128)S(1)}, f32[162,128]{1,0:T(8,128)S(1)}, u32[]{:S(2)}, u32[]{:S(2)}) %collective-permute-start.9) | collective-permute-done | bytes 82976 | tf_op jit(solution)/shard_map/halo_back/ppermute | solution.py:128
  60.2 1.2 %owner_sums.1 = (f32[3,128]{1,0:T(4,128)}, f32[128,128]{1,0:T(8,128)}) custom-call(f32[330,128]{1,0:T(8,128)S(1)} %get-tuple-element.50.refs_0_, f32[128,128]{1,0:T(8,128)S(1)} %get-tuple-element.87.refs_1_, f32[3,128]{1,0:T(4,128)S(1)} %get-tuple-element.88.refs_2_, f32[128,128]{1,0:T(8,128)S(1)} %copy-done, ...), custom_call_target="tpu_custom_call" | custom-call | tf_op jit(solution)/shard_map/owner_sums/pallas_call | solution.py:1066
  (12 shorter events, 0.1 us)
Async XLA Ops:
  1.3 0.7 %copy-start.10 = (s32[1,12,8]{1,2,0:T(8,128)S(1)}, s32[1,12,8]{1,2,0:T(8,128)}, u32[]{:S(2)}) copy-start(s32[1,12,8]{1,2,0:T(8,128)} %param.19) | copy-start | bytes 1156
  2.0 0.7 %copy-start.4 = (f32[3,128]{1,0:T(4,128)S(1)}, f32[3,128]{1,0:T(4,128)}, u32[]{:S(2)}) copy-start(f32[3,128]{1,0:T(4,128)} %refs_2_.1) | copy-start | bytes 4612
  2.7 5.2 %copy-start.2 = (s32[6144]{0:T(1024)S(1)}, s32[6144]{0:T(1024)}, u32[]{:S(2)}) copy-start(s32[6144]{0:T(1024)} %param.21) | copy-start | bytes 73732
  2.7 5.2 %copy-start.3 = (s32[6144]{0:T(1024)S(1)}, s32[6144]{0:T(1024)}, u32[]{:S(2)}) copy-start(s32[6144]{0:T(1024)} %param.22) | copy-start | bytes 73732
  3.6 7.0 %copy-start = (f32[128,128]{1,0:T(8,128)S(1)}, f32[128,128]{1,0:T(8,128)}, u32[]{:S(2)}) copy-start(f32[128,128]{1,0:T(8,128)} %refs_3_.3) | copy-start | bytes 196612
  3.6 7.0 %copy-start.1 = (f32[128,128]{1,0:T(8,128)S(1)}, f32[128,128]{1,0:T(8,128)}, u32[]{:S(2)}) copy-start(f32[128,128]{1,0:T(8,128)} %wa_ref.1) | copy-start | bytes 196612
  4.3 6.3 %collective-permute-start = (f32[162,128]{1,0:T(8,128)S(1)}, f32[162,128]{1,0:T(8,128)S(1)}, u32[]{:S(2)}, u32[]{:S(2)}) collective-permute-start(f32[162,128]{1,0:T(8,128)S(1)} %get-tuple-element.51), channel_id=1, source_target_pairs={{0,1},{1,0},{2,3},{3,2},{4,5},{5,4},{6,7},{7,6},{8,9},{9,8},{10,11... | collective-permute-start | bytes 248840 | tf_op jit(solution)/shard_map/halo_z/ppermute | solution.py:128
  7.9 2.6 %copy-start.9 = (f32[8,128]{1,0:T(8,128)S(1)}, f32[8,128]{1,0:T(8,128)}, u32[]{:S(2)}) copy-start(f32[8,128]{1,0:T(8,128)} %param.26) | copy-start | bytes 12292
  10.6 3.7 %copy-start.5 = (bf16[256,128]{1,0:T(8,128)(2,1)S(1)}, bf16[256,128]{1,0:T(8,128)(2,1)}, u32[]{:S(2)}) copy-start(bf16[256,128]{1,0:T(8,128)(2,1)} %param.30) | copy-start | bytes 196612
  10.6 3.7 %copy-start.6 = (bf16[128,128]{1,0:T(8,128)(2,1)S(1)}, bf16[128,128]{1,0:T(8,128)(2,1)}, u32[]{:S(2)}) copy-start(bf16[128,128]{1,0:T(8,128)(2,1)} %param.29) | copy-start | bytes 98308
  10.6 3.7 %copy-start.7 = (bf16[128,128]{1,0:T(8,128)(2,1)S(1)}, bf16[128,128]{1,0:T(8,128)(2,1)}, u32[]{:S(2)}) copy-start(bf16[128,128]{1,0:T(8,128)(2,1)} %param.28) | copy-start | bytes 98308
  10.6 3.7 %copy-start.8 = (bf16[128,128]{1,0:T(8,128)(2,1)S(1)}, bf16[128,128]{1,0:T(8,128)(2,1)}, u32[]{:S(2)}) copy-start(bf16[128,128]{1,0:T(8,128)(2,1)} %param.27) | copy-start | bytes 98308
  10.6 5.4 %collective-permute-start.1 = (f32[81,128]{1,0:T(8,128)S(1)}, f32[81,128]{1,0:T(8,128)S(1)}, u32[]{:S(2)}, u32[]{:S(2)}) collective-permute-start(f32[81,128]{1,0:T(8,128)S(1)} %get-tuple-element.58), channel_id=1, source_target_pairs={{0,6},{2,0},{4,2},{6,4},{1,7},{3,1},{5,3},{7,5},{8,14},{10,8},{12,... | collective-permute-start | bytes 124424 | tf_op jit(solution)/shard_map/halo_y/ppermute | solution.py:128
  14.3 0.7 %copy-start.11 = (bf16[128]{0:T(256)(128)(2,1)S(1)}, bf16[128]{0:T(256)(128)(2,1)}, u32[]{:S(2)}) copy-start(bf16[128]{0:T(256)(128)(2,1)} %param.31) | copy-start | bytes 772
  14.3 5.8 %collective-permute-start.2 = (f32[81,128]{1,0:T(8,128)S(1)}, f32[81,128]{1,0:T(8,128)S(1)}, u32[]{:S(2)}, u32[]{:S(2)}) collective-permute-start(f32[81,128]{1,0:T(8,128)S(1)} %get-tuple-element.59), channel_id=1, source_target_pairs={{0,2},{2,4},{4,6},{6,0},{1,3},{3,5},{5,7},{7,1},{8,10},{10,12},{12... | collective-permute-start | bytes 124424 | tf_op jit(solution)/shard_map/halo_y/ppermute | solution.py:128
  20.2 1.8 %collective-permute-start.3 = (f32[81,128]{1,0:T(8,128)S(1)}, f32[81,128]{1,0:T(8,128)S(1)}, u32[]{:S(2)}, u32[]{:S(2)}) collective-permute-start(f32[81,128]{1,0:T(8,128)S(1)} %get-tuple-element.75), channel_id=1, source_target_pairs={{0,24},{8,0},{16,8},{24,16},{1,25},{9,1},{17,9},{25,17},{2,26},{10... | collective-permute-start | bytes 124424 | tf_op jit(solution)/shard_map/halo_x/ppermute | solution.py:128
  20.2 4.0 %collective-permute-start.4 = (f32[81,128]{1,0:T(8,128)S(1)}, f32[81,128]{1,0:T(8,128)S(1)}, u32[]{:S(2)}, u32[]{:S(2)}) collective-permute-start(f32[81,128]{1,0:T(8,128)S(1)} %get-tuple-element.76), channel_id=1, source_target_pairs={{0,8},{8,16},{16,24},{24,0},{1,9},{9,17},{17,25},{25,1},{2,10},{10... | collective-permute-start | bytes 124424 | tf_op jit(solution)/shard_map/halo_x/ppermute | solution.py:128
  41.5 6.5 %collective-permute-start.5 = (f32[81,128]{1,0:T(8,128)S(1)}, f32[81,128]{1,0:T(8,128)S(1)}, u32[]{:S(2)}, u32[]{:S(2)}) collective-permute-start(f32[81,128]{1,0:T(8,128)S(1)} %get-tuple-element.89), channel_id=1, source_target_pairs={{0,8},{8,16},{16,24},{24,0},{1,9},{9,17},{17,25},{25,1},{2,10},{10... | collective-permute-start | bytes 124424 | tf_op jit(solution)/shard_map/halo_back/ppermute | solution.py:128
  47.1 1.7 %collective-permute-start.6 = (f32[81,128]{1,0:T(8,128)S(1)}, f32[81,128]{1,0:T(8,128)S(1)}, u32[]{:S(2)}, u32[]{:S(2)}) collective-permute-start(f32[81,128]{1,0:T(8,128)S(1)} %get-tuple-element.90), channel_id=1, source_target_pairs={{0,24},{8,0},{16,8},{24,16},{1,25},{9,1},{17,9},{25,17},{2,26},{10... | collective-permute-start | bytes 124424 | tf_op jit(solution)/shard_map/halo_back/ppermute | solution.py:128
  48.9 5.9 %collective-permute-start.7 = (f32[81,128]{1,0:T(8,128)S(1)}, f32[81,128]{1,0:T(8,128)S(1)}, u32[]{:S(2)}, u32[]{:S(2)}) collective-permute-start(f32[81,128]{1,0:T(8,128)S(1)} %get-tuple-element.92), channel_id=1, source_target_pairs={{0,2},{2,4},{4,6},{6,0},{1,3},{3,5},{5,7},{7,1},{8,10},{10,12},{12... | collective-permute-start | bytes 124424 | tf_op jit(solution)/shard_map/halo_back/ppermute | solution.py:128
  49.2 5.5 %collective-permute-start.8 = (f32[81,128]{1,0:T(8,128)S(1)}, f32[81,128]{1,0:T(8,128)S(1)}, u32[]{:S(2)}, u32[]{:S(2)}) collective-permute-start(f32[81,128]{1,0:T(8,128)S(1)} %get-tuple-element.93), channel_id=1, source_target_pairs={{0,6},{2,0},{4,2},{6,4},{1,7},{3,1},{5,3},{7,5},{8,14},{10,8},{12,... | collective-permute-start | bytes 124424 | tf_op jit(solution)/shard_map/halo_back/ppermute | solution.py:128
  54.8 5.4 %collective-permute-start.9 = (f32[162,128]{1,0:T(8,128)S(1)}, f32[162,128]{1,0:T(8,128)S(1)}, u32[]{:S(2)}, u32[]{:S(2)}) collective-permute-start(f32[162,128]{1,0:T(8,128)S(1)} %halo_back.3), channel_id=1, source_target_pairs={{0,1},{1,0},{2,3},{3,2},{4,5},{5,4},{6,7},{7,6},{8,9},{9,8},{10,11... | collective-permute-start | bytes 248840 | tf_op jit(solution)/shard_map/halo_back/ppermute | solution.py:128

commit v4 on v2

--- a/solution.py
+++ b/solution.py
@@ -160,19 +160,19 @@
     return out[:, 0 : x.shape[1]] + out[:, x.shape[1] :]
 
 
-def prep_kernel(plan, rows_ref, *outs):
+def prep_kernel(plan, rows_ref, pos_ref, corner_ref, *outs):
     n_z = len(plan.groups[2])
     sends, rest_ref, sel_ref, turn_ref = outs[:n_z], outs[n_z], outs[n_z + 1], outs[n_z + 2]
     own = sel_ref.shape[1]
     lane = lax.broadcasted_iota(jnp.int32, (1, own), 1).astype(F32)
     n_faces = len(CLASSES[0])
     turn_ref[...] = jnp.zeros_like(turn_ref)
-    turn_ref[0:n_faces, :] = rows_ref[own + 8 : own + 8 + n_faces, :]
-    columns = [turn_ref[...].T]
-    at = own + 16
-    for width in plan.widths[1:]:
-        columns.append(rows_ref[at : at + width, :])
-        at += -(-width // 8) * 8
+    turn_ref[0:n_faces, :] = rows_ref[own : own + n_faces, :]
+    columns = [
+        turn_ref[...].T,
+        rows_ref[own + 8 : own + 8 + plan.widths[1], :],
+        corner_ref[0].astype(F32),
+    ]
     sel_ref[...] = jnp.zeros_like(sel_ref)
     messages = plan.groups[2] + [plan.own_rest]
     at = 0
@@ -183,7 +183,7 @@
             column = columns[kind(off)][0:live, key : key + 1]
             sel_ref[at + begin : at + begin + live, :] = (column == lane).astype(F32)
         at += plan.total(blocks)
-    pos = dot_tn(rows_ref[own : own + 3, :], group_rows(3), HIGH)
+    pos = dot_tn(pos_ref[...], group_rows(3), HIGH)
     sel = sel_ref[...]
     rows = dot_nn(sel, rows_ref[0:own, :], HIGH)
     places = dot_nn(sel, pos, HIGH)
@@ -228,7 +228,8 @@
     group = regs * 8
     row = lax.broadcasted_iota(jnp.int32, (rows, LANES), 0)
     lane = lax.broadcasted_iota(jnp.int32, (rows, LANES), 1)
-    live = row * LANES + lane < count_ref[0]
+    count = count_ref[count_ref.shape[0] - 8 : count_ref.shape[0] - 7, 0:1].astype(jnp.int32)
+    live = row * LANES + lane < count
     centre = centre_ref[...]
     key = jnp.where(live, (centre << OTHER_BITS) + other_ref[...], dead).astype(F32)
     x = [key[8 * v : 8 * v + 8, :] for v in range(rows // 8)]
@@ -419,7 +420,7 @@
 
 
 def main_kernel(plan, *refs):
-    bound_ref, key_ref, pos_ref, wb_ref = refs[:4]
+    bound_ref, key_ref, pos_ref, wide_ref = refs[:4]
     came, refs = plan.cut(refs[4:], 0, 1, 2)
     half_ref, w1t_ref, wevt_ref, w2t_ref, w1_ref, wev_ref, w2_ref, wcol_ref = refs[:8]
     ae_ref, own_ref = refs[8:10]
@@ -473,7 +474,7 @@
     ghost_pos = dot_nt(group_rows(8), place_ref[...], HIGH)
     pos_t = jnp.concatenate([pos_ref[...], ghost_pos[0:3, :]], axis=1)
     f_hi, f_lo = split(ghost_ref[...])
-    w_hi, w_lo = split(wb_ref[...])
+    w_hi, w_lo = split(wide_ref[chans : 2 * chans, :])
     tab_ref[0 : 2 * own, :] = half_ref[0 : 2 * own, :]
     tab_ref[2 * own : n_sel, :] = dot_nn(
         jnp.concatenate([f_hi, f_lo, f_hi], axis=1).astype(BF16),
@@ -791,33 +792,49 @@
             ref[row + live : row + live + 1, :] = jnp.sum(diagonal(block), axis=0, keepdims=True)
 
 
-def own_kernel(ae_ref, own_ref, wa_ref, wb_ref, energy_ref, fg_ref, force_ref):
-    chans = wa_ref.shape[1]
-    own = force_ref.shape[1]
-    energy_ref[...] = jnp.sum(ae_ref[0:own, :].T, axis=0, keepdims=True)
-    fg_ref[...] = dot_nt(own_ref[0:own, 0:chans], wa_ref[...], HIGH) + dot_nt(
-        own_ref[own:, 0:chans], wb_ref[...], HIGH
-    )
-    force = (own_ref[own:, LANES:] - own_ref[0:own, LANES:]).T
-    force_ref[...] = force[0:3, :] + force[3:6, :]
-
-
-def last_kernel(plan, sel_ref, fg_ref, force_ref, wb_ref, *refs):
-    came, refs = plan.cut(refs, 0, 1, 2)
-    out_force_ref, out_fg_ref, both_ref = refs
+def returned_sums(plan, came, axes, messages, first, sel_ref, both_ref):
+    chans = both_ref.shape[1] - LANES
     both_ref[...] = jnp.zeros_like(both_ref)
-    chans = fg_ref.shape[1]
     at = 0
-    for blocks in plan.groups[2] + [plan.own_rest]:
+    for blocks in messages:
         for off, row in plan.spans(blocks):
             live = plan.live(off)
-            src, begin = plan.find(came, (2, 1, 0), None, [], off)
+            src, begin = plan.find(came, axes, None, [], off)
             here = slice(at + row, at + row + live)
             both_ref[here, 0:chans] = src[begin : begin + live, :]
             both_ref[here, chans:] = spread(src[begin + live : begin + live + 1, :], live)
         at += plan.total(blocks)
-    sums = dot_exact(sel_ref[...].astype(BF16), both_ref[...], ((0,), (0,)))
-    out_fg_ref[...] = fg_ref[...] + dot_nt(sums[:, 0:chans], wb_ref[...], HIGH)
+    hot = sel_ref[first : first + at, :].astype(BF16)
+    return dot_exact(hot, both_ref[...], ((0,), (0,)))
+
+
+def own_kernel(plan, ae_ref, own_ref, wide_ref, sel_ref, *refs):
+    came, refs = plan.cut(refs, 0, 1)
+    energy_ref, fg_ref, force_ref, both_ref = refs
+    chans = fg_ref.shape[1]
+    own = force_ref.shape[1]
+    first = sum(plan.total(blocks) for blocks in plan.groups[2])
+    sums = returned_sums(plan, came, (1, 0), [plan.own_rest], first, sel_ref, both_ref)
+    energy_ref[...] = jnp.sum(ae_ref[0:own, :].T, axis=0, keepdims=True)
+    fg_ref[...] = dot_nt(own_ref[0:own, 0:chans], wide_ref[0:chans, :], HIGH) + dot_nt(
+        own_ref[own:, 0:chans] + sums[:, 0:chans], wide_ref[chans : 2 * chans, :], HIGH
+    )
+    force = (own_ref[own:, LANES:] - own_ref[0:own, LANES:]).T
+    total = dot_nt(group_rows(8), sums[:, chans:], HIGH)
+    force_ref[...] = force[0:3, :] + force[3:6, :] + total[0:3, :]
+
+
+def last_kernel(plan, sel_ref, fg_ref, force_ref, wide_ref, *refs):
+    came, refs = plan.cut(refs, 2)
+    out_force_ref, out_fg_ref, both_ref = refs
+    chans = fg_ref.shape[1]
+    sums = returned_sums(plan, came, (2,), plan.groups[2], 0, sel_ref, both_ref)
+    s_hi, s_lo = split(sums[:, 0:chans])
+    w_hi, w_lo = split(wide_ref[chans : 2 * chans, :])
+    out_fg_ref[...] = fg_ref[...] + dot_nt(
+        jnp.concatenate([s_hi, s_lo, s_hi], axis=1).astype(BF16),
+        jnp.concatenate([w_hi, w_hi, w_lo], axis=1).astype(BF16),
+    )
     total = dot_nt(group_rows(8), sums[:, chans:], HIGH)
     out_force_ref[...] = -(force_ref[...] + total[0:3, :])
 
@@ -871,21 +888,17 @@
 
     with jax.named_scope("prep"):
         rows = stack(
-            atom_features,
-            positions,
-            send_face[0],
-            jnp.transpose(send_edge[0]),
-            jnp.transpose(send_corner[0]),
+            atom_features, send_face[0], jnp.transpose(send_edge[0]), edge_count.reshape(1, 1)
         )
         *sends, own_rows, sel = pl.pallas_call(
             lambda *refs: prep_kernel(plan, *refs),
             out_shape=plan.shapes(2, chans)
             + [shape(plan.total(plan.own_rest), chans), shape(n_send, own)],
-            in_specs=[VMEM],
+            in_specs=[VMEM] * 3,
             out_specs=[VMEM] * (len(plan.groups[2]) + 2),
             scratch_shapes=[pltpu.VMEM((LANES, LANES), F32)],
             compiler_params=PARAMS,
-        )(rows)
+        )(rows, positions, jnp.transpose(send_corner, (0, 2, 1)))
 
     came = {}
     with jax.named_scope("halo_z"):
@@ -900,12 +913,12 @@
                 shape(n_chunks, CHUNK // LANES, LANES, dtype=jnp.int32),
                 shape(2, LANES, dtype=jnp.int32),
             ],
-            in_specs=[SMEM, VMEM, VMEM],
+            in_specs=[VMEM] * 3,
             out_specs=[VMEM] * 2,
             scratch_shapes=[pltpu.VMEM((16 * regs, LANES), F32)],
             compiler_params=PARAMS,
         )(
-            edge_count,
+            rows,
             jnp.pad(centre, pad).reshape(n_rows, LANES),
             jnp.pad(other, pad).reshape(n_rows, LANES),
         )
@@ -968,7 +981,7 @@
         pltpu.VMEM((own + WIN, 2 * LANES), F32),
     ]
     with jax.named_scope("layer"):
-        given = [bounds, key, positions, w_proj_b]
+        given = [bounds, key, positions, wide]
         given += [*came[0], *came[1], *came[2], half, *weights]
         atom_sums, own_sums, *back, held = pl.pallas_call(
             lambda *refs: main_kernel(plan, *refs),
@@ -987,22 +1000,25 @@
         home[2] = plan.send(2, glue(plan, 2, (1, 0), plan.held_rest, held, home), back=True)
 
     with jax.named_scope("own_part"):
+        given = [atom_sums, own_sums, wide, sel, *home[0], *home[1]]
         energy, fg, force = pl.pallas_call(
-            own_kernel,
+            lambda *refs: own_kernel(plan, *refs),
             out_shape=[shape(1, own), shape(own, chans), shape(3, own)],
-            in_specs=[VMEM] * 4,
+            in_specs=[VMEM] * len(given),
             out_specs=[VMEM] * 3,
+            scratch_shapes=[pltpu.VMEM((plan.total(plan.own_rest), chans + LANES), F32)],
             compiler_params=PARAMS,
-        )(atom_sums, own_sums, w_proj_a, w_proj_b)
+        )(*given)
 
     with jax.named_scope("owner_sums"):
-        given = [sel, fg, force, w_proj_b, *home[0], *home[1], *home[2]]
+        given = [sel, fg, force, wide, *home[2]]
+        n_z = n_send - plan.total(plan.own_rest)
         forces, feature_grad = pl.pallas_call(
             lambda *refs: last_kernel(plan, *refs),
             out_shape=[shape(3, own), shape(own, chans)],
             in_specs=[VMEM] * len(given),
             out_specs=[VMEM] * 2,
-            scratch_shapes=[pltpu.VMEM((n_send, chans + LANES), F32)],
+            scratch_shapes=[pltpu.VMEM((n_z, chans + LANES), F32)],
             compiler_params=PARAMS,
         )(*given)
     return forces, energy.reshape(own), feature_grad

time: 55.8 us -> 55.3 us (level)
  other arithmetic: 2.26 us -> 0.89 us
  starting transfers between devices: 14.1 us -> 14.8 us
  local copies, waits for them, and re-layouts: 1.35 us -> 2.02 us
    convert_element_type x3 -> x2, other arithmetic: 1.38 us -> 0.01 us  [stack(): part = jnp.pad(x.astype(dtype), ((at, below), (0, LANES - x.shape[1])))]
    ppermute x10, starting transfers between devices: 14.1 us -> 14.8 us  [send(): lax.ppermute(message, AXES[a], [(i, (i + step) % n) for i in range(n)])]
    unnamed x24 -> x28, local copies, waits for them, and re-layouts: 1.35 us -> 2.02 us
    ppermute x10, waiting for transfers between devices: 15 us -> 14.5 us  [send(): lax.ppermute(message, AXES[a], [(i, (i + step) % n) for i in range(n)])]
where the time goes in v4:
time: 55.3 us; the launch traced here: 55.1 us
  Pallas kernels  21.4 us (39%)
  starting transfers between devices  14.8 us (27%)
  waiting for transfers between devices  14.5 us (26%)
  local copies, waits for them, and re-layouts  2.02 us (4%)
  between operations  1.5 us (3%)
  other arithmetic  0.89 us (2%)
    pallas_call x1, Pallas kernels, local(): pl.pallas_call(lambda *refs: main_kernel(plan, *refs), out_shape=[shape(o...  15.7 us
    ppermute x10, starting transfers between devices, send(): lax.ppermute(message, AXES[a], [(i, (i + step) % n) for i in range(n)])  14.8 us
    ppermute x10, waiting for transfers between devices, send(): lax.ppermute(message, AXES[a], [(i, (i + step) % n) for i in range(n)])  14.5 us
    pallas_call x1, Pallas kernels, local(): pl.pallas_call(lambda *refs: sort_kernel(own, *refs), out_shape=[shape(n_...  2.55 us
    unnamed x28, local copies, waits for them, and re-layouts  2.02 us
  transfers between devices with their start and end apart: 10, of which 7 were waited for; matrix products, arithmetic and copies ran while one was open for 0% of the time, Pallas kernels for 7%

profile of v4, /device:TPU:0, one launch (start us, length us, event | category | flops | bytes accessed | tf_op | source)
XLA Modules:
  0.0 55.1 jit_solution(13182237416711944224)
XLA Ops:
  0.6 0.0 copy-start.12
  1.3 0.0 copy-start.11
  1.3 0.0 copy-done.12
  1.3 0.7 %copy-done.11 = s32[1,12,8]{1,2,0:T(8,128)S(1)} copy-done((s32[1,12,8]{1,2,0:T(8,128)S(1)}, s32[1,12,8]{1,2,0:T(8,128)}, u32[]{:S(2)}) %copy-start.11) | copy-done | bytes 408
  2.0 0.9 %pad_add_fusion.2.refs_0_.rows_ref = f32[152,128]{1,0:T(8,128)S(1)} fusion(f32[1,1]{1,0:T(1,128)} %bitcast.3, f32[8,12]{1,0:T(8,128)S(1)} %convert_bitcast_fusion, f32[6,32]{1,0:T(8,128)S(1)} %fusion, f32[128,128]{1,0:T(8,128)} %param.17), kind=kLoop, calls=%fused_computation.2 | loop fusion | flops 58368 | bytes 144516 | tf_op jit(solution)/shard_map/prep/add | solution.py:852
  2.9 0.0 copy-done.2
  2.9 0.7 %copy-done.3 = s32[1,8,2]{1,2,0:T(2,128)S(1)} copy-done((s32[1,8,2]{1,2,0:T(2,128)S(1)}, s32[1,8,2]{1,2,0:T(2,128)}, u32[]{:S(2)}) %copy-start.3) | copy-done | bytes 88
  3.5 0.7 %prep.1 = (f32[162,128]{1,0:T(8,128)S(1)}, f32[168,128]{1,0:T(8,128)S(1)}, f32[330,128]{1,0:T(8,128)S(1)}) custom-call(f32[152,128]{1,0:T(8,128)S(1)} %pad_add_fusion.2.refs_0_.rows_ref, f32[3,128]{1,0:T(4,128)S(1)} %copy-done.2, s32[1,2,8]{2,1,0:T(2,128)S(1)} %bitcast.14), custom_call_target="tpu_custom_call" | custom-call | tf_op jit(solution)/shard_map/prep/pallas_call | solution.py:893
  4.2 0.0 copy-start.5
  4.2 0.0 copy-start.4
  4.2 3.0 %collective-permute-start = (f32[162,128]{1,0:T(8,128)S(1)}, f32[162,128]{1,0:T(8,128)S(1)}, u32[]{:S(2)}, u32[]{:S(2)}) collective-permute-start(f32[162,128]{1,0:T(8,128)S(1)} %get-tuple-element.51), channel_id=1, source_target_pairs={{0,1},{1,0},{2,3},{3,2},{4,5},{5,4},{6,7},{7,6},{8,9},{9,8},{10,11... | collective-permute-start | bytes 248840 | tf_op jit(solution)/shard_map/halo_z/ppermute | solution.py:128
  7.2 0.0 copy-done
  7.2 0.0 copy-done.1
  7.2 2.5 %group_edges.1 = (s32[2,24,128]{2,1,0:T(8,128)S(1)}, s32[2,128]{1,0:T(2,128)S(1)}) custom-call(f32[152,128]{1,0:T(8,128)S(1)} %pad_add_fusion.2.refs_0_.rows_ref, s32[48,128]{1,0:T(8,128)S(1)} %bitcast.12, s32[48,128]{1,0:T(8,128)S(1)} %bitcast.13), custom_call_target="tpu_custom_call" | custom-call | tf_op jit(solution)/shard_map/group_edges/pallas_call | solution.py:910
  9.8 0.0 copy-done.10
  9.8 0.0 copy-done.5
  9.8 0.0 copy-done.4
  9.8 0.0 collective-permute-done.refs_1_.refs_3_.refs_8_
  9.9 0.0 copy-start.6
  9.9 0.0 copy-start.7
  9.9 0.0 copy-start.8
  9.9 0.0 copy-start.9
  9.9 4.0 %collective-permute-start.1 = (f32[81,128]{1,0:T(8,128)S(1)}, f32[81,128]{1,0:T(8,128)S(1)}, u32[]{:S(2)}, u32[]{:S(2)}) collective-permute-start(f32[81,128]{1,0:T(8,128)S(1)} %get-tuple-element.58), channel_id=1, source_target_pairs={{0,6},{2,0},{4,2},{6,4},{1,7},{3,1},{5,3},{7,5},{8,14},{10,8},{12,... | collective-permute-start | bytes 124424 | tf_op jit(solution)/shard_map/halo_y/ppermute | solution.py:128
  13.9 0.0 collective-permute-start.2
  13.9 0.0 copy-done.6
  13.9 0.0 copy-done.7
  13.9 0.0 copy-done.8
  14.0 0.6 %copy-done.13 = bf16[128]{0:T(256)(128)(2,1)S(1)} copy-done((bf16[128]{0:T(256)(128)(2,1)S(1)}, bf16[128]{0:T(256)(128)(2,1)}, u32[]{:S(2)}) %copy-start.13) | copy-done | bytes 280
  14.6 0.3 weights.1
  14.9 0.7 %collective-permute-done.1.refs_1_.refs_6_ = f32[81,128]{1,0:T(8,128)S(1)} collective-permute-done((f32[81,128]{1,0:T(8,128)S(1)}, f32[81,128]{1,0:T(8,128)S(1)}, u32[]{:S(2)}, u32[]{:S(2)}) %collective-permute-start.1) | collective-permute-done | bytes 41504 | tf_op jit(solution)/shard_map/halo_y/ppermute | solution.py:128
  15.6 4.1 %collective-permute-done.2.refs_2_.refs_7_ = f32[81,128]{1,0:T(8,128)S(1)} collective-permute-done((f32[81,128]{1,0:T(8,128)S(1)}, f32[81,128]{1,0:T(8,128)S(1)}, u32[]{:S(2)}, u32[]{:S(2)}) %collective-permute-start.2) | collective-permute-done | bytes 41504 | tf_op jit(solution)/shard_map/halo_y/ppermute | solution.py:128
  19.8 0.1 collective-permute-start.3
  19.8 0.5 collective-permute-start.4
  20.3 1.2 %collective-permute-done.3.refs_4_ = f32[81,128]{1,0:T(8,128)S(1)} collective-permute-done((f32[81,128]{1,0:T(8,128)S(1)}, f32[81,128]{1,0:T(8,128)S(1)}, u32[]{:S(2)}, u32[]{:S(2)}) %collective-permute-start.3) | collective-permute-done | bytes 41504 | tf_op jit(solution)/shard_map/halo_x/ppermute | solution.py:128
  21.6 2.3 %collective-permute-done.4.refs_5_ = f32[81,128]{1,0:T(8,128)S(1)} collective-permute-done((f32[81,128]{1,0:T(8,128)S(1)}, f32[81,128]{1,0:T(8,128)S(1)}, u32[]{:S(2)}, u32[]{:S(2)}) %collective-permute-start.4) | collective-permute-done | bytes 41504 | tf_op jit(solution)/shard_map/halo_x/ppermute | solution.py:128
  23.8 15.7 %layer.1 = (f32[144,128]{1,0:T(8,128)S(1)}, f32[256,256]{1,0:T(8,128)S(1)}, f32[81,128]{1,0:T(8,128)S(1)}, f32[81,128]{1,0:T(8,128)S(1)}, f32[168,128]{1,0:T(8,128)S(1)}) custom-call(s32[2,128]{1,0:T(2,128)S(1)} %get-tuple-element.54.refs_0_, s32[2,24,128]{2,1,0:T(8,128)S(1)} %get-tuple-element.55.refs_1_, f32[3,128]{1,0:T(4,128)S(1)} %copy-done.2, ...), custom_call_target="tpu_custom_call" | custom-call | tf_op jit(solution)/shard_map/layer/pallas_call | solution.py:986
  39.5 0.2 collective-permute-start.5
  39.7 1.6 %collective-permute-start.6 = (f32[81,128]{1,0:T(8,128)S(1)}, f32[81,128]{1,0:T(8,128)S(1)}, u32[]{:S(2)}, u32[]{:S(2)}) collective-permute-start(f32[81,128]{1,0:T(8,128)S(1)} %get-tuple-element.88), channel_id=1, source_target_pairs={{0,24},{8,0},{16,8},{24,16},{1,25},{9,1},{17,9},{25,17},{2,26},{10... | collective-permute-start | bytes 124424 | tf_op jit(solution)/shard_map/halo_back/ppermute | solution.py:128
  41.3 1.7 %collective-permute-done.5.refs_1_.refs_4_.refs_3_ = f32[81,128]{1,0:T(8,128)S(1)} collective-permute-done((f32[81,128]{1,0:T(8,128)S(1)}, f32[81,128]{1,0:T(8,128)S(1)}, u32[]{:S(2)}, u32[]{:S(2)}) %collective-permute-start.5) | collective-permute-done | bytes 41504 | tf_op jit(solution)/shard_map/halo_back/ppermute | solution.py:128
  43.1 0.0 collective-permute-done.6.refs_2_.refs_5_.refs_4_
  43.1 0.1 collective-permute-start.7
  43.2 3.8 %collective-permute-start.8 = (f32[81,128]{1,0:T(8,128)S(1)}, f32[81,128]{1,0:T(8,128)S(1)}, u32[]{:S(2)}, u32[]{:S(2)}) collective-permute-start(f32[81,128]{1,0:T(8,128)S(1)} %get-tuple-element.91), channel_id=1, source_target_pairs={{0,6},{2,0},{4,2},{6,4},{1,7},{3,1},{5,3},{7,5},{8,14},{10,8},{12,... | collective-permute-start | bytes 124424 | tf_op jit(solution)/shard_map/halo_back/ppermute | solution.py:128
  47.0 2.3 %collective-permute-done.7.refs_6_.refs_1_ = f32[81,128]{1,0:T(8,128)S(1)} collective-permute-done((f32[81,128]{1,0:T(8,128)S(1)}, f32[81,128]{1,0:T(8,128)S(1)}, u32[]{:S(2)}, u32[]{:S(2)}) %collective-permute-start.7) | collective-permute-done | bytes 41504 | tf_op jit(solution)/shard_map/halo_back/ppermute | solution.py:128
  49.3 0.0 collective-permute-done.8.refs_7_.refs_2_
  49.3 1.6 %collective-permute-start.9 = (f32[162,128]{1,0:T(8,128)S(1)}, f32[162,128]{1,0:T(8,128)S(1)}, u32[]{:S(2)}, u32[]{:S(2)}) collective-permute-start(f32[162,128]{1,0:T(8,128)S(1)} %halo_back.3), channel_id=1, source_target_pairs={{0,1},{1,0},{2,3},{3,2},{4,5},{5,4},{6,7},{7,6},{8,9},{9,8},{10,11... | collective-permute-start | bytes 248840 | tf_op jit(solution)/shard_map/halo_back/ppermute | solution.py:128
  50.8 1.1 %own_part.1 = (f32[1,128]{1,0:T(1,128)}, f32[128,128]{1,0:T(8,128)S(1)}, f32[3,128]{1,0:T(4,128)S(1)}) custom-call(f32[144,128]{1,0:T(8,128)S(1)} %get-tuple-element.85.refs_0_, f32[256,256]{1,0:T(8,128)S(1)} %get-tuple-element.86.refs_1_, f32[264,128]{1,0:T(8,128)S(1)} %pad_add_fusion.1.wide_ref.refs_3_.refs_2_, ...), custom_call_target="tpu_custom_call" | custom-call | tf_op jit(solution)/shard_map/own_part/pallas_call | solution.py:1004
  51.9 2.1 %collective-permute-done.9.refs_4_ = f32[162,128]{1,0:T(8,128)S(1)} collective-permute-done((f32[162,128]{1,0:T(8,128)S(1)}, f32[162,128]{1,0:T(8,128)S(1)}, u32[]{:S(2)}, u32[]{:S(2)}) %collective-permute-start.9) | collective-permute-done | bytes 82976 | tf_op jit(solution)/shard_map/halo_back/ppermute | solution.py:128
  54.0 1.0 %owner_sums.1 = (f32[3,128]{1,0:T(4,128)}, f32[128,128]{1,0:T(8,128)}) custom-call(f32[330,128]{1,0:T(8,128)S(1)} %get-tuple-element.50.refs_3_.refs_0_, f32[128,128]{1,0:T(8,128)S(1)} %get-tuple-element.92.refs_1_, f32[3,128]{1,0:T(4,128)S(1)} %get-tuple-element.93.refs_2_, f32[264,128]{1,0:T(8,128)S(1)} %pad_add_fusion.1.wide_ref.refs_3_.refs_2_, ...), custom_call_target="tpu_custom_call" | custom-call | tf_op jit(solution)/shard_map/owner_sums/pallas_call | solution.py:1016
  (15 shorter events, 0.1 us)
Async XLA Ops:
  0.6 0.7 %copy-start.12 = (s32[1,6,32]{2,0,1:T(1,128)S(1)}, s32[1,6,32]{2,0,1:T(1,128)}, u32[]{:S(2)}) copy-start(s32[1,6,32]{2,0,1:T(1,128)} %param.18) | copy-start | bytes 2308
  1.3 0.7 %copy-start.11 = (s32[1,12,8]{1,2,0:T(8,128)S(1)}, s32[1,12,8]{1,2,0:T(8,128)}, u32[]{:S(2)}) copy-start(s32[1,12,8]{1,2,0:T(8,128)} %param.19) | copy-start | bytes 1156
  2.0 0.9 %copy-start.2 = (f32[3,128]{1,0:T(4,128)S(1)}, f32[3,128]{1,0:T(4,128)}, u32[]{:S(2)}) copy-start(f32[3,128]{1,0:T(4,128)} %refs_2_.1) | copy-start | bytes 4612
  2.9 0.7 %copy-start.3 = (s32[1,8,2]{1,2,0:T(2,128)S(1)}, s32[1,8,2]{1,2,0:T(2,128)}, u32[]{:S(2)}) copy-start(s32[1,8,2]{1,2,0:T(2,128)} %param.20) | copy-start | bytes 196
  3.5 3.7 %copy-start = (s32[6144]{0:T(1024)S(1)}, s32[6144]{0:T(1024)}, u32[]{:S(2)}) copy-start(s32[6144]{0:T(1024)} %param.21) | copy-start | bytes 73732
  3.5 3.7 %copy-start.1 = (s32[6144]{0:T(1024)S(1)}, s32[6144]{0:T(1024)}, u32[]{:S(2)}) copy-start(s32[6144]{0:T(1024)} %param.22) | copy-start | bytes 73732
  3.5 6.3 %copy-start.10 = (f32[8,128]{1,0:T(8,128)S(1)}, f32[8,128]{1,0:T(8,128)}, u32[]{:S(2)}) copy-start(f32[8,128]{1,0:T(8,128)} %param.26) | copy-start | bytes 12292
  4.2 5.6 %copy-start.5 = (f32[128,128]{1,0:T(8,128)S(1)}, f32[128,128]{1,0:T(8,128)}, u32[]{:S(2)}) copy-start(f32[128,128]{1,0:T(8,128)} %param.24) | copy-start | bytes 196612
  4.2 5.6 %copy-start.4 = (f32[128,128]{1,0:T(8,128)S(1)}, f32[128,128]{1,0:T(8,128)}, u32[]{:S(2)}) copy-start(f32[128,128]{1,0:T(8,128)} %param.25) | copy-start | bytes 196612
  4.2 5.6 %collective-permute-start = (f32[162,128]{1,0:T(8,128)S(1)}, f32[162,128]{1,0:T(8,128)S(1)}, u32[]{:S(2)}, u32[]{:S(2)}) collective-permute-start(f32[162,128]{1,0:T(8,128)S(1)} %get-tuple-element.51), channel_id=1, source_target_pairs={{0,1},{1,0},{2,3},{3,2},{4,5},{5,4},{6,7},{7,6},{8,9},{9,8},{10,11... | collective-permute-start | bytes 248840 | tf_op jit(solution)/shard_map/halo_z/ppermute | solution.py:128
  9.9 4.1 %copy-start.6 = (bf16[256,128]{1,0:T(8,128)(2,1)S(1)}, bf16[256,128]{1,0:T(8,128)(2,1)}, u32[]{:S(2)}) copy-start(bf16[256,128]{1,0:T(8,128)(2,1)} %param.30) | copy-start | bytes 196612
  9.9 4.1 %copy-start.7 = (bf16[128,128]{1,0:T(8,128)(2,1)S(1)}, bf16[128,128]{1,0:T(8,128)(2,1)}, u32[]{:S(2)}) copy-start(bf16[128,128]{1,0:T(8,128)(2,1)} %param.29) | copy-start | bytes 98308
  9.9 4.1 %copy-start.8 = (bf16[128,128]{1,0:T(8,128)(2,1)S(1)}, bf16[128,128]{1,0:T(8,128)(2,1)}, u32[]{:S(2)}) copy-start(bf16[128,128]{1,0:T(8,128)(2,1)} %param.28) | copy-start | bytes 98308
  9.9 4.1 %copy-start.9 = (bf16[128,128]{1,0:T(8,128)(2,1)S(1)}, bf16[128,128]{1,0:T(8,128)(2,1)}, u32[]{:S(2)}) copy-start(bf16[128,128]{1,0:T(8,128)(2,1)} %param.27) | copy-start | bytes 98308
  9.9 5.7 %collective-permute-start.1 = (f32[81,128]{1,0:T(8,128)S(1)}, f32[81,128]{1,0:T(8,128)S(1)}, u32[]{:S(2)}, u32[]{:S(2)}) collective-permute-start(f32[81,128]{1,0:T(8,128)S(1)} %get-tuple-element.58), channel_id=1, source_target_pairs={{0,6},{2,0},{4,2},{6,4},{1,7},{3,1},{5,3},{7,5},{8,14},{10,8},{12,... | collective-permute-start | bytes 124424 | tf_op jit(solution)/shard_map/halo_y/ppermute | solution.py:128
  13.9 0.7 %copy-start.13 = (bf16[128]{0:T(256)(128)(2,1)S(1)}, bf16[128]{0:T(256)(128)(2,1)}, u32[]{:S(2)}) copy-start(bf16[128]{0:T(256)(128)(2,1)} %param.31) | copy-start | bytes 772
  13.9 5.8 %collective-permute-start.2 = (f32[81,128]{1,0:T(8,128)S(1)}, f32[81,128]{1,0:T(8,128)S(1)}, u32[]{:S(2)}, u32[]{:S(2)}) collective-permute-start(f32[81,128]{1,0:T(8,128)S(1)} %get-tuple-element.59), channel_id=1, source_target_pairs={{0,2},{2,4},{4,6},{6,0},{1,3},{3,5},{5,7},{7,1},{8,10},{10,12},{12... | collective-permute-start | bytes 124424 | tf_op jit(solution)/shard_map/halo_y/ppermute | solution.py:128
  19.8 1.8 %collective-permute-start.3 = (f32[81,128]{1,0:T(8,128)S(1)}, f32[81,128]{1,0:T(8,128)S(1)}, u32[]{:S(2)}, u32[]{:S(2)}) collective-permute-start(f32[81,128]{1,0:T(8,128)S(1)} %get-tuple-element.75), channel_id=1, source_target_pairs={{0,24},{8,0},{16,8},{24,16},{1,25},{9,1},{17,9},{25,17},{2,26},{10... | collective-permute-start | bytes 124424 | tf_op jit(solution)/shard_map/halo_x/ppermute | solution.py:128
  19.8 4.0 %collective-permute-start.4 = (f32[81,128]{1,0:T(8,128)S(1)}, f32[81,128]{1,0:T(8,128)S(1)}, u32[]{:S(2)}, u32[]{:S(2)}) collective-permute-start(f32[81,128]{1,0:T(8,128)S(1)} %get-tuple-element.76), channel_id=1, source_target_pairs={{0,8},{8,16},{16,24},{24,0},{1,9},{9,17},{17,25},{25,1},{2,10},{10... | collective-permute-start | bytes 124424 | tf_op jit(solution)/shard_map/halo_x/ppermute | solution.py:128
  39.5 3.5 %collective-permute-start.5 = (f32[81,128]{1,0:T(8,128)S(1)}, f32[81,128]{1,0:T(8,128)S(1)}, u32[]{:S(2)}, u32[]{:S(2)}) collective-permute-start(f32[81,128]{1,0:T(8,128)S(1)} %get-tuple-element.87), channel_id=1, source_target_pairs={{0,8},{8,16},{16,24},{24,0},{1,9},{9,17},{17,25},{25,1},{2,10},{10... | collective-permute-start | bytes 124424 | tf_op jit(solution)/shard_map/halo_back/ppermute | solution.py:128
  39.7 3.4 %collective-permute-start.6 = (f32[81,128]{1,0:T(8,128)S(1)}, f32[81,128]{1,0:T(8,128)S(1)}, u32[]{:S(2)}, u32[]{:S(2)}) collective-permute-start(f32[81,128]{1,0:T(8,128)S(1)} %get-tuple-element.88), channel_id=1, source_target_pairs={{0,24},{8,0},{16,8},{24,16},{1,25},{9,1},{17,9},{25,17},{2,26},{10... | collective-permute-start | bytes 124424 | tf_op jit(solution)/shard_map/halo_back/ppermute | solution.py:128
  43.1 6.2 %collective-permute-start.7 = (f32[81,128]{1,0:T(8,128)S(1)}, f32[81,128]{1,0:T(8,128)S(1)}, u32[]{:S(2)}, u32[]{:S(2)}) collective-permute-start(f32[81,128]{1,0:T(8,128)S(1)} %get-tuple-element.90), channel_id=1, source_target_pairs={{0,2},{2,4},{4,6},{6,0},{1,3},{3,5},{5,7},{7,1},{8,10},{10,12},{12... | collective-permute-start | bytes 124424 | tf_op jit(solution)/shard_map/halo_back/ppermute | solution.py:128
  43.2 6.1 %collective-permute-start.8 = (f32[81,128]{1,0:T(8,128)S(1)}, f32[81,128]{1,0:T(8,128)S(1)}, u32[]{:S(2)}, u32[]{:S(2)}) collective-permute-start(f32[81,128]{1,0:T(8,128)S(1)} %get-tuple-element.91), channel_id=1, source_target_pairs={{0,6},{2,0},{4,2},{6,4},{1,7},{3,1},{5,3},{7,5},{8,14},{10,8},{12,... | collective-permute-start | bytes 124424 | tf_op jit(solution)/shard_map/halo_back/ppermute | solution.py:128
  49.3 4.7 %collective-permute-start.9 = (f32[162,128]{1,0:T(8,128)S(1)}, f32[162,128]{1,0:T(8,128)S(1)}, u32[]{:S(2)}, u32[]{:S(2)}) collective-permute-start(f32[162,128]{1,0:T(8,128)S(1)} %halo_back.3), channel_id=1, source_target_pairs={{0,1},{1,0},{2,3},{3,2},{4,5},{5,4},{6,7},{7,6},{8,9},{9,8},{10,11... | collective-permute-start | bytes 248840 | tf_op jit(solution)/shard_map/halo_back/ppermute | solution.py:128

commit v5 on v4

--- a/solution.py
+++ b/solution.py
@@ -122,10 +122,21 @@
 
     def send(self, a, messages, back=False):
         n = self.sizes[a]
-        got = []
-        for blocks, message in zip(self.groups[a], messages):
-            step = -blocks[0][a] if back else blocks[0][a]
-            got.append(lax.ppermute(message, AXES[a], [(i, (i + step) % n) for i in range(n)]))
+        steps = [-blocks[0][a] if back else blocks[0][a] for blocks in self.groups[a]]
+        if n % 2 or n == 2:
+            return [
+                lax.ppermute(message, AXES[a], [(i, (i + step) % n) for i in range(n)])
+                for step, message in zip(steps, messages)
+            ]
+        up, down = steps.index(1), steps.index(-1)
+        even = lax.axis_index(AXES[a]) % 2 == 0
+        ahead = [(i, i + 1 - 2 * (i % 2)) for i in range(n)]
+        behind = [(i, (i - 1 + 2 * (i % 2)) % n) for i in range(n)]
+        first = lax.ppermute(jnp.where(even, messages[up], messages[down]), AXES[a], ahead)
+        second = lax.ppermute(jnp.where(even, messages[down], messages[up]), AXES[a], behind)
+        got = [None, None]
+        got[up] = jnp.where(even, second, first)
+        got[down] = jnp.where(even, first, second)
         return got
 
 

time: 55.3 us -> 54.2 us (0.980)
  starting transfers between devices: 14.8 us -> 13 us
  local copies, waits for them, and re-layouts: 2.02 us -> 2.76 us
    ppermute x10 -> x2, waiting for transfers between devices: 14.5 us -> 2.28 us  [send(): lax.ppermute(message, AXES[a], [(i, (i + step) % n) for i in range(n)])]
    ppermute x0 -> x8, waiting for transfers between devices: none -> 11.9 us  [the longest x4 8.17 us: send(): lax.ppermute(jnp.where(even, messages[down], messages[up]), AXES[a], behind)]
    ppermute x10 -> x2, starting transfers between devices: 14.8 us -> 4.2 us  [send(): lax.ppermute(message, AXES[a], [(i, (i + step) % n) for i in range(n)])]
    ppermute x0 -> x8, starting transfers between devices: none -> 8.81 us  [the longest x4 6.51 us: send(): lax.ppermute(jnp.where(even, messages[down], messages[up]), AXES[a], behind)]
    unnamed x28, local copies, waits for them, and re-layouts: 2.02 us -> 2.76 us
where the time goes in v5:
time: 54.2 us; the launch traced here: 53.9 us
  Pallas kernels  21.4 us (39%)
  waiting for transfers between devices  14.2 us (26%)
  starting transfers between devices  13 us (24%)
  local copies, waits for them, and re-layouts  2.76 us (5%)
  between operations  1.54 us (3%)
  other arithmetic  0.97 us (2%)
    pallas_call x1, Pallas kernels, local(): pl.pallas_call(lambda *refs: main_kernel(plan, *refs), out_shape=[shape(o...  15.7 us
    ppermute x4, waiting for transfers between devices, send(): lax.ppermute(jnp.where(even, messages[down], messages[up]), AXES[a], behind)  8.17 us
    ppermute x4, starting transfers between devices, send(): lax.ppermute(jnp.where(even, messages[down], messages[up]), AXES[a], behind)  6.51 us
    ppermute x2, starting transfers between devices, send(): lax.ppermute(message, AXES[a], [(i, (i + step) % n) for i in range(n)])  4.2 us
    ppermute x4, waiting for transfers between devices, send(): lax.ppermute(jnp.where(even, messages[up], messages[down]), AXES[a], ahead)  3.77 us
    unnamed x28, local copies, waits for them, and re-layouts  2.76 us
    pallas_call x1, Pallas kernels, local(): pl.pallas_call(lambda *refs: sort_kernel(own, *refs), out_shape=[shape(n_...  2.55 us
    ppermute x4, starting transfers between devices, send(): lax.ppermute(jnp.where(even, messages[up], messages[down]), AXES[a], ahead)  2.3 us
  transfers between devices with their start and end apart: 10, of which 7 were waited for; matrix products, arithmetic and copies ran while one was open for 0% of the time, Pallas kernels for 7%

profile of v5, /device:TPU:0, one launch (start us, length us, event | category | flops | bytes accessed | tf_op | source)
XLA Modules:
  0.0 53.9 jit_solution(2723134744619398074)
XLA Ops:
  0.6 0.0 copy-start.12
  1.3 0.0 copy-start.11
  1.3 0.0 copy-done.12
  1.3 0.7 %copy-done.11 = s32[1,12,8]{1,2,0:T(8,128)S(1)} copy-done((s32[1,12,8]{1,2,0:T(8,128)S(1)}, s32[1,12,8]{1,2,0:T(8,128)}, u32[]{:S(2)}) %copy-start.11) | copy-done | bytes 408
  2.0 0.0 copy-start.2
  2.0 0.9 %pad_add_fusion.2.refs_0_.rows_ref = f32[152,128]{1,0:T(8,128)S(1)} fusion(f32[1,1]{1,0:T(1,128)} %bitcast.3, f32[8,12]{1,0:T(8,128)S(1)} %convert_bitcast_fusion, f32[6,32]{1,0:T(8,128)S(1)} %fusion, f32[128,128]{1,0:T(8,128)} %param.17), kind=kLoop, calls=%fused_computation.2 | loop fusion | flops 58368 | bytes 144516 | tf_op jit(solution)/shard_map/prep/add | solution.py:863
  2.9 0.0 copy-done.2
  2.9 0.7 %copy-done.3 = s32[1,8,2]{1,2,0:T(2,128)S(1)} copy-done((s32[1,8,2]{1,2,0:T(2,128)S(1)}, s32[1,8,2]{1,2,0:T(2,128)}, u32[]{:S(2)}) %copy-start.3) | copy-done | bytes 88
  3.5 0.7 %prep.1 = (f32[162,128]{1,0:T(8,128)S(1)}, f32[168,128]{1,0:T(8,128)S(1)}, f32[330,128]{1,0:T(8,128)S(1)}) custom-call(f32[152,128]{1,0:T(8,128)S(1)} %pad_add_fusion.2.refs_0_.rows_ref, f32[3,128]{1,0:T(4,128)S(1)} %copy-done.2, s32[1,2,8]{2,1,0:T(2,128)S(1)} %bitcast.14), custom_call_target="tpu_custom_call" | custom-call | tf_op jit(solution)/shard_map/prep/pallas_call | solution.py:904
  4.2 3.0 %collective-permute-start = (f32[162,128]{1,0:T(8,128)S(1)}, f32[162,128]{1,0:T(8,128)S(1)}, u32[]{:S(2)}, u32[]{:S(2)}) collective-permute-start(f32[162,128]{1,0:T(8,128)S(1)} %get-tuple-element.51), channel_id=1, source_target_pairs={{0,1},{1,0},{2,3},{3,2},{4,5},{5,4},{6,7},{7,6},{8,9},{9,8},{10,11... | collective-permute-start | bytes 248840 | tf_op jit(solution)/shard_map/halo_z/ppermute | solution.py:128
  7.2 0.7 %copy-done.1 = s32[6144]{0:T(1024)S(1)} copy-done((s32[6144]{0:T(1024)S(1)}, s32[6144]{0:T(1024)}, u32[]{:S(2)}) %copy-start.1) | copy-done | bytes 24600
  8.0 0.0 copy-done
  8.0 2.5 %group_edges.1 = (s32[2,24,128]{2,1,0:T(8,128)S(1)}, s32[2,128]{1,0:T(2,128)S(1)}) custom-call(f32[152,128]{1,0:T(8,128)S(1)} %pad_add_fusion.2.refs_0_.rows_ref, s32[48,128]{1,0:T(8,128)S(1)} %bitcast.12, s32[48,128]{1,0:T(8,128)S(1)} %bitcast.13), custom_call_target="tpu_custom_call" | custom-call | tf_op jit(solution)/shard_map/group_edges/pallas_call | solution.py:921
  10.5 0.0 copy-done.5
  10.5 0.0 copy-done.4
  10.5 0.0 copy-done.10
  10.6 0.0 collective-permute-done.refs_1_.refs_3_.refs_8_
  10.6 0.0 copy-start.6
  10.6 0.0 copy-start.7
  10.6 0.0 copy-start.8
  10.6 0.0 copy-start.9
  10.7 3.7 %collective-permute-start.2 = (f32[81,128]{1,0:T(8,128)S(1)}, f32[81,128]{1,0:T(8,128)S(1)}, u32[]{:S(2)}, u32[]{:S(2)}) collective-permute-start(f32[81,128]{1,0:T(8,128)S(1)} %get-tuple-element.111), channel_id=1, source_target_pairs={{0,6},{2,4},{4,2},{6,0},{1,7},{3,5},{5,3},{7,1},{8,14},{10,12},{12... | collective-permute-start | bytes 124424 | tf_op jit(solution)/shard_map/halo_y/ppermute | solution.py:136
  14.3 0.0 collective-permute-start.1
  14.3 0.0 copy-done.6
  14.3 0.0 copy-done.7
  14.3 0.0 copy-done.8
  14.4 0.0 copy-done.9
  14.4 0.6 %copy-done.13 = bf16[128]{0:T(256)(128)(2,1)S(1)} copy-done((bf16[128]{0:T(256)(128)(2,1)S(1)}, bf16[128]{0:T(256)(128)(2,1)}, u32[]{:S(2)}) %copy-start.13) | copy-done | bytes 280
  15.0 0.3 weights.1
  15.3 1.3 %collective-permute-done.2 = f32[81,128]{1,0:T(8,128)S(1)} collective-permute-done((f32[81,128]{1,0:T(8,128)S(1)}, f32[81,128]{1,0:T(8,128)S(1)}, u32[]{:S(2)}, u32[]{:S(2)}) %collective-permute-start.2) | collective-permute-done | bytes 41504 | tf_op jit(solution)/shard_map/halo_y/ppermute | solution.py:136
  16.6 1.8 %collective-permute-done.1 = f32[81,128]{1,0:T(8,128)S(1)} collective-permute-done((f32[81,128]{1,0:T(8,128)S(1)}, f32[81,128]{1,0:T(8,128)S(1)}, u32[]{:S(2)}, u32[]{:S(2)}) %collective-permute-start.1) | collective-permute-done | bytes 41504 | tf_op jit(solution)/shard_map/halo_y/ppermute | solution.py:135
  18.4 0.1 collective-permute-start.4
  18.5 1.6 %collective-permute-start.3 = (f32[81,128]{1,0:T(8,128)S(1)}, f32[81,128]{1,0:T(8,128)S(1)}, u32[]{:S(2)}, u32[]{:S(2)}) collective-permute-start(f32[81,128]{1,0:T(8,128)S(1)} %get-tuple-element.108), channel_id=1, source_target_pairs={{0,8},{8,0},{16,24},{24,16},{1,9},{9,1},{17,25},{25,17},{2,10},{10... | collective-permute-start | bytes 124424 | tf_op jit(solution)/shard_map/halo_x/ppermute | solution.py:135
  20.1 2.2 %collective-permute-done.4 = f32[81,128]{1,0:T(8,128)S(1)} collective-permute-done((f32[81,128]{1,0:T(8,128)S(1)}, f32[81,128]{1,0:T(8,128)S(1)}, u32[]{:S(2)}, u32[]{:S(2)}) %collective-permute-start.4) | collective-permute-done | bytes 41504 | tf_op jit(solution)/shard_map/halo_x/ppermute | solution.py:136
  22.4 0.0 collective-permute-done.3
  22.4 15.7 %layer.1 = (f32[144,128]{1,0:T(8,128)S(1)}, f32[256,256]{1,0:T(8,128)S(1)}, f32[81,128]{1,0:T(8,128)S(1)}, f32[81,128]{1,0:T(8,128)S(1)}, f32[168,128]{1,0:T(8,128)S(1)}) custom-call(s32[2,128]{1,0:T(2,128)S(1)} %get-tuple-element.54.refs_0_, s32[2,24,128]{2,1,0:T(8,128)S(1)} %get-tuple-element.55.refs_1_, f32[3,128]{1,0:T(4,128)S(1)} %copy-done.2, ...), custom_call_target="tpu_custom_call" | custom-call | tf_op jit(solution)/shard_map/layer/pallas_call | solution.py:997
  38.1 0.2 collective-permute-start.6
  38.3 1.1 %collective-permute-start.5 = (f32[81,128]{1,0:T(8,128)S(1)}, f32[81,128]{1,0:T(8,128)S(1)}, u32[]{:S(2)}, u32[]{:S(2)}) collective-permute-start(f32[81,128]{1,0:T(8,128)S(1)} %get-tuple-element.104), channel_id=1, source_target_pairs={{0,24},{8,16},{16,8},{24,0},{1,25},{9,17},{17,9},{25,1},{2,26},{10... | collective-permute-start | bytes 124424 | tf_op jit(solution)/shard_map/halo_back/ppermute | solution.py:136
  39.5 0.0 collective-permute-done.6
  39.5 2.4 %collective-permute-done.5 = f32[81,128]{1,0:T(8,128)S(1)} collective-permute-done((f32[81,128]{1,0:T(8,128)S(1)}, f32[81,128]{1,0:T(8,128)S(1)}, u32[]{:S(2)}, u32[]{:S(2)}) %collective-permute-start.5) | collective-permute-done | bytes 41504 | tf_op jit(solution)/shard_map/halo_back/ppermute | solution.py:136
  41.9 0.5 collective-permute-start.8
  42.4 1.6 %collective-permute-start.7 = (f32[81,128]{1,0:T(8,128)S(1)}, f32[81,128]{1,0:T(8,128)S(1)}, u32[]{:S(2)}, u32[]{:S(2)}) collective-permute-start(f32[81,128]{1,0:T(8,128)S(1)} %get-tuple-element.100), channel_id=1, source_target_pairs={{0,6},{2,4},{4,2},{6,0},{1,7},{3,5},{5,3},{7,1},{8,14},{10,12},{12... | collective-permute-start | bytes 124424 | tf_op jit(solution)/shard_map/halo_back/ppermute | solution.py:136
  44.0 2.0 %collective-permute-done.8 = f32[81,128]{1,0:T(8,128)S(1)} collective-permute-done((f32[81,128]{1,0:T(8,128)S(1)}, f32[81,128]{1,0:T(8,128)S(1)}, u32[]{:S(2)}, u32[]{:S(2)}) %collective-permute-start.8) | collective-permute-done | bytes 41504 | tf_op jit(solution)/shard_map/halo_back/ppermute | solution.py:135
  46.0 2.3 %collective-permute-done.7 = f32[81,128]{1,0:T(8,128)S(1)} collective-permute-done((f32[81,128]{1,0:T(8,128)S(1)}, f32[81,128]{1,0:T(8,128)S(1)}, u32[]{:S(2)}, u32[]{:S(2)}) %collective-permute-start.7) | collective-permute-done | bytes 41504 | tf_op jit(solution)/shard_map/halo_back/ppermute | solution.py:136
  48.3 1.2 %collective-permute-start.9 = (f32[162,128]{1,0:T(8,128)S(1)}, f32[162,128]{1,0:T(8,128)S(1)}, u32[]{:S(2)}, u32[]{:S(2)}) collective-permute-start(f32[162,128]{1,0:T(8,128)S(1)} %halo_back.3), channel_id=1, source_target_pairs={{0,1},{1,0},{2,3},{3,2},{4,5},{5,4},{6,7},{7,6},{8,9},{9,8},{10,11... | collective-permute-start | bytes 248840 | tf_op jit(solution)/shard_map/halo_back/ppermute | solution.py:128
  49.5 1.1 %own_part.1 = (f32[1,128]{1,0:T(1,128)}, f32[128,128]{1,0:T(8,128)S(1)}, f32[3,128]{1,0:T(4,128)S(1)}) custom-call(f32[144,128]{1,0:T(8,128)S(1)} %get-tuple-element.85.refs_0_, f32[256,256]{1,0:T(8,128)S(1)} %get-tuple-element.86.refs_1_, f32[264,128]{1,0:T(8,128)S(1)} %pad_add_fusion.1.wide_ref.refs_3_.refs_2_, ...), custom_call_target="tpu_custom_call" | custom-call | tf_op jit(solution)/shard_map/own_part/pallas_call | solution.py:1015
  50.6 2.3 %collective-permute-done.9.refs_4_ = f32[162,128]{1,0:T(8,128)S(1)} collective-permute-done((f32[162,128]{1,0:T(8,128)S(1)}, f32[162,128]{1,0:T(8,128)S(1)}, u32[]{:S(2)}, u32[]{:S(2)}) %collective-permute-start.9) | collective-permute-done | bytes 82976 | tf_op jit(solution)/shard_map/halo_back/ppermute | solution.py:128
  52.9 1.0 %owner_sums.1 = (f32[3,128]{1,0:T(4,128)}, f32[128,128]{1,0:T(8,128)}) custom-call(f32[330,128]{1,0:T(8,128)S(1)} %get-tuple-element.50.refs_3_.refs_0_, f32[128,128]{1,0:T(8,128)S(1)} %get-tuple-element.92.refs_1_, f32[3,128]{1,0:T(4,128)S(1)} %get-tuple-element.93.refs_2_, f32[264,128]{1,0:T(8,128)S(1)} %pad_add_fusion.1.wide_ref.refs_3_.refs_2_, ...), custom_call_target="tpu_custom_call" | custom-call | tf_op jit(solution)/shard_map/owner_sums/pallas_call | solution.py:1027
  (23 shorter events, 0.2 us)
Async XLA Ops:
  0.6 0.7 %copy-start.12 = (s32[1,6,32]{2,0,1:T(1,128)S(1)}, s32[1,6,32]{2,0,1:T(1,128)}, u32[]{:S(2)}) copy-start(s32[1,6,32]{2,0,1:T(1,128)} %param.18) | copy-start | bytes 2308
  1.3 0.7 %copy-start.11 = (s32[1,12,8]{1,2,0:T(8,128)S(1)}, s32[1,12,8]{1,2,0:T(8,128)}, u32[]{:S(2)}) copy-start(s32[1,12,8]{1,2,0:T(8,128)} %param.19) | copy-start | bytes 1156
  2.0 0.9 %copy-start.2 = (f32[3,128]{1,0:T(4,128)S(1)}, f32[3,128]{1,0:T(4,128)}, u32[]{:S(2)}) copy-start(f32[3,128]{1,0:T(4,128)} %refs_2_.1) | copy-start | bytes 4612
  2.9 0.7 %copy-start.3 = (s32[1,8,2]{1,2,0:T(2,128)S(1)}, s32[1,8,2]{1,2,0:T(2,128)}, u32[]{:S(2)}) copy-start(s32[1,8,2]{1,2,0:T(2,128)} %param.20) | copy-start | bytes 196
  3.5 7.0 %copy-start.5 = (f32[128,128]{1,0:T(8,128)S(1)}, f32[128,128]{1,0:T(8,128)}, u32[]{:S(2)}) copy-start(f32[128,128]{1,0:T(8,128)} %param.24) | copy-start | bytes 196612
  4.2 6.4 %collective-permute-start = (f32[162,128]{1,0:T(8,128)S(1)}, f32[162,128]{1,0:T(8,128)S(1)}, u32[]{:S(2)}, u32[]{:S(2)}) collective-permute-start(f32[162,128]{1,0:T(8,128)S(1)} %get-tuple-element.51), channel_id=1, source_target_pairs={{0,1},{1,0},{2,3},{3,2},{4,5},{5,4},{6,7},{7,6},{8,9},{9,8},{10,11... | collective-permute-start | bytes 248840 | tf_op jit(solution)/shard_map/halo_z/ppermute | solution.py:128
  7.2 0.7 %copy-start.1 = (s32[6144]{0:T(1024)S(1)}, s32[6144]{0:T(1024)}, u32[]{:S(2)}) copy-start(s32[6144]{0:T(1024)} %param.22) | copy-start | bytes 73732
  7.2 0.8 %copy-start = (s32[6144]{0:T(1024)S(1)}, s32[6144]{0:T(1024)}, u32[]{:S(2)}) copy-start(s32[6144]{0:T(1024)} %param.21) | copy-start | bytes 73732
  7.2 3.3 %copy-start.4 = (f32[128,128]{1,0:T(8,128)S(1)}, f32[128,128]{1,0:T(8,128)}, u32[]{:S(2)}) copy-start(f32[128,128]{1,0:T(8,128)} %param.25) | copy-start | bytes 196612
  8.0 2.6 %copy-start.10 = (f32[8,128]{1,0:T(8,128)S(1)}, f32[8,128]{1,0:T(8,128)}, u32[]{:S(2)}) copy-start(f32[8,128]{1,0:T(8,128)} %param.26) | copy-start | bytes 12292
  10.6 3.7 %copy-start.6 = (bf16[256,128]{1,0:T(8,128)(2,1)S(1)}, bf16[256,128]{1,0:T(8,128)(2,1)}, u32[]{:S(2)}) copy-start(bf16[256,128]{1,0:T(8,128)(2,1)} %param.30) | copy-start | bytes 196612
  10.6 3.7 %copy-start.7 = (bf16[128,128]{1,0:T(8,128)(2,1)S(1)}, bf16[128,128]{1,0:T(8,128)(2,1)}, u32[]{:S(2)}) copy-start(bf16[128,128]{1,0:T(8,128)(2,1)} %param.29) | copy-start | bytes 98308
  10.6 3.7 %copy-start.8 = (bf16[128,128]{1,0:T(8,128)(2,1)S(1)}, bf16[128,128]{1,0:T(8,128)(2,1)}, u32[]{:S(2)}) copy-start(bf16[128,128]{1,0:T(8,128)(2,1)} %param.28) | copy-start | bytes 98308
  10.6 3.7 %copy-start.9 = (bf16[128,128]{1,0:T(8,128)(2,1)S(1)}, bf16[128,128]{1,0:T(8,128)(2,1)}, u32[]{:S(2)}) copy-start(bf16[128,128]{1,0:T(8,128)(2,1)} %param.27) | copy-start | bytes 98308
  10.7 5.9 %collective-permute-start.2 = (f32[81,128]{1,0:T(8,128)S(1)}, f32[81,128]{1,0:T(8,128)S(1)}, u32[]{:S(2)}, u32[]{:S(2)}) collective-permute-start(f32[81,128]{1,0:T(8,128)S(1)} %get-tuple-element.111), channel_id=1, source_target_pairs={{0,6},{2,4},{4,2},{6,0},{1,7},{3,5},{5,3},{7,1},{8,14},{10,12},{12... | collective-permute-start | bytes 124424 | tf_op jit(solution)/shard_map/halo_y/ppermute | solution.py:136
  14.3 0.7 %copy-start.13 = (bf16[128]{0:T(256)(128)(2,1)S(1)}, bf16[128]{0:T(256)(128)(2,1)}, u32[]{:S(2)}) copy-start(bf16[128]{0:T(256)(128)(2,1)} %param.31) | copy-start | bytes 772
  14.3 4.0 %collective-permute-start.1 = (f32[81,128]{1,0:T(8,128)S(1)}, f32[81,128]{1,0:T(8,128)S(1)}, u32[]{:S(2)}, u32[]{:S(2)}) collective-permute-start(f32[81,128]{1,0:T(8,128)S(1)} %get-tuple-element.112), channel_id=1, source_target_pairs={{0,2},{2,0},{4,6},{6,4},{1,3},{3,1},{5,7},{7,5},{8,10},{10,8},{12,... | collective-permute-start | bytes 124424 | tf_op jit(solution)/shard_map/halo_y/ppermute | solution.py:135
  18.4 3.9 %collective-permute-start.4 = (f32[81,128]{1,0:T(8,128)S(1)}, f32[81,128]{1,0:T(8,128)S(1)}, u32[]{:S(2)}, u32[]{:S(2)}) collective-permute-start(f32[81,128]{1,0:T(8,128)S(1)} %get-tuple-element.107), channel_id=1, source_target_pairs={{0,24},{8,16},{16,8},{24,0},{1,25},{9,17},{17,9},{25,1},{2,26},{10... | collective-permute-start | bytes 124424 | tf_op jit(solution)/shard_map/halo_x/ppermute | solution.py:136
  18.5 3.9 %collective-permute-start.3 = (f32[81,128]{1,0:T(8,128)S(1)}, f32[81,128]{1,0:T(8,128)S(1)}, u32[]{:S(2)}, u32[]{:S(2)}) collective-permute-start(f32[81,128]{1,0:T(8,128)S(1)} %get-tuple-element.108), channel_id=1, source_target_pairs={{0,8},{8,0},{16,24},{24,16},{1,9},{9,1},{17,25},{25,17},{2,10},{10... | collective-permute-start | bytes 124424 | tf_op jit(solution)/shard_map/halo_x/ppermute | solution.py:135
  38.1 1.3 %collective-permute-start.6 = (f32[81,128]{1,0:T(8,128)S(1)}, f32[81,128]{1,0:T(8,128)S(1)}, u32[]{:S(2)}, u32[]{:S(2)}) collective-permute-start(f32[81,128]{1,0:T(8,128)S(1)} %get-tuple-element.103), channel_id=1, source_target_pairs={{0,8},{8,0},{16,24},{24,16},{1,9},{9,1},{17,25},{25,17},{2,10},{10... | collective-permute-start | bytes 124424 | tf_op jit(solution)/shard_map/halo_back/ppermute | solution.py:135
  38.3 3.5 %collective-permute-start.5 = (f32[81,128]{1,0:T(8,128)S(1)}, f32[81,128]{1,0:T(8,128)S(1)}, u32[]{:S(2)}, u32[]{:S(2)}) collective-permute-start(f32[81,128]{1,0:T(8,128)S(1)} %get-tuple-element.104), channel_id=1, source_target_pairs={{0,24},{8,16},{16,8},{24,0},{1,25},{9,17},{17,9},{25,1},{2,26},{10... | collective-permute-start | bytes 124424 | tf_op jit(solution)/shard_map/halo_back/ppermute | solution.py:136
  41.9 4.1 %collective-permute-start.8 = (f32[81,128]{1,0:T(8,128)S(1)}, f32[81,128]{1,0:T(8,128)S(1)}, u32[]{:S(2)}, u32[]{:S(2)}) collective-permute-start(f32[81,128]{1,0:T(8,128)S(1)} %get-tuple-element.99), channel_id=1, source_target_pairs={{0,2},{2,0},{4,6},{6,4},{1,3},{3,1},{5,7},{7,5},{8,10},{10,8},{12,... | collective-permute-start | bytes 124424 | tf_op jit(solution)/shard_map/halo_back/ppermute | solution.py:135
  42.4 5.9 %collective-permute-start.7 = (f32[81,128]{1,0:T(8,128)S(1)}, f32[81,128]{1,0:T(8,128)S(1)}, u32[]{:S(2)}, u32[]{:S(2)}) collective-permute-start(f32[81,128]{1,0:T(8,128)S(1)} %get-tuple-element.100), channel_id=1, source_target_pairs={{0,6},{2,4},{4,2},{6,0},{1,7},{3,5},{5,3},{7,1},{8,14},{10,12},{12... | collective-permute-start | bytes 124424 | tf_op jit(solution)/shard_map/halo_back/ppermute | solution.py:136
  48.3 4.6 %collective-permute-start.9 = (f32[162,128]{1,0:T(8,128)S(1)}, f32[162,128]{1,0:T(8,128)S(1)}, u32[]{:S(2)}, u32[]{:S(2)}) collective-permute-start(f32[162,128]{1,0:T(8,128)S(1)} %halo_back.3), channel_id=1, source_target_pairs={{0,1},{1,0},{2,3},{3,2},{4,5},{5,4},{6,7},{7,6},{8,9},{9,8},{10,11... | collective-permute-start | bytes 248840 | tf_op jit(solution)/shard_map/halo_back/ppermute | solution.py:128

commit v6 on v5

--- a/solution.py
+++ b/solution.py
@@ -11,7 +11,7 @@
 BF16 = jnp.bfloat16
 HIGH = lax.Precision.HIGHEST
 AXES = ("gx", "gy", "gz")
-CHUNK = 3072
+CHUNK = 2048
 SUB = 256
 WIN = 16
 OTHER_BITS = 9
@@ -72,6 +72,7 @@
         self.widths = widths
         self.sizes = sizes
         self.groups = [self.group(a) for a in range(3)]
+        self.even = [lax.axis_index(axis) % 2 == 0 for axis in AXES]
         self.own_rest = [off for off in OFFSETS if off[2] == 0]
         self.held_rest = [off for off in OFFSETS if off[0] == 0]
 
@@ -129,7 +130,7 @@
                 for step, message in zip(steps, messages)
             ]
         up, down = steps.index(1), steps.index(-1)
-        even = lax.axis_index(AXES[a]) % 2 == 0
+        even = self.even[a]
         ahead = [(i, i + 1 - 2 * (i % 2)) for i in range(n)]
         behind = [(i, (i - 1 + 2 * (i % 2)) % n) for i in range(n)]
         first = lax.ppermute(jnp.where(even, messages[up], messages[down]), AXES[a], ahead)
@@ -171,19 +172,19 @@
     return out[:, 0 : x.shape[1]] + out[:, x.shape[1] :]
 
 
-def prep_kernel(plan, rows_ref, pos_ref, corner_ref, *outs):
+def prep_kernel(plan, rows_ref, pos_ref, face_ref, *outs):
     n_z = len(plan.groups[2])
     sends, rest_ref, sel_ref, turn_ref = outs[:n_z], outs[n_z], outs[n_z + 1], outs[n_z + 2]
     own = sel_ref.shape[1]
     lane = lax.broadcasted_iota(jnp.int32, (1, own), 1).astype(F32)
-    n_faces = len(CLASSES[0])
     turn_ref[...] = jnp.zeros_like(turn_ref)
-    turn_ref[0:n_faces, :] = rows_ref[own : own + n_faces, :]
-    columns = [
-        turn_ref[...].T,
-        rows_ref[own + 8 : own + 8 + plan.widths[1], :],
-        corner_ref[0].astype(F32),
-    ]
+    for key in range(face_ref.shape[0]):
+        turn_ref[key : key + 1, 0 : face_ref.shape[2]] = face_ref[key].astype(F32)
+    columns = [turn_ref[...].T]
+    at = own
+    for width in plan.widths[1:]:
+        columns.append(rows_ref[at : at + width, :])
+        at += -(-width // 8) * 8
     sel_ref[...] = jnp.zeros_like(sel_ref)
     messages = plan.groups[2] + [plan.own_rest]
     at = 0
@@ -696,14 +697,14 @@
             dew = dot_tn(d_win, a)
             here = lanes_of(s, 1)
             pair = jnp.concatenate([dt_ref[k, :, here], ew_ref[k, :, here]], axis=0)
-            prods = dot_nn(jnp.concatenate([e_win, d_win], axis=1), pair)
+            prods = dot_nn(jnp.concatenate([e_win, d_win], axis=1)[WIN:], pair)
             hot = a[0:WIN].astype(F32)
             if fresh:
                 big_ref[:, part(j)] = dew
             else:
                 big_ref[:, part(j)] += dew
             for m in range(1, 9):
-                row = jnp.sum(prods[m * WIN : (m + 1) * WIN] * hot, axis=0, keepdims=True)
+                row = jnp.sum(prods[(m - 1) * WIN : m * WIN] * hot, axis=0, keepdims=True)
                 for i in range(sub_rows):
                     at = j * sub_rows + i
                     piece = row[:, i * LANES : (i + 1) * LANES]
@@ -855,13 +856,13 @@
     tile = 32 // dtype.itemsize
     starts = [0]
     for x in arrays:
-        starts.append(starts[-1] + -(-x.shape[0] // tile) * tile)
+        starts.append(starts[-1] + -(-x.shape[1] // tile) * tile)
     total = None
     for x, at in zip(arrays, starts):
-        below = starts[-1] - at - x.shape[0]
-        part = jnp.pad(x.astype(dtype), ((at, below), (0, LANES - x.shape[1])))
+        below = starts[-1] - at - x.shape[1]
+        part = jnp.pad(x.astype(dtype), ((0, 0), (at, below), (0, LANES - x.shape[2])))
         total = part if total is None else total + part
-    return total
+    return total[0]
 
 
 def local(
@@ -898,8 +899,12 @@
     n_chunks = edges_up // CHUNK
 
     with jax.named_scope("prep"):
+        atom_features, plan.even = lax.optimization_barrier((atom_features, plan.even))
         rows = stack(
-            atom_features, send_face[0], jnp.transpose(send_edge[0]), edge_count.reshape(1, 1)
+            atom_features[None],
+            jnp.transpose(send_edge, (0, 2, 1)),
+            jnp.transpose(send_corner, (0, 2, 1)),
+            edge_count.reshape(1, 1, 1),
         )
         *sends, own_rows, sel = pl.pallas_call(
             lambda *refs: prep_kernel(plan, *refs),
@@ -909,7 +914,7 @@
             out_specs=[VMEM] * (len(plan.groups[2]) + 2),
             scratch_shapes=[pltpu.VMEM((LANES, LANES), F32)],
             compiler_params=PARAMS,
-        )(rows, positions, jnp.transpose(send_corner, (0, 2, 1)))
+        )(rows, positions, jnp.transpose(send_face, (1, 0, 2)))
 
     came = {}
     with jax.named_scope("halo_z"):
@@ -941,8 +946,10 @@
         came[1] = plan.send(1, glue(plan, 1, (2,), plan.own_rest, own_rows, came))
 
     with jax.named_scope("weights"):
-        wide = stack(w_proj_a, w_proj_b, w_radial)
-        narrow = stack(w_first, w_env, w_value, w_second, w_out[None, :])
+        wide = stack(w_proj_a[None], w_proj_b[None], w_radial[None])
+        narrow = stack(
+            w_first[None], w_env[None], w_value[None], w_second[None], w_out[None, None, :]
+        )
         half, *weights = pl.pallas_call(
             weight_kernel,
             out_shape=[

time: 54.2 us -> 53.7 us (level)
  waiting for transfers between devices: 14.2 us -> 15.9 us
  starting transfers between devices: 13 us -> 11.6 us
  local copies, waits for them, and re-layouts: 2.76 us -> 1.36 us
    ppermute x4, waiting for transfers between devices: 3.77 us -> 6.16 us  [send(): lax.ppermute(jnp.where(even, messages[up], messages[down]), AXES[a], ahead)]
    ppermute x4, starting transfers between devices: 6.51 us -> 4.63 us  [send(): lax.ppermute(jnp.where(even, messages[down], messages[up]), AXES[a], behind)]
    unnamed x28 -> x26, local copies, waits for them, and re-layouts: 2.76 us -> 1.36 us
    convert_element_type x2, other arithmetic: 0.01 us -> 1.37 us  [stack(): x.astype(dtype)]
    add x3 -> x0, other arithmetic: 0.88 us -> none  [stack(): total = part if total is None else total + part]
    ppermute x2, starting transfers between devices: 4.2 us -> 4.77 us  [send(): lax.ppermute(message, AXES[a], [(i, (i + step) % n) for i in range(n)])]
    ppermute x2, waiting for transfers between devices: 2.28 us -> 1.7 us  [send(): lax.ppermute(message, AXES[a], [(i, (i + step) % n) for i in range(n)])]
  transfers between devices with their start and end apart: 10 -> 10, of which waited for: 7 -> 8; matrix products, arithmetic and copies ran while one was open for 0% -> 0% of each run, Pallas kernels for 7% -> 7%
where the time goes in v6:
time: 53.7 us
  Pallas kernels  21.7 us (40%)
  waiting for transfers between devices  15.9 us (30%)
  starting transfers between devices  11.6 us (22%)
  between operations  1.58 us (3%)
  other arithmetic  1.48 us (3%)
  local copies, waits for them, and re-layouts  1.36 us (3%)
    pallas_call x1, Pallas kernels, local(): pl.pallas_call(lambda *refs: main_kernel(plan, *refs), out_shape=[shape(o...  16 us
    ppermute x4, waiting for transfers between devices, send(): lax.ppermute(jnp.where(even, messages[down], messages[up]), AXES[a], behind)  8.04 us
    ppermute x4, waiting for transfers between devices, send(): lax.ppermute(jnp.where(even, messages[up], messages[down]), AXES[a], ahead)  6.16 us
    ppermute x2, starting transfers between devices, send(): lax.ppermute(message, AXES[a], [(i, (i + step) % n) for i in range(n)])  4.77 us
    ppermute x4, starting transfers between devices, send(): lax.ppermute(jnp.where(even, messages[down], messages[up]), AXES[a], behind)  4.63 us
    pallas_call x1, Pallas kernels, local(): pl.pallas_call(lambda *refs: sort_kernel(own, *refs), out_shape=[shape(n_...  2.55 us
    ppermute x4, starting transfers between devices, send(): lax.ppermute(jnp.where(even, messages[up], messages[down]), AXES[a], ahead)  2.23 us
    ppermute x2, waiting for transfers between devices, send(): lax.ppermute(message, AXES[a], [(i, (i + step) % n) for i in range(n)])  1.7 us
  transfers between devices with their start and end apart: 10, of which 8 were waited for; matrix products, arithmetic and copies ran while one was open for 0% of the time, Pallas kernels for 7%

profile of v6, /device:TPU:0, one launch (start us, length us, event | category | flops | bytes accessed | tf_op | source)
XLA Modules:
  0.0 53.7 jit_solution(15376569373959262522)
XLA Ops:
  0.6 0.0 copy-start.4
  1.3 0.7 %convert_bitcast_fusion.1 = f32[1,2,8]{2,1,0:T(2,128)S(1)} fusion(s32[1,8,2]{1,2,0:T(2,128)} %param.20), kind=kLoop, calls=%fused_computation.20 | loop fusion | flops 16 | bytes 128 | tf_op jit(solution)/shard_map/prep/convert_element_type | solution.py:863
  2.0 0.7 %convert_bitcast_fusion = f32[1,8,12]{2,1,0:T(8,128)S(1)} fusion(s32[1,12,8]{1,2,0:T(8,128)} %param.19), kind=kLoop, calls=%fused_computation.19 | loop fusion | flops 96 | bytes 768 | tf_op jit(solution)/shard_map/prep/convert_element_type | solution.py:863
  2.7 0.0 copy-done.4
  2.7 0.0 copy-start.2
  2.7 0.0 copy-start.3
  2.7 0.7 %copy-done.2 = f32[3,128]{1,0:T(4,128)S(1)} copy-done((f32[3,128]{1,0:T(4,128)S(1)}, f32[3,128]{1,0:T(4,128)}, u32[]{:S(2)}) %copy-start.2) | copy-done | bytes 1560
  3.4 0.0 copy-done.3
  3.4 0.7 %prep.1 = (f32[162,128]{1,0:T(8,128)S(1)}, f32[168,128]{1,0:T(8,128)S(1)}, f32[330,128]{1,0:T(8,128)S(1)}) custom-call(f32[152,128]{1,0:T(8,128)S(1)} %add_bitcast_fusion.2.refs_0_.rows_ref, f32[3,128]{1,0:T(4,128)S(1)} %copy-done.2, s32[6,1,32]{2,1,0:T(1,128)S(1)} %bitcast.26), custom_call_target="tpu_custom_call" | custom-call | tf_op jit(solution)/shard_map/prep/pallas_call | solution.py:909
  4.1 3.0 %collective-permute-start = (f32[162,128]{1,0:T(8,128)S(1)}, f32[162,128]{1,0:T(8,128)S(1)}, u32[]{:S(2)}, u32[]{:S(2)}) collective-permute-start(f32[162,128]{1,0:T(8,128)S(1)} %get-tuple-element.55), channel_id=1, source_target_pairs={{0,1},{1,0},{2,3},{3,2},{4,5},{5,4},{6,7},{7,6},{8,9},{9,8},{10,11... | collective-permute-start | bytes 248840 | tf_op jit(solution)/shard_map/halo_z/ppermute | solution.py:129
  7.1 0.0 copy-done
  7.1 0.0 copy-done.1
  7.1 2.5 %group_edges.1 = (s32[3,16,128]{2,1,0:T(8,128)S(1)}, s32[2,128]{1,0:T(2,128)S(1)}) custom-call(f32[152,128]{1,0:T(8,128)S(1)} %add_bitcast_fusion.2.refs_0_.rows_ref, s32[48,128]{1,0:T(8,128)S(1)} %bitcast.24, s32[48,128]{1,0:T(8,128)S(1)} %bitcast.25), custom_call_target="tpu_custom_call" | custom-call | tf_op jit(solution)/shard_map/group_edges/pallas_call | solution.py:926
  9.7 0.0 copy-done.11
  9.7 0.0 copy-done.5
  9.7 0.0 copy-done.6
  9.7 0.0 collective-permute-done.refs_1_.refs_3_.refs_8_
  9.7 0.0 copy-start.7
  9.8 0.0 copy-start.8
  9.8 0.0 copy-start.9
  9.8 0.0 copy-start.10
  9.8 4.0 %collective-permute-start.2 = (f32[81,128]{1,0:T(8,128)S(1)}, f32[81,128]{1,0:T(8,128)S(1)}, u32[]{:S(2)}, u32[]{:S(2)}) collective-permute-start(f32[81,128]{1,0:T(8,128)S(1)} %get-tuple-element.117), channel_id=1, source_target_pairs={{0,6},{2,4},{4,2},{6,0},{1,7},{3,5},{5,3},{7,1},{8,14},{10,12},{12... | collective-permute-start | bytes 124424 | tf_op jit(solution)/shard_map/halo_y/ppermute | solution.py:137
  13.8 0.0 collective-permute-start.1
  13.8 0.0 copy-done.7
  13.8 0.0 copy-done.8
  13.9 0.0 copy-done.9
  13.9 0.0 copy-done.10
  13.9 0.6 %copy-done.12 = bf16[128]{0:T(256)(128)(2,1)S(1)} copy-done((bf16[128]{0:T(256)(128)(2,1)S(1)}, bf16[128]{0:T(256)(128)(2,1)}, u32[]{:S(2)}) %copy-start.12) | copy-done | bytes 280
  14.5 0.3 weights.1
  14.8 1.1 %collective-permute-done.2 = f32[81,128]{1,0:T(8,128)S(1)} collective-permute-done((f32[81,128]{1,0:T(8,128)S(1)}, f32[81,128]{1,0:T(8,128)S(1)}, u32[]{:S(2)}, u32[]{:S(2)}) %collective-permute-start.2) | collective-permute-done | bytes 41504 | tf_op jit(solution)/shard_map/halo_y/ppermute | solution.py:137
  16.0 1.9 %collective-permute-done.1 = f32[81,128]{1,0:T(8,128)S(1)} collective-permute-done((f32[81,128]{1,0:T(8,128)S(1)}, f32[81,128]{1,0:T(8,128)S(1)}, u32[]{:S(2)}, u32[]{:S(2)}) %collective-permute-start.1) | collective-permute-done | bytes 41504 | tf_op jit(solution)/shard_map/halo_y/ppermute | solution.py:136
  17.9 0.1 collective-permute-start.4
  18.0 1.6 %collective-permute-start.3 = (f32[81,128]{1,0:T(8,128)S(1)}, f32[81,128]{1,0:T(8,128)S(1)}, u32[]{:S(2)}, u32[]{:S(2)}) collective-permute-start(f32[81,128]{1,0:T(8,128)S(1)} %get-tuple-element.114), channel_id=1, source_target_pairs={{0,8},{8,0},{16,24},{24,16},{1,9},{9,1},{17,25},{25,17},{2,10},{10... | collective-permute-start | bytes 124424 | tf_op jit(solution)/shard_map/halo_x/ppermute | solution.py:136
  19.6 2.2 %collective-permute-done.4 = f32[81,128]{1,0:T(8,128)S(1)} collective-permute-done((f32[81,128]{1,0:T(8,128)S(1)}, f32[81,128]{1,0:T(8,128)S(1)}, u32[]{:S(2)}, u32[]{:S(2)}) %collective-permute-start.4) | collective-permute-done | bytes 41504 | tf_op jit(solution)/shard_map/halo_x/ppermute | solution.py:137
  21.9 0.0 collective-permute-done.3
  21.9 16.0 %layer.1 = (f32[144,128]{1,0:T(8,128)S(1)}, f32[256,256]{1,0:T(8,128)S(1)}, f32[81,128]{1,0:T(8,128)S(1)}, f32[81,128]{1,0:T(8,128)S(1)}, f32[168,128]{1,0:T(8,128)S(1)}) custom-call(s32[2,128]{1,0:T(2,128)S(1)} %get-tuple-element.58.refs_0_, s32[3,16,128]{2,1,0:T(8,128)S(1)} %get-tuple-element.59.refs_1_, f32[3,128]{1,0:T(4,128)S(1)} %copy-done.2, ...), custom_call_target="tpu_custom_call" | custom-call | tf_op jit(solution)/shard_map/layer/pallas_call | solution.py:1004
  37.9 0.1 collective-permute-start.6
  38.0 0.1 collective-permute-start.5
  38.1 1.1 %collective-permute-done.6 = f32[81,128]{1,0:T(8,128)S(1)} collective-permute-done((f32[81,128]{1,0:T(8,128)S(1)}, f32[81,128]{1,0:T(8,128)S(1)}, u32[]{:S(2)}, u32[]{:S(2)}) %collective-permute-start.6) | collective-permute-done | bytes 41504 | tf_op jit(solution)/shard_map/halo_back/ppermute | solution.py:136
  39.2 2.3 %collective-permute-done.5 = f32[81,128]{1,0:T(8,128)S(1)} collective-permute-done((f32[81,128]{1,0:T(8,128)S(1)}, f32[81,128]{1,0:T(8,128)S(1)}, u32[]{:S(2)}, u32[]{:S(2)}) %collective-permute-start.5) | collective-permute-done | bytes 41504 | tf_op jit(solution)/shard_map/halo_back/ppermute | solution.py:137
  41.6 0.5 %collective-permute-start.8 = (f32[81,128]{1,0:T(8,128)S(1)}, f32[81,128]{1,0:T(8,128)S(1)}, u32[]{:S(2)}, u32[]{:S(2)}) collective-permute-start(f32[81,128]{1,0:T(8,128)S(1)} %get-tuple-element.105), channel_id=1, source_target_pairs={{0,2},{2,0},{4,6},{6,4},{1,3},{3,1},{5,7},{7,5},{8,10},{10,8},{12,... | collective-permute-start | bytes 124424 | tf_op jit(solution)/shard_map/halo_back/ppermute | solution.py:136
  42.1 0.5 collective-permute-start.7
  42.6 3.1 %collective-permute-done.8 = f32[81,128]{1,0:T(8,128)S(1)} collective-permute-done((f32[81,128]{1,0:T(8,128)S(1)}, f32[81,128]{1,0:T(8,128)S(1)}, u32[]{:S(2)}, u32[]{:S(2)}) %collective-permute-start.8) | collective-permute-done | bytes 41504 | tf_op jit(solution)/shard_map/halo_back/ppermute | solution.py:136
  45.7 2.3 %collective-permute-done.7 = f32[81,128]{1,0:T(8,128)S(1)} collective-permute-done((f32[81,128]{1,0:T(8,128)S(1)}, f32[81,128]{1,0:T(8,128)S(1)}, u32[]{:S(2)}, u32[]{:S(2)}) %collective-permute-start.7) | collective-permute-done | bytes 41504 | tf_op jit(solution)/shard_map/halo_back/ppermute | solution.py:137
  48.1 1.8 %collective-permute-start.9 = (f32[162,128]{1,0:T(8,128)S(1)}, f32[162,128]{1,0:T(8,128)S(1)}, u32[]{:S(2)}, u32[]{:S(2)}) collective-permute-start(f32[162,128]{1,0:T(8,128)S(1)} %halo_back.3), channel_id=1, source_target_pairs={{0,1},{1,0},{2,3},{3,2},{4,5},{5,4},{6,7},{7,6},{8,9},{9,8},{10,11... | collective-permute-start | bytes 248840 | tf_op jit(solution)/shard_map/halo_back/ppermute | solution.py:129
  49.8 1.1 %own_part.1 = (f32[1,128]{1,0:T(1,128)}, f32[128,128]{1,0:T(8,128)S(1)}, f32[3,128]{1,0:T(4,128)S(1)}) custom-call(f32[144,128]{1,0:T(8,128)S(1)} %get-tuple-element.91.refs_0_, f32[256,256]{1,0:T(8,128)S(1)} %get-tuple-element.92.refs_1_, f32[264,128]{1,0:T(8,128)S(1)} %add_bitcast_fusion.1.wide_ref.refs_3_.refs_2_, ...), custom_call_target="tpu_custom_call" | custom-call | tf_op jit(solution)/shard_map/own_part/pallas_call | solution.py:1022
  50.9 1.7 %collective-permute-done.9.refs_4_ = f32[162,128]{1,0:T(8,128)S(1)} collective-permute-done((f32[162,128]{1,0:T(8,128)S(1)}, f32[162,128]{1,0:T(8,128)S(1)}, u32[]{:S(2)}, u32[]{:S(2)}) %collective-permute-start.9) | collective-permute-done | bytes 82976 | tf_op jit(solution)/shard_map/halo_back/ppermute | solution.py:129
  52.6 1.0 %owner_sums.1 = (f32[3,128]{1,0:T(4,128)}, f32[128,128]{1,0:T(8,128)}) custom-call(f32[330,128]{1,0:T(8,128)S(1)} %get-tuple-element.54.refs_3_.refs_0_, f32[128,128]{1,0:T(8,128)S(1)} %get-tuple-element.98.refs_1_, f32[3,128]{1,0:T(4,128)S(1)} %get-tuple-element.99.refs_2_, f32[264,128]{1,0:T(8,128)S(1)} %add_bitcast_fusion.1.wide_ref.refs_3_.refs_2_, ...), custom_call_target="tpu_custom_call" | custom-call | tf_op jit(solution)/shard_map/owner_sums/pallas_call | solution.py:1034
  (21 shorter events, 0.2 us)
Async XLA Ops:
  0.6 2.1 %copy-start.4 = (f32[128,128]{1,0:T(8,128)S(1)}, f32[128,128]{1,0:T(8,128)}, u32[]{:S(2)}) copy-start(f32[128,128]{1,0:T(8,128)} %param.17) | copy-start | bytes 196612
  2.7 0.7 %copy-start.2 = (f32[3,128]{1,0:T(4,128)S(1)}, f32[3,128]{1,0:T(4,128)}, u32[]{:S(2)}) copy-start(f32[3,128]{1,0:T(4,128)} %refs_2_.1) | copy-start | bytes 4612
  2.7 0.7 %copy-start.3 = (s32[1,6,32]{2,0,1:T(1,128)S(1)}, s32[1,6,32]{2,0,1:T(1,128)}, u32[]{:S(2)}) copy-start(s32[1,6,32]{2,0,1:T(1,128)} %param.18) | copy-start | bytes 2308
  3.4 3.7 %copy-start = (s32[6144]{0:T(1024)S(1)}, s32[6144]{0:T(1024)}, u32[]{:S(2)}) copy-start(s32[6144]{0:T(1024)} %param.21) | copy-start | bytes 73732
  3.4 3.7 %copy-start.1 = (s32[6144]{0:T(1024)S(1)}, s32[6144]{0:T(1024)}, u32[]{:S(2)}) copy-start(s32[6144]{0:T(1024)} %param.22) | copy-start | bytes 73732
  3.4 6.2 %copy-start.11 = (f32[8,128]{1,0:T(8,128)S(1)}, f32[8,128]{1,0:T(8,128)}, u32[]{:S(2)}) copy-start(f32[8,128]{1,0:T(8,128)} %param.26) | copy-start | bytes 12292
  4.1 5.6 %collective-permute-start = (f32[162,128]{1,0:T(8,128)S(1)}, f32[162,128]{1,0:T(8,128)S(1)}, u32[]{:S(2)}, u32[]{:S(2)}) collective-permute-start(f32[162,128]{1,0:T(8,128)S(1)} %get-tuple-element.55), channel_id=1, source_target_pairs={{0,1},{1,0},{2,3},{3,2},{4,5},{5,4},{6,7},{7,6},{8,9},{9,8},{10,11... | collective-permute-start | bytes 248840 | tf_op jit(solution)/shard_map/halo_z/ppermute | solution.py:129
  7.1 2.6 %copy-start.5 = (f32[128,128]{1,0:T(8,128)S(1)}, f32[128,128]{1,0:T(8,128)}, u32[]{:S(2)}) copy-start(f32[128,128]{1,0:T(8,128)} %param.25) | copy-start | bytes 196612
  7.1 2.6 %copy-start.6 = (f32[128,128]{1,0:T(8,128)S(1)}, f32[128,128]{1,0:T(8,128)}, u32[]{:S(2)}) copy-start(f32[128,128]{1,0:T(8,128)} %param.24) | copy-start | bytes 196612
  9.7 4.1 %copy-start.7 = (bf16[256,128]{1,0:T(8,128)(2,1)S(1)}, bf16[256,128]{1,0:T(8,128)(2,1)}, u32[]{:S(2)}) copy-start(bf16[256,128]{1,0:T(8,128)(2,1)} %param.30) | copy-start | bytes 196612
  9.8 4.1 %copy-start.8 = (bf16[128,128]{1,0:T(8,128)(2,1)S(1)}, bf16[128,128]{1,0:T(8,128)(2,1)}, u32[]{:S(2)}) copy-start(bf16[128,128]{1,0:T(8,128)(2,1)} %param.29) | copy-start | bytes 98308
  9.8 4.1 %copy-start.9 = (bf16[128,128]{1,0:T(8,128)(2,1)S(1)}, bf16[128,128]{1,0:T(8,128)(2,1)}, u32[]{:S(2)}) copy-start(bf16[128,128]{1,0:T(8,128)(2,1)} %param.28) | copy-start | bytes 98308
  9.8 4.1 %copy-start.10 = (bf16[128,128]{1,0:T(8,128)(2,1)S(1)}, bf16[128,128]{1,0:T(8,128)(2,1)}, u32[]{:S(2)}) copy-start(bf16[128,128]{1,0:T(8,128)(2,1)} %param.27) | copy-start | bytes 98308
  9.8 6.2 %collective-permute-start.2 = (f32[81,128]{1,0:T(8,128)S(1)}, f32[81,128]{1,0:T(8,128)S(1)}, u32[]{:S(2)}, u32[]{:S(2)}) collective-permute-start(f32[81,128]{1,0:T(8,128)S(1)} %get-tuple-element.117), channel_id=1, source_target_pairs={{0,6},{2,4},{4,2},{6,0},{1,7},{3,5},{5,3},{7,1},{8,14},{10,12},{12... | collective-permute-start | bytes 124424 | tf_op jit(solution)/shard_map/halo_y/ppermute | solution.py:137
  13.8 4.0 %collective-permute-start.1 = (f32[81,128]{1,0:T(8,128)S(1)}, f32[81,128]{1,0:T(8,128)S(1)}, u32[]{:S(2)}, u32[]{:S(2)}) collective-permute-start(f32[81,128]{1,0:T(8,128)S(1)} %get-tuple-element.118), channel_id=1, source_target_pairs={{0,2},{2,0},{4,6},{6,4},{1,3},{3,1},{5,7},{7,5},{8,10},{10,8},{12,... | collective-permute-start | bytes 124424 | tf_op jit(solution)/shard_map/halo_y/ppermute | solution.py:136
  13.8 0.7 %copy-start.12 = (bf16[128]{0:T(256)(128)(2,1)S(1)}, bf16[128]{0:T(256)(128)(2,1)}, u32[]{:S(2)}) copy-start(bf16[128]{0:T(256)(128)(2,1)} %param.31) | copy-start | bytes 772
  17.9 3.9 %collective-permute-start.4 = (f32[81,128]{1,0:T(8,128)S(1)}, f32[81,128]{1,0:T(8,128)S(1)}, u32[]{:S(2)}, u32[]{:S(2)}) collective-permute-start(f32[81,128]{1,0:T(8,128)S(1)} %get-tuple-element.113), channel_id=1, source_target_pairs={{0,24},{8,16},{16,8},{24,0},{1,25},{9,17},{17,9},{25,1},{2,26},{10... | collective-permute-start | bytes 124424 | tf_op jit(solution)/shard_map/halo_x/ppermute | solution.py:137
  18.0 3.9 %collective-permute-start.3 = (f32[81,128]{1,0:T(8,128)S(1)}, f32[81,128]{1,0:T(8,128)S(1)}, u32[]{:S(2)}, u32[]{:S(2)}) collective-permute-start(f32[81,128]{1,0:T(8,128)S(1)} %get-tuple-element.114), channel_id=1, source_target_pairs={{0,8},{8,0},{16,24},{24,16},{1,9},{9,1},{17,25},{25,17},{2,10},{10... | collective-permute-start | bytes 124424 | tf_op jit(solution)/shard_map/halo_x/ppermute | solution.py:136
  37.9 1.3 %collective-permute-start.6 = (f32[81,128]{1,0:T(8,128)S(1)}, f32[81,128]{1,0:T(8,128)S(1)}, u32[]{:S(2)}, u32[]{:S(2)}) collective-permute-start(f32[81,128]{1,0:T(8,128)S(1)} %get-tuple-element.109), channel_id=1, source_target_pairs={{0,8},{8,0},{16,24},{24,16},{1,9},{9,1},{17,25},{25,17},{2,10},{10... | collective-permute-start | bytes 124424 | tf_op jit(solution)/shard_map/halo_back/ppermute | solution.py:136
  38.0 3.5 %collective-permute-start.5 = (f32[81,128]{1,0:T(8,128)S(1)}, f32[81,128]{1,0:T(8,128)S(1)}, u32[]{:S(2)}, u32[]{:S(2)}) collective-permute-start(f32[81,128]{1,0:T(8,128)S(1)} %get-tuple-element.110), channel_id=1, source_target_pairs={{0,24},{8,16},{16,8},{24,0},{1,25},{9,17},{17,9},{25,1},{2,26},{10... | collective-permute-start | bytes 124424 | tf_op jit(solution)/shard_map/halo_back/ppermute | solution.py:137
  41.6 4.1 %collective-permute-start.8 = (f32[81,128]{1,0:T(8,128)S(1)}, f32[81,128]{1,0:T(8,128)S(1)}, u32[]{:S(2)}, u32[]{:S(2)}) collective-permute-start(f32[81,128]{1,0:T(8,128)S(1)} %get-tuple-element.105), channel_id=1, source_target_pairs={{0,2},{2,0},{4,6},{6,4},{1,3},{3,1},{5,7},{7,5},{8,10},{10,8},{12,... | collective-permute-start | bytes 124424 | tf_op jit(solution)/shard_map/halo_back/ppermute | solution.py:136
  42.1 5.9 %collective-permute-start.7 = (f32[81,128]{1,0:T(8,128)S(1)}, f32[81,128]{1,0:T(8,128)S(1)}, u32[]{:S(2)}, u32[]{:S(2)}) collective-permute-start(f32[81,128]{1,0:T(8,128)S(1)} %get-tuple-element.106), channel_id=1, source_target_pairs={{0,6},{2,4},{4,2},{6,0},{1,7},{3,5},{5,3},{7,1},{8,14},{10,12},{12... | collective-permute-start | bytes 124424 | tf_op jit(solution)/shard_map/halo_back/ppermute | solution.py:137
  48.1 4.6 %collective-permute-start.9 = (f32[162,128]{1,0:T(8,128)S(1)}, f32[162,128]{1,0:T(8,128)S(1)}, u32[]{:S(2)}, u32[]{:S(2)}) collective-permute-start(f32[162,128]{1,0:T(8,128)S(1)} %halo_back.3), channel_id=1, source_target_pairs={{0,1},{1,0},{2,3},{3,2},{4,5},{5,4},{6,7},{7,6},{8,9},{9,8},{10,11... | collective-permute-start | bytes 248840 | tf_op jit(solution)/shard_map/halo_back/ppermute | solution.py:129

commit v7 on v6

--- a/solution.py
+++ b/solution.py
@@ -11,7 +11,7 @@
 BF16 = jnp.bfloat16
 HIGH = lax.Precision.HIGHEST
 AXES = ("gx", "gy", "gz")
-CHUNK = 2048
+CHUNK = 3072
 SUB = 256
 WIN = 16
 OTHER_BITS = 9
@@ -172,7 +172,7 @@
     return out[:, 0 : x.shape[1]] + out[:, x.shape[1] :]
 
 
-def prep_kernel(plan, rows_ref, pos_ref, face_ref, *outs):
+def prep_kernel(plan, rows_ref, pos_ref, face_ref, edge_ref, corner_ref, *outs):
     n_z = len(plan.groups[2])
     sends, rest_ref, sel_ref, turn_ref = outs[:n_z], outs[n_z], outs[n_z + 1], outs[n_z + 2]
     own = sel_ref.shape[1]
@@ -180,11 +180,7 @@
     turn_ref[...] = jnp.zeros_like(turn_ref)
     for key in range(face_ref.shape[0]):
         turn_ref[key : key + 1, 0 : face_ref.shape[2]] = face_ref[key].astype(F32)
-    columns = [turn_ref[...].T]
-    at = own
-    for width in plan.widths[1:]:
-        columns.append(rows_ref[at : at + width, :])
-        at += -(-width // 8) * 8
+    columns = [turn_ref[...].T, edge_ref[0].astype(F32), corner_ref[0].astype(F32)]
     sel_ref[...] = jnp.zeros_like(sel_ref)
     messages = plan.groups[2] + [plan.own_rest]
     at = 0
@@ -345,6 +341,7 @@
     def flip(w):
         return w.astype(F32).T.astype(BF16)
 
+    w1, w2 = (0.5 * w1.astype(F32)).astype(BF16), (0.5 * w2.astype(F32)).astype(BF16)
     down = dot_nn(rad, w1.astype(F32), HIGH)
     w1_ref[0:chans, :] = w1
     w1_ref[chans:, :] = jnp.concatenate([down, jnp.zeros_like(down)], axis=0).astype(BF16)
@@ -624,10 +621,10 @@
         hots.append(jnp.concatenate([b_hi, b_lo], axis=0).astype(BF16))
         hots.append(jnp.concatenate([b_hi, jnp.zeros_like(b_hi)], axis=0).astype(BF16))
         mixed = dot_nn(table_ref[...], jnp.concatenate(hots, axis=0)).astype(BF16)
-        z1 = dot_nn(w1t_ref[...], mixed)
-        sg = 0.5 + 0.5 * jnp.tanh(0.5 * z1)
-        first = z1 * sg
-        dsilu_ref[k, :, lanes] = (sg + first * (1.0 - sg)).astype(BF16)
+        half = dot_nn(w1t_ref[...], mixed)
+        up = 1.0 + jnp.tanh(half)
+        first = half * up
+        dsilu_ref[k, :, lanes] = (up + first * (2.0 - up)).astype(BF16)
         first = first.astype(BF16)
         first_ref[k, :, lanes] = first
         both = dot_nn(wevt_ref[...], first)
@@ -657,9 +654,9 @@
         total = 0.2 * big_ref[:, 0 : n * SUB]
         value = val_ref[k, :, lanes].astype(F32)
         scalar = (value * total).astype(BF16)
-        z2 = dot_nn(w2t_ref[...], jnp.concatenate([first_ref[k, :, lanes], scalar], axis=0))
-        sg = 0.5 + 0.5 * jnp.tanh(0.5 * z2)
-        second = z2 * sg
+        half = dot_nn(w2t_ref[...], jnp.concatenate([first_ref[k, :, lanes], scalar], axis=0))
+        up = 1.0 + jnp.tanh(half)
+        second = half * up
         wcol = jnp.concatenate([wcol_ref[...]] * (n * sub_rows), axis=1)
         ee = jnp.sum(second.astype(BF16).astype(F32) * wcol, axis=0, keepdims=True)
         envv = in_lanes(plane(6, k, s, n))
@@ -668,7 +665,7 @@
         for j in range(n * sub_rows):
             live_ref[k, pl.ds(first_row + j, 1), :] = live[:, j * LANES : (j + 1) * LANES]
         energy = ee * envv
-        dz2 = ((wcol * envv) * (sg + second * (1.0 - sg))).astype(BF16)
+        dz2 = ((wcol * envv) * (up + second * (2.0 - up))).astype(BF16)
         dj = dot_nn(w2_ref[...], dz2)
         dfa_ref[k, :, lanes] = dj[0:chans].astype(BF16)
         dscalar = dj[chans:]
@@ -900,21 +897,22 @@
 
     with jax.named_scope("prep"):
         atom_features, plan.even = lax.optimization_barrier((atom_features, plan.even))
-        rows = stack(
-            atom_features[None],
-            jnp.transpose(send_edge, (0, 2, 1)),
-            jnp.transpose(send_corner, (0, 2, 1)),
-            edge_count.reshape(1, 1, 1),
-        )
+        rows = stack(atom_features[None], edge_count.reshape(1, 1, 1))
         *sends, own_rows, sel = pl.pallas_call(
             lambda *refs: prep_kernel(plan, *refs),
             out_shape=plan.shapes(2, chans)
             + [shape(plan.total(plan.own_rest), chans), shape(n_send, own)],
-            in_specs=[VMEM] * 3,
+            in_specs=[VMEM] * 5,
             out_specs=[VMEM] * (len(plan.groups[2]) + 2),
             scratch_shapes=[pltpu.VMEM((LANES, LANES), F32)],
             compiler_params=PARAMS,
-        )(rows, positions, jnp.transpose(send_face, (1, 0, 2)))
+        )(
+            rows,
+            positions,
+            jnp.transpose(send_face, (1, 0, 2)),
+            jnp.transpose(send_edge, (0, 2, 1)),
+            jnp.transpose(send_corner, (0, 2, 1)),
+        )
 
     came = {}
     with jax.named_scope("halo_z"):

time: 53.7 us -> 52.1 us (0.970)
  waiting for transfers between devices: 15.9 us -> 14.3 us
  other arithmetic: 1.48 us -> 0.11 us
  starting transfers between devices: 11.6 us -> 12.9 us
  local copies, waits for them, and re-layouts: 1.36 us -> 2.17 us
  Pallas kernels: 21.7 us -> 20.9 us
    ppermute x4, waiting for transfers between devices: 6.16 us -> 3.93 us  [send(): lax.ppermute(jnp.where(even, messages[up], messages[down]), AXES[a], ahead)]
    ppermute x4, starting transfers between devices: 4.63 us -> 6.32 us  [send(): lax.ppermute(jnp.where(even, messages[down], messages[up]), AXES[a], behind)]
    convert_element_type x2 -> x0, other arithmetic: 1.37 us -> none  [stack(): x.astype(dtype)]
    unnamed x26 -> x30, local copies, waits for them, and re-layouts: 1.36 us -> 2.17 us
    pallas_call x1, Pallas kernels: 16 us -> 15.2 us  [local(): pl.pallas_call(lambda *refs: main_kernel(plan, *refs), out_shape=[shape(o...]
  transfers between devices with their start and end apart: 10 -> 10, of which waited for: 8 -> 7; matrix products, arithmetic and copies ran while one was open for 0% -> 0% of each run, Pallas kernels for 7% -> 8%
where the time goes in v7:
time: 52.1 us; the launch traced here: 52 us
  Pallas kernels  20.9 us (40%)
  waiting for transfers between devices  14.3 us (27%)
  starting transfers between devices  12.9 us (25%)
  local copies, waits for them, and re-layouts  2.17 us (4%)
  between operations  1.58 us (3%)
    pallas_call x1, Pallas kernels, local(): pl.pallas_call(lambda *refs: main_kernel(plan, *refs), out_shape=[shape(o...  15.2 us
    ppermute x4, waiting for transfers between devices, send(): lax.ppermute(jnp.where(even, messages[down], messages[up]), AXES[a], behind)  8.18 us
    ppermute x4, starting transfers between devices, send(): lax.ppermute(jnp.where(even, messages[down], messages[up]), AXES[a], behind)  6.32 us
    ppermute x2, starting transfers between devices, send(): lax.ppermute(message, AXES[a], [(i, (i + step) % n) for i in range(n)])  4.29 us
    ppermute x4, waiting for transfers between devices, send(): lax.ppermute(jnp.where(even, messages[up], messages[down]), AXES[a], ahead)  3.93 us
    pallas_call x1, Pallas kernels, local(): pl.pallas_call(lambda *refs: sort_kernel(own, *refs), out_shape=[shape(n_...  2.55 us
    ppermute x4, starting transfers between devices, send(): lax.ppermute(jnp.where(even, messages[up], messages[down]), AXES[a], ahead)  2.31 us
    ppermute x2, waiting for transfers between devices, send(): lax.ppermute(message, AXES[a], [(i, (i + step) % n) for i in range(n)])  2.19 us
  transfers between devices with their start and end apart: 10, of which 7 were waited for; matrix products, arithmetic and copies ran while one was open for 0% of the time, Pallas kernels for 8%

profile of v7, /device:TPU:0, one launch (start us, length us, event | category | flops | bytes accessed | tf_op | source)
XLA Modules:
  0.0 52.0 jit_solution(5808874688310706671)
XLA Ops:
  0.6 0.0 copy-start.6
  1.3 0.1 copy-done.6
  1.5 0.0 copy-start.4
  1.5 0.0 copy-start.2
  1.5 0.6 %copy-done.3 = s32[1,12,8]{1,2,0:T(8,128)S(1)} copy-done((s32[1,12,8]{1,2,0:T(8,128)S(1)}, s32[1,12,8]{1,2,0:T(8,128)}, u32[]{:S(2)}) %copy-start.3) | copy-done | bytes 408
  2.2 0.0 copy-done.5
  2.2 0.0 copy-done.4
  2.2 0.0 copy-done.2
  2.2 0.7 %prep.1 = (f32[162,128]{1,0:T(8,128)S(1)}, f32[168,128]{1,0:T(8,128)S(1)}, f32[330,128]{1,0:T(8,128)S(1)}) custom-call(f32[136,128]{1,0:T(8,128)S(1)} %add_bitcast_fusion.2.refs_0_.rows_ref, f32[3,128]{1,0:T(4,128)S(1)} %copy-done.2, s32[6,1,32]{2,1,0:T(1,128)S(1)} %bitcast.25, s32[1,8,12]{2,1,0:T(8,128)S(1)} %bitcast.24, s32[1,2,8]{2,1,0:T(2,128)S(1)} %bitcast.26), custom_call_target="tpu_custom_call" | custom-call | tf_op jit(solution)/shard_map/prep/pallas_call | solution.py:901
  2.9 0.0 copy-start.7
  2.9 3.0 %collective-permute-start = (f32[162,128]{1,0:T(8,128)S(1)}, f32[162,128]{1,0:T(8,128)S(1)}, u32[]{:S(2)}, u32[]{:S(2)}) collective-permute-start(f32[162,128]{1,0:T(8,128)S(1)} %get-tuple-element.55), channel_id=1, source_target_pairs={{0,1},{1,0},{2,3},{3,2},{4,5},{5,4},{6,7},{7,6},{8,9},{9,8},{10,11... | collective-permute-start | bytes 248840 | tf_op jit(solution)/shard_map/halo_z/ppermute | solution.py:129
  5.9 0.0 copy-done
  5.9 0.0 copy-done.1
  5.9 2.5 %group_edges.1 = (s32[2,24,128]{2,1,0:T(8,128)S(1)}, s32[2,128]{1,0:T(2,128)S(1)}) custom-call(f32[136,128]{1,0:T(8,128)S(1)} %add_bitcast_fusion.2.refs_0_.rows_ref, s32[48,128]{1,0:T(8,128)S(1)} %bitcast.22, s32[48,128]{1,0:T(8,128)S(1)} %bitcast.23), custom_call_target="tpu_custom_call" | custom-call | tf_op jit(solution)/shard_map/group_edges/pallas_call | solution.py:924
  8.5 0.0 copy-start.13
  8.5 0.0 copy-done.8
  8.5 0.0 copy-done.7
  8.5 0.7 %copy-done.13 = f32[8,128]{1,0:T(8,128)S(1)} copy-done((f32[8,128]{1,0:T(8,128)S(1)}, f32[8,128]{1,0:T(8,128)}, u32[]{:S(2)}) %copy-start.13) | copy-done | bytes 4120
  9.2 0.0 collective-permute-done.refs_1_.refs_3_.refs_8_
  9.2 0.0 copy-start.9
  9.2 0.0 copy-start.10
  9.2 0.0 copy-start.11
  9.2 0.0 copy-start.12
  9.3 3.7 %collective-permute-start.2 = (f32[81,128]{1,0:T(8,128)S(1)}, f32[81,128]{1,0:T(8,128)S(1)}, u32[]{:S(2)}, u32[]{:S(2)}) collective-permute-start(f32[81,128]{1,0:T(8,128)S(1)} %get-tuple-element.117), channel_id=1, source_target_pairs={{0,6},{2,4},{4,2},{6,0},{1,7},{3,5},{5,3},{7,1},{8,14},{10,12},{12... | collective-permute-start | bytes 124424 | tf_op jit(solution)/shard_map/halo_y/ppermute | solution.py:137
  12.9 0.0 collective-permute-start.1
  12.9 0.0 copy-done.9
  12.9 0.0 copy-done.10
  13.0 0.6 %copy-done.14 = bf16[128]{0:T(256)(128)(2,1)S(1)} copy-done((bf16[128]{0:T(256)(128)(2,1)S(1)}, bf16[128]{0:T(256)(128)(2,1)}, u32[]{:S(2)}) %copy-start.14) | copy-done | bytes 280
  13.6 0.3 weights.1
  13.9 1.3 %collective-permute-done.2 = f32[81,128]{1,0:T(8,128)S(1)} collective-permute-done((f32[81,128]{1,0:T(8,128)S(1)}, f32[81,128]{1,0:T(8,128)S(1)}, u32[]{:S(2)}, u32[]{:S(2)}) %collective-permute-start.2) | collective-permute-done | bytes 41504 | tf_op jit(solution)/shard_map/halo_y/ppermute | solution.py:137
  15.2 1.8 %collective-permute-done.1 = f32[81,128]{1,0:T(8,128)S(1)} collective-permute-done((f32[81,128]{1,0:T(8,128)S(1)}, f32[81,128]{1,0:T(8,128)S(1)}, u32[]{:S(2)}, u32[]{:S(2)}) %collective-permute-start.1) | collective-permute-done | bytes 41504 | tf_op jit(solution)/shard_map/halo_y/ppermute | solution.py:136
  17.0 0.1 collective-permute-start.4
  17.1 1.6 %collective-permute-start.3 = (f32[81,128]{1,0:T(8,128)S(1)}, f32[81,128]{1,0:T(8,128)S(1)}, u32[]{:S(2)}, u32[]{:S(2)}) collective-permute-start(f32[81,128]{1,0:T(8,128)S(1)} %get-tuple-element.114), channel_id=1, source_target_pairs={{0,8},{8,0},{16,24},{24,16},{1,9},{9,1},{17,25},{25,17},{2,10},{10... | collective-permute-start | bytes 124424 | tf_op jit(solution)/shard_map/halo_x/ppermute | solution.py:136
  18.7 2.2 %collective-permute-done.4 = f32[81,128]{1,0:T(8,128)S(1)} collective-permute-done((f32[81,128]{1,0:T(8,128)S(1)}, f32[81,128]{1,0:T(8,128)S(1)}, u32[]{:S(2)}, u32[]{:S(2)}) %collective-permute-start.4) | collective-permute-done | bytes 41504 | tf_op jit(solution)/shard_map/halo_x/ppermute | solution.py:137
  21.0 0.0 collective-permute-done.3
  21.0 15.2 %layer.1 = (f32[144,128]{1,0:T(8,128)S(1)}, f32[256,256]{1,0:T(8,128)S(1)}, f32[81,128]{1,0:T(8,128)S(1)}, f32[81,128]{1,0:T(8,128)S(1)}, f32[168,128]{1,0:T(8,128)S(1)}) custom-call(s32[2,128]{1,0:T(2,128)S(1)} %get-tuple-element.58.refs_0_, s32[2,24,128]{2,1,0:T(8,128)S(1)} %get-tuple-element.59.refs_1_, f32[3,128]{1,0:T(4,128)S(1)} %copy-done.2, ...), custom_call_target="tpu_custom_call" | custom-call | tf_op jit(solution)/shard_map/layer/pallas_call | solution.py:1002
  36.2 0.2 collective-permute-start.6
  36.4 1.1 %collective-permute-start.5 = (f32[81,128]{1,0:T(8,128)S(1)}, f32[81,128]{1,0:T(8,128)S(1)}, u32[]{:S(2)}, u32[]{:S(2)}) collective-permute-start(f32[81,128]{1,0:T(8,128)S(1)} %get-tuple-element.110), channel_id=1, source_target_pairs={{0,24},{8,16},{16,8},{24,0},{1,25},{9,17},{17,9},{25,1},{2,26},{10... | collective-permute-start | bytes 124424 | tf_op jit(solution)/shard_map/halo_back/ppermute | solution.py:137
  37.5 0.0 collective-permute-done.6
  37.5 2.4 %collective-permute-done.5 = f32[81,128]{1,0:T(8,128)S(1)} collective-permute-done((f32[81,128]{1,0:T(8,128)S(1)}, f32[81,128]{1,0:T(8,128)S(1)}, u32[]{:S(2)}, u32[]{:S(2)}) %collective-permute-start.5) | collective-permute-done | bytes 41504 | tf_op jit(solution)/shard_map/halo_back/ppermute | solution.py:137
  39.9 0.5 collective-permute-start.8
  40.4 1.5 %collective-permute-start.7 = (f32[81,128]{1,0:T(8,128)S(1)}, f32[81,128]{1,0:T(8,128)S(1)}, u32[]{:S(2)}, u32[]{:S(2)}) collective-permute-start(f32[81,128]{1,0:T(8,128)S(1)} %get-tuple-element.106), channel_id=1, source_target_pairs={{0,6},{2,4},{4,2},{6,0},{1,7},{3,5},{5,3},{7,1},{8,14},{10,12},{12... | collective-permute-start | bytes 124424 | tf_op jit(solution)/shard_map/halo_back/ppermute | solution.py:137
  41.9 2.2 %collective-permute-done.8 = f32[81,128]{1,0:T(8,128)S(1)} collective-permute-done((f32[81,128]{1,0:T(8,128)S(1)}, f32[81,128]{1,0:T(8,128)S(1)}, u32[]{:S(2)}, u32[]{:S(2)}) %collective-permute-start.8) | collective-permute-done | bytes 41504 | tf_op jit(solution)/shard_map/halo_back/ppermute | solution.py:136
  44.1 2.3 %collective-permute-done.7 = f32[81,128]{1,0:T(8,128)S(1)} collective-permute-done((f32[81,128]{1,0:T(8,128)S(1)}, f32[81,128]{1,0:T(8,128)S(1)}, u32[]{:S(2)}, u32[]{:S(2)}) %collective-permute-start.7) | collective-permute-done | bytes 41504 | tf_op jit(solution)/shard_map/halo_back/ppermute | solution.py:137
  46.4 1.3 %collective-permute-start.9 = (f32[162,128]{1,0:T(8,128)S(1)}, f32[162,128]{1,0:T(8,128)S(1)}, u32[]{:S(2)}, u32[]{:S(2)}) collective-permute-start(f32[162,128]{1,0:T(8,128)S(1)} %halo_back.3), channel_id=1, source_target_pairs={{0,1},{1,0},{2,3},{3,2},{4,5},{5,4},{6,7},{7,6},{8,9},{9,8},{10,11... | collective-permute-start | bytes 248840 | tf_op jit(solution)/shard_map/halo_back/ppermute | solution.py:129
  47.7 1.1 %own_part.1 = (f32[1,128]{1,0:T(1,128)}, f32[128,128]{1,0:T(8,128)S(1)}, f32[3,128]{1,0:T(4,128)S(1)}) custom-call(f32[144,128]{1,0:T(8,128)S(1)} %get-tuple-element.91.refs_0_, f32[256,256]{1,0:T(8,128)S(1)} %get-tuple-element.92.refs_1_, f32[264,128]{1,0:T(8,128)S(1)} %add_bitcast_fusion.1.wide_ref.refs_3_.refs_2_, ...), custom_call_target="tpu_custom_call" | custom-call | tf_op jit(solution)/shard_map/own_part/pallas_call | solution.py:1020
  48.7 2.2 %collective-permute-done.9.refs_4_ = f32[162,128]{1,0:T(8,128)S(1)} collective-permute-done((f32[162,128]{1,0:T(8,128)S(1)}, f32[162,128]{1,0:T(8,128)S(1)}, u32[]{:S(2)}, u32[]{:S(2)}) %collective-permute-start.9) | collective-permute-done | bytes 82976 | tf_op jit(solution)/shard_map/halo_back/ppermute | solution.py:129
  50.9 1.0 %owner_sums.1 = (f32[3,128]{1,0:T(4,128)}, f32[128,128]{1,0:T(8,128)}) custom-call(f32[330,128]{1,0:T(8,128)S(1)} %get-tuple-element.54.refs_3_.refs_0_, f32[128,128]{1,0:T(8,128)S(1)} %get-tuple-element.98.refs_1_, f32[3,128]{1,0:T(4,128)S(1)} %get-tuple-element.99.refs_2_, f32[264,128]{1,0:T(8,128)S(1)} %add_bitcast_fusion.1.wide_ref.refs_3_.refs_2_, ...), custom_call_target="tpu_custom_call" | custom-call | tf_op jit(solution)/shard_map/owner_sums/pallas_call | solution.py:1032
  (23 shorter events, 0.2 us)
Async XLA Ops:
  0.6 0.8 %copy-start.6 = (f32[128,128]{1,0:T(8,128)S(1)}, f32[128,128]{1,0:T(8,128)}, u32[]{:S(2)}) copy-start(f32[128,128]{1,0:T(8,128)} %param.17) | copy-start | bytes 196612
  1.5 0.7 %copy-start.3 = (s32[1,12,8]{1,2,0:T(8,128)S(1)}, s32[1,12,8]{1,2,0:T(8,128)}, u32[]{:S(2)}) copy-start(s32[1,12,8]{1,2,0:T(8,128)} %param.19) | copy-start | bytes 1156
  1.5 0.7 %copy-start.5 = (s32[1,8,2]{1,2,0:T(2,128)S(1)}, s32[1,8,2]{1,2,0:T(2,128)}, u32[]{:S(2)}) copy-start(s32[1,8,2]{1,2,0:T(2,128)} %param.20) | copy-start | bytes 196
  1.5 0.7 %copy-start.4 = (s32[1,6,32]{2,0,1:T(1,128)S(1)}, s32[1,6,32]{2,0,1:T(1,128)}, u32[]{:S(2)}) copy-start(s32[1,6,32]{2,0,1:T(1,128)} %param.18) | copy-start | bytes 2308
  1.5 0.7 %copy-start.2 = (f32[3,128]{1,0:T(4,128)S(1)}, f32[3,128]{1,0:T(4,128)}, u32[]{:S(2)}) copy-start(f32[3,128]{1,0:T(4,128)} %refs_2_.1) | copy-start | bytes 4612
  2.2 3.7 %copy-start = (s32[6144]{0:T(1024)S(1)}, s32[6144]{0:T(1024)}, u32[]{:S(2)}) copy-start(s32[6144]{0:T(1024)} %param.21) | copy-start | bytes 73732
  2.2 3.7 %copy-start.1 = (s32[6144]{0:T(1024)S(1)}, s32[6144]{0:T(1024)}, u32[]{:S(2)}) copy-start(s32[6144]{0:T(1024)} %param.22) | copy-start | bytes 73732
  2.2 6.3 %copy-start.8 = (f32[128,128]{1,0:T(8,128)S(1)}, f32[128,128]{1,0:T(8,128)}, u32[]{:S(2)}) copy-start(f32[128,128]{1,0:T(8,128)} %param.24) | copy-start | bytes 196612
  2.9 5.6 %copy-start.7 = (f32[128,128]{1,0:T(8,128)S(1)}, f32[128,128]{1,0:T(8,128)}, u32[]{:S(2)}) copy-start(f32[128,128]{1,0:T(8,128)} %param.25) | copy-start | bytes 196612
  2.9 6.3 %collective-permute-start = (f32[162,128]{1,0:T(8,128)S(1)}, f32[162,128]{1,0:T(8,128)S(1)}, u32[]{:S(2)}, u32[]{:S(2)}) collective-permute-start(f32[162,128]{1,0:T(8,128)S(1)} %get-tuple-element.55), channel_id=1, source_target_pairs={{0,1},{1,0},{2,3},{3,2},{4,5},{5,4},{6,7},{7,6},{8,9},{9,8},{10,11... | collective-permute-start | bytes 248840 | tf_op jit(solution)/shard_map/halo_z/ppermute | solution.py:129
  8.5 0.7 %copy-start.13 = (f32[8,128]{1,0:T(8,128)S(1)}, f32[8,128]{1,0:T(8,128)}, u32[]{:S(2)}) copy-start(f32[8,128]{1,0:T(8,128)} %param.26) | copy-start | bytes 12292
  9.2 3.7 %copy-start.9 = (bf16[256,128]{1,0:T(8,128)(2,1)S(1)}, bf16[256,128]{1,0:T(8,128)(2,1)}, u32[]{:S(2)}) copy-start(bf16[256,128]{1,0:T(8,128)(2,1)} %param.30) | copy-start | bytes 196612
  9.2 3.7 %copy-start.10 = (bf16[128,128]{1,0:T(8,128)(2,1)S(1)}, bf16[128,128]{1,0:T(8,128)(2,1)}, u32[]{:S(2)}) copy-start(bf16[128,128]{1,0:T(8,128)(2,1)} %param.29) | copy-start | bytes 98308
  9.2 3.7 %copy-start.11 = (bf16[128,128]{1,0:T(8,128)(2,1)S(1)}, bf16[128,128]{1,0:T(8,128)(2,1)}, u32[]{:S(2)}) copy-start(bf16[128,128]{1,0:T(8,128)(2,1)} %param.28) | copy-start | bytes 98308
  9.2 3.7 %copy-start.12 = (bf16[128,128]{1,0:T(8,128)(2,1)S(1)}, bf16[128,128]{1,0:T(8,128)(2,1)}, u32[]{:S(2)}) copy-start(bf16[128,128]{1,0:T(8,128)(2,1)} %param.27) | copy-start | bytes 98308
  9.3 5.9 %collective-permute-start.2 = (f32[81,128]{1,0:T(8,128)S(1)}, f32[81,128]{1,0:T(8,128)S(1)}, u32[]{:S(2)}, u32[]{:S(2)}) collective-permute-start(f32[81,128]{1,0:T(8,128)S(1)} %get-tuple-element.117), channel_id=1, source_target_pairs={{0,6},{2,4},{4,2},{6,0},{1,7},{3,5},{5,3},{7,1},{8,14},{10,12},{12... | collective-permute-start | bytes 124424 | tf_op jit(solution)/shard_map/halo_y/ppermute | solution.py:137
  12.9 4.0 %collective-permute-start.1 = (f32[81,128]{1,0:T(8,128)S(1)}, f32[81,128]{1,0:T(8,128)S(1)}, u32[]{:S(2)}, u32[]{:S(2)}) collective-permute-start(f32[81,128]{1,0:T(8,128)S(1)} %get-tuple-element.118), channel_id=1, source_target_pairs={{0,2},{2,0},{4,6},{6,4},{1,3},{3,1},{5,7},{7,5},{8,10},{10,8},{12,... | collective-permute-start | bytes 124424 | tf_op jit(solution)/shard_map/halo_y/ppermute | solution.py:136
  12.9 0.7 %copy-start.14 = (bf16[128]{0:T(256)(128)(2,1)S(1)}, bf16[128]{0:T(256)(128)(2,1)}, u32[]{:S(2)}) copy-start(bf16[128]{0:T(256)(128)(2,1)} %param.31) | copy-start | bytes 772
  17.0 3.9 %collective-permute-start.4 = (f32[81,128]{1,0:T(8,128)S(1)}, f32[81,128]{1,0:T(8,128)S(1)}, u32[]{:S(2)}, u32[]{:S(2)}) collective-permute-start(f32[81,128]{1,0:T(8,128)S(1)} %get-tuple-element.113), channel_id=1, source_target_pairs={{0,24},{8,16},{16,8},{24,0},{1,25},{9,17},{17,9},{25,1},{2,26},{10... | collective-permute-start | bytes 124424 | tf_op jit(solution)/shard_map/halo_x/ppermute | solution.py:137
  17.1 3.9 %collective-permute-start.3 = (f32[81,128]{1,0:T(8,128)S(1)}, f32[81,128]{1,0:T(8,128)S(1)}, u32[]{:S(2)}, u32[]{:S(2)}) collective-permute-start(f32[81,128]{1,0:T(8,128)S(1)} %get-tuple-element.114), channel_id=1, source_target_pairs={{0,8},{8,0},{16,24},{24,16},{1,9},{9,1},{17,25},{25,17},{2,10},{10... | collective-permute-start | bytes 124424 | tf_op jit(solution)/shard_map/halo_x/ppermute | solution.py:136
  36.2 1.3 %collective-permute-start.6 = (f32[81,128]{1,0:T(8,128)S(1)}, f32[81,128]{1,0:T(8,128)S(1)}, u32[]{:S(2)}, u32[]{:S(2)}) collective-permute-start(f32[81,128]{1,0:T(8,128)S(1)} %get-tuple-element.109), channel_id=1, source_target_pairs={{0,8},{8,0},{16,24},{24,16},{1,9},{9,1},{17,25},{25,17},{2,10},{10... | collective-permute-start | bytes 124424 | tf_op jit(solution)/shard_map/halo_back/ppermute | solution.py:136
  36.4 3.5 %collective-permute-start.5 = (f32[81,128]{1,0:T(8,128)S(1)}, f32[81,128]{1,0:T(8,128)S(1)}, u32[]{:S(2)}, u32[]{:S(2)}) collective-permute-start(f32[81,128]{1,0:T(8,128)S(1)} %get-tuple-element.110), channel_id=1, source_target_pairs={{0,24},{8,16},{16,8},{24,0},{1,25},{9,17},{17,9},{25,1},{2,26},{10... | collective-permute-start | bytes 124424 | tf_op jit(solution)/shard_map/halo_back/ppermute | solution.py:137
  39.9 4.1 %collective-permute-start.8 = (f32[81,128]{1,0:T(8,128)S(1)}, f32[81,128]{1,0:T(8,128)S(1)}, u32[]{:S(2)}, u32[]{:S(2)}) collective-permute-start(f32[81,128]{1,0:T(8,128)S(1)} %get-tuple-element.105), channel_id=1, source_target_pairs={{0,2},{2,0},{4,6},{6,4},{1,3},{3,1},{5,7},{7,5},{8,10},{10,8},{12,... | collective-permute-start | bytes 124424 | tf_op jit(solution)/shard_map/halo_back/ppermute | solution.py:136
  40.4 5.9 %collective-permute-start.7 = (f32[81,128]{1,0:T(8,128)S(1)}, f32[81,128]{1,0:T(8,128)S(1)}, u32[]{:S(2)}, u32[]{:S(2)}) collective-permute-start(f32[81,128]{1,0:T(8,128)S(1)} %get-tuple-element.106), channel_id=1, source_target_pairs={{0,6},{2,4},{4,2},{6,0},{1,7},{3,5},{5,3},{7,1},{8,14},{10,12},{12... | collective-permute-start | bytes 124424 | tf_op jit(solution)/shard_map/halo_back/ppermute | solution.py:137
  46.4 4.6 %collective-permute-start.9 = (f32[162,128]{1,0:T(8,128)S(1)}, f32[162,128]{1,0:T(8,128)S(1)}, u32[]{:S(2)}, u32[]{:S(2)}) collective-permute-start(f32[162,128]{1,0:T(8,128)S(1)} %halo_back.3), channel_id=1, source_target_pairs={{0,1},{1,0},{2,3},{3,2},{4,5},{5,4},{6,7},{7,6},{8,9},{9,8},{10,11... | collective-permute-start | bytes 248840 | tf_op jit(solution)/shard_map/halo_back/ppermute | solution.py:129

commit v8 on v7

--- a/solution.py
+++ b/solution.py
@@ -341,19 +341,23 @@
     def flip(w):
         return w.astype(F32).T.astype(BF16)
 
-    w1, w2 = (0.5 * w1.astype(F32)).astype(BF16), (0.5 * w2.astype(F32)).astype(BF16)
+    w1 = (0.5 * w1.astype(F32)).astype(BF16)
+    wout = half_ref[5 * chans : 5 * chans + 1, :].astype(F32)
+    w2 = (0.5 * w2.astype(F32)).astype(BF16)
+    w2_out = (w2.astype(F32) * wout).astype(BF16)
+    wval = (0.2 * wval.astype(F32)).astype(BF16)
     down = dot_nn(rad, w1.astype(F32), HIGH)
     w1_ref[0:chans, :] = w1
     w1_ref[chans:, :] = jnp.concatenate([down, jnp.zeros_like(down)], axis=0).astype(BF16)
-    w2_ref[...] = w2
+    w2_ref[...] = w2_out[chans:, :]
     w1t_ref[...] = flip(w1)
     wevt_ref[0:chans, :] = flip(wenv)
     wevt_ref[chans:, :] = flip(wval)
     w2t_ref[:, 0:chans] = flip(w2[0:chans, :])
     w2t_ref[:, chans:] = flip(w2[chans:, :])
     wev_ref[:, 0:chans] = wenv
-    wev_ref[:, chans:] = wval
-    wout = half_ref[5 * chans : 5 * chans + 1, :].astype(F32)
+    wev_ref[:, chans : 2 * chans] = wval
+    wev_ref[:, 2 * chans :] = w2_out[0:chans, :]
     wcol_ref[...] = jnp.broadcast_to(wout, (LANES, chans)).T
     feat = rows_ref[0:own, :]
     tab_ref[0:own, :] = dot_nn(feat, wa, HIGH)
@@ -453,7 +457,8 @@
         big_ref,
         dt_ref,
         dv_ref,
-        dfa_ref,
+        dz2_ref,
+        hots_ref,
         live_ref,
         dy_ref,
         db_ref,
@@ -574,12 +579,14 @@
         return lax.broadcasted_iota(jnp.int32, (WIN, SUB), 0) == crow
 
     def select(k, s, start):
-        hot = window_hot(k, s, start)
+        near = jnp.clip(in_lanes(keys_of(k, s, 1) >> OTHER_BITS) - start, -1, WIN).astype(BF16)
+        hot = lax.broadcasted_iota(jnp.int32, (WIN, SUB), 0).astype(BF16) == near
         ys = stacked(y_ref, k, s, 1, 8)
-        parts = [hot.astype(F32)]
+        none = jnp.zeros((), BF16)
+        parts = [jnp.where(hot, jnp.ones((), BF16), none)]
         for m in range(8):
-            parts.append(jnp.where(hot, ys[m : m + 1, :], 0.0))
-        return jnp.concatenate(parts, axis=0).astype(BF16)
+            parts.append(jnp.where(hot, ys[m : m + 1, :].astype(BF16), none))
+        return jnp.concatenate(parts, axis=0)
 
     def load_window(ref, start):
         return jnp.concatenate(
@@ -615,7 +622,9 @@
     def phase_a(k, s, n, slow):
         lanes = lanes_of(s, n)
         crow = in_lanes(keys_of(k, s, n) >> OTHER_BITS)
-        hots = [one_hot(crow, 0, own)] + table_hots(k, s, n)
+        table = jnp.concatenate(table_hots(k, s, n), axis=0)
+        hots_ref[k, :, lanes] = table
+        hots = [one_hot(crow, 0, own), table]
         basis = stacked(basis_ref, k, s, n, n_basis)
         b_hi, b_lo = split(basis)
         hots.append(jnp.concatenate([b_hi, b_lo], axis=0).astype(BF16))
@@ -651,25 +660,24 @@
                 big_ref[:, part(j)] += value
 
         each_window(k, s, n, slow, totals)
-        total = 0.2 * big_ref[:, 0 : n * SUB]
+        total = big_ref[:, 0 : n * SUB]
         value = val_ref[k, :, lanes].astype(F32)
         scalar = (value * total).astype(BF16)
         half = dot_nn(w2t_ref[...], jnp.concatenate([first_ref[k, :, lanes], scalar], axis=0))
         up = 1.0 + jnp.tanh(half)
         second = half * up
         wcol = jnp.concatenate([wcol_ref[...]] * (n * sub_rows), axis=1)
-        ee = jnp.sum(second.astype(BF16).astype(F32) * wcol, axis=0, keepdims=True)
+        ee = jnp.sum(second * wcol, axis=0, keepdims=True)
         envv = in_lanes(plane(6, k, s, n))
         live = ee * in_lanes(plane(7, k, s, n))
         first_row = s * sub_rows
         for j in range(n * sub_rows):
             live_ref[k, pl.ds(first_row + j, 1), :] = live[:, j * LANES : (j + 1) * LANES]
         energy = ee * envv
-        dz2 = ((wcol * envv) * (up + second * (2.0 - up))).astype(BF16)
-        dj = dot_nn(w2_ref[...], dz2)
-        dfa_ref[k, :, lanes] = dj[0:chans].astype(BF16)
-        dscalar = dj[chans:]
-        dt = (0.2 * value * dscalar).astype(BF16)
+        dz2 = (envv * (up + second * (2.0 - up))).astype(BF16)
+        dz2_ref[k, :, lanes] = dz2
+        dscalar = dot_nn(w2_ref[...], dz2)
+        dt = (value * dscalar).astype(BF16)
         dt_ref[k, :, lanes] = dt
         dv_ref[k, :, lanes] = (total * dscalar).astype(BF16)
 
@@ -716,9 +724,8 @@
         denv_row = jnp.sum(dew * ew_ref[k, :, lanes].astype(F32), axis=0, keepdims=True)
         for j in range(height):
             dy_ref[0, j : j + 1, :] = denv_row[:, j * LANES : (j + 1) * LANES]
-        dfirst = dfa_ref[k, :, lanes].astype(F32) + dot_nn(
-            wev_ref[...], jnp.concatenate([dpre, dv_ref[k, :, lanes]], axis=0)
-        )
+        joined = jnp.concatenate([dpre, dv_ref[k, :, lanes], dz2_ref[k, :, lanes]], axis=0)
+        dfirst = dot_nn(wev_ref[...], joined)
         dz1 = (dfirst * dsilu_ref[k, :, lanes].astype(F32)).astype(BF16)
         dboth = dot_nn(w1_ref[...], dz1)
         dmixed = dboth[0:chans].astype(BF16)
@@ -749,7 +756,7 @@
             dr_ref[pl.ds(3 + i, height, stride=16), :] = lo
         dr = jnp.concatenate([dr_ref[j * 16 : (j + 1) * 16, :] for j in range(height)], axis=1)
         moved = jnp.concatenate([dmixed, dr.astype(BF16)], axis=0)
-        sums = dot_nt(jnp.concatenate(table_hots(k, s, n), axis=0), moved)
+        sums = dot_nt(hots_ref[k, :, lanes], moved)
         acc_ref[:, 0:chans] += sums[:, 0:chans]
         acc_ref[:, chans : chans + 16] += sums[:, chans:]
 
@@ -938,9 +945,9 @@
         )
 
     with jax.named_scope("halo_y"):
-        came[2], key, bounds, w_first, w_env, w_value, w_second, w_out = lax.optimization_barrier(
-            (came[2], key, bounds, w_first, w_env, w_value, w_second, w_out)
-        )
+        given = (w_proj_a, w_proj_b, w_radial, w_first, w_env, w_value, w_second, w_out)
+        came[2], key, bounds, given = lax.optimization_barrier((came[2], key, bounds, given))
+        w_proj_a, w_proj_b, w_radial, w_first, w_env, w_value, w_second, w_out = given
         came[1] = plan.send(1, glue(plan, 1, (2,), plan.own_rest, own_rows, came))
 
     with jax.named_scope("weights"):
@@ -956,8 +963,8 @@
                 shape(2 * chans, chans, dtype=BF16),
                 shape(chans, 2 * chans, dtype=BF16),
                 shape(chans + 2 * n_basis, chans, dtype=BF16),
-                shape(chans, 2 * chans, dtype=BF16),
-                shape(2 * chans, chans, dtype=BF16),
+                shape(chans, 3 * chans, dtype=BF16),
+                shape(chans, chans, dtype=BF16),
                 shape(chans, LANES),
             ],
             in_specs=[VMEM] * 3,
@@ -989,6 +996,7 @@
         pltpu.VMEM(planes, BF16),
         pltpu.VMEM(planes, BF16),
         pltpu.VMEM(planes, BF16),
+        pltpu.VMEM((n_chunks, n_sel - own, CHUNK), BF16),
         pltpu.VMEM((n_chunks, CHUNK // LANES, LANES), F32),
         pltpu.VMEM((9, CHUNK // LANES, LANES), F32),
         pltpu.VMEM((CHUNK // LANES * n_basis, LANES), F32),

time: 52.1 us -> 51.5 us (0.988)
  starting transfers between devices: 12.9 us -> 20.5 us
  Pallas kernels: 20.9 us -> 13.9 us
  waiting for transfers between devices: 14.3 us -> 12.7 us
    pallas_call x1, Pallas kernels: 15.2 us -> 8.22 us  [local(): pl.pallas_call(lambda *refs: main_kernel(plan, *refs), out_shape=[shape(o...]
    ppermute x4, starting transfers between devices: 6.32 us -> 13.2 us  [send(): lax.ppermute(jnp.where(even, messages[down], messages[up]), AXES[a], behind)]
    ppermute x4, waiting for transfers between devices: 8.18 us -> 7.18 us  [send(): lax.ppermute(jnp.where(even, messages[down], messages[up]), AXES[a], behind)]
where the time goes in v8:
time: 51.5 us; the launch traced here: 51.2 us
  starting transfers between devices  20.5 us (40%)
  Pallas kernels  13.9 us (27%)
  waiting for transfers between devices  12.7 us (25%)
  local copies, waits for them, and re-layouts  2.34 us (5%)
  between operations  1.56 us (3%)
    ppermute x4, starting transfers between devices, send(): lax.ppermute(jnp.where(even, messages[down], messages[up]), AXES[a], behind)  13.2 us
    pallas_call x1, Pallas kernels, local(): pl.pallas_call(lambda *refs: main_kernel(plan, *refs), out_shape=[shape(o...  8.22 us
    ppermute x4, waiting for transfers between devices, send(): lax.ppermute(jnp.where(even, messages[down], messages[up]), AXES[a], behind)  7.18 us
    ppermute x2, starting transfers between devices, send(): lax.ppermute(message, AXES[a], [(i, (i + step) % n) for i in range(n)])  4.54 us
    ppermute x4, waiting for transfers between devices, send(): lax.ppermute(jnp.where(even, messages[up], messages[down]), AXES[a], ahead)  3.61 us
    ppermute x4, starting transfers between devices, send(): lax.ppermute(jnp.where(even, messages[up], messages[down]), AXES[a], ahead)  2.81 us
    pallas_call x1, Pallas kernels, local(): pl.pallas_call(lambda *refs: sort_kernel(own, *refs), out_shape=[shape(n_...  2.55 us
    unnamed x30, local copies, waits for them, and re-layouts  2.34 us
  transfers between devices with their start and end apart: 10, of which 7 were waited for; matrix products, arithmetic and copies ran while one was open for 0% of the time, Pallas kernels for 8%

profile of v8, /device:TPU:0, one launch (start us, length us, event | category | flops | bytes accessed | tf_op | source)
XLA Modules:
  0.0 51.2 jit_solution(10699491317926905995)
XLA Ops:
  0.6 0.0 copy-start.6
  1.3 0.1 copy-done.6
  1.5 0.0 copy-start.4
  1.5 0.0 copy-start.2
  1.5 0.6 %copy-done.3 = s32[1,12,8]{1,2,0:T(8,128)S(1)} copy-done((s32[1,12,8]{1,2,0:T(8,128)S(1)}, s32[1,12,8]{1,2,0:T(8,128)}, u32[]{:S(2)}) %copy-start.3) | copy-done | bytes 408
  2.2 0.0 copy-done.5
  2.2 0.0 copy-done.4
  2.2 0.0 copy-done.2
  2.2 0.7 %prep.1 = (f32[162,128]{1,0:T(8,128)S(1)}, f32[168,128]{1,0:T(8,128)S(1)}, f32[330,128]{1,0:T(8,128)S(1)}) custom-call(f32[136,128]{1,0:T(8,128)S(1)} %add_bitcast_fusion.2.refs_0_.rows_ref, f32[3,128]{1,0:T(4,128)S(1)} %copy-done.2, s32[6,1,32]{2,1,0:T(1,128)S(1)} %bitcast.25, s32[1,8,12]{2,1,0:T(8,128)S(1)} %bitcast.24, s32[1,2,8]{2,1,0:T(2,128)S(1)} %bitcast.26), custom_call_target="tpu_custom_call" | custom-call | tf_op jit(solution)/shard_map/prep/pallas_call | solution.py:908
  2.9 3.0 %collective-permute-start = (f32[162,128]{1,0:T(8,128)S(1)}, f32[162,128]{1,0:T(8,128)S(1)}, u32[]{:S(2)}, u32[]{:S(2)}) collective-permute-start(f32[162,128]{1,0:T(8,128)S(1)} %get-tuple-element.58), channel_id=1, source_target_pairs={{0,1},{1,0},{2,3},{3,2},{4,5},{5,4},{6,7},{7,6},{8,9},{9,8},{10,11... | collective-permute-start | bytes 248840 | tf_op jit(solution)/shard_map/halo_z/ppermute | solution.py:129
  5.9 0.0 copy-done
  5.9 0.0 copy-done.1
  5.9 2.5 %group_edges.1 = (s32[2,24,128]{2,1,0:T(8,128)S(1)}, s32[2,128]{1,0:T(2,128)S(1)}) custom-call(f32[136,128]{1,0:T(8,128)S(1)} %add_bitcast_fusion.2.refs_0_.rows_ref, s32[48,128]{1,0:T(8,128)S(1)} %bitcast.22, s32[48,128]{1,0:T(8,128)S(1)} %bitcast.23), custom_call_target="tpu_custom_call" | custom-call | tf_op jit(solution)/shard_map/group_edges/pallas_call | solution.py:931
  8.4 0.0 collective-permute-done.refs_1_.refs_3_.refs_8_
  8.5 0.0 copy-start.7
  8.5 0.0 copy-start.10
  8.5 0.0 copy-start.11
  8.5 0.0 copy-start.12
  8.5 4.1 %collective-permute-start.2 = (f32[81,128]{1,0:T(8,128)S(1)}, f32[81,128]{1,0:T(8,128)S(1)}, u32[]{:S(2)}, u32[]{:S(2)}) collective-permute-start(f32[81,128]{1,0:T(8,128)S(1)} %get-tuple-element.123), channel_id=1, source_target_pairs={{0,6},{2,4},{4,2},{6,0},{1,7},{3,5},{5,3},{7,1},{8,14},{10,12},{12... | collective-permute-start | bytes 124424 | tf_op jit(solution)/shard_map/halo_y/ppermute | solution.py:137
  12.6 0.0 collective-permute-start.1
  12.6 0.0 copy-done.7
  12.6 0.0 copy-done.10
  12.6 0.0 copy-done.11
  12.7 0.0 copy-done.12
  12.7 0.6 %copy-done.14 = bf16[128]{0:T(256)(128)(2,1)S(1)} copy-done((bf16[128]{0:T(256)(128)(2,1)S(1)}, bf16[128]{0:T(256)(128)(2,1)}, u32[]{:S(2)}) %copy-start.14) | copy-done | bytes 280
  13.3 0.0 copy-start.13
  13.3 0.8 %copy-done.8 = f32[128,128]{1,0:T(8,128)S(1)} copy-done((f32[128,128]{1,0:T(8,128)S(1)}, f32[128,128]{1,0:T(8,128)}, u32[]{:S(2)}) %copy-start.8) | copy-done | bytes 65560
  14.1 0.0 copy-done.9
  14.2 0.3 weights.1
  14.5 0.3 collective-permute-done.2
  14.8 1.9 %collective-permute-done.1 = f32[81,128]{1,0:T(8,128)S(1)} collective-permute-done((f32[81,128]{1,0:T(8,128)S(1)}, f32[81,128]{1,0:T(8,128)S(1)}, u32[]{:S(2)}, u32[]{:S(2)}) %collective-permute-start.1) | collective-permute-done | bytes 41504 | tf_op jit(solution)/shard_map/halo_y/ppermute | solution.py:136
  16.7 0.1 collective-permute-start.4
  16.8 1.6 %collective-permute-start.3 = (f32[81,128]{1,0:T(8,128)S(1)}, f32[81,128]{1,0:T(8,128)S(1)}, u32[]{:S(2)}, u32[]{:S(2)}) collective-permute-start(f32[81,128]{1,0:T(8,128)S(1)} %get-tuple-element.120), channel_id=1, source_target_pairs={{0,8},{8,0},{16,24},{24,16},{1,9},{9,1},{17,25},{25,17},{2,10},{10... | collective-permute-start | bytes 124424 | tf_op jit(solution)/shard_map/halo_x/ppermute | solution.py:136
  18.4 2.2 %collective-permute-done.4 = f32[81,128]{1,0:T(8,128)S(1)} collective-permute-done((f32[81,128]{1,0:T(8,128)S(1)}, f32[81,128]{1,0:T(8,128)S(1)}, u32[]{:S(2)}, u32[]{:S(2)}) %collective-permute-start.4) | collective-permute-done | bytes 41504 | tf_op jit(solution)/shard_map/halo_x/ppermute | solution.py:137
  20.7 0.0 collective-permute-done.3
  20.7 8.2 %layer.1 = (f32[144,128]{1,0:T(8,128)S(1)}, f32[256,256]{1,0:T(8,128)S(1)}, f32[81,128]{1,0:T(8,128)S(1)}, f32[81,128]{1,0:T(8,128)S(1)}, f32[168,128]{1,0:T(8,128)S(1)}) custom-call(s32[2,128]{1,0:T(2,128)S(1)} %get-tuple-element.61.refs_0_, s32[2,24,128]{2,1,0:T(8,128)S(1)} %get-tuple-element.62.refs_1_, f32[3,128]{1,0:T(4,128)S(1)} %copy-done.2, ...), custom_call_target="tpu_custom_call" | custom-call | tf_op jit(solution)/shard_map/layer/pallas_call | solution.py:1010
  28.9 0.2 collective-permute-start.6
  29.1 7.6 %collective-permute-start.5 = (f32[81,128]{1,0:T(8,128)S(1)}, f32[81,128]{1,0:T(8,128)S(1)}, u32[]{:S(2)}, u32[]{:S(2)}) collective-permute-start(f32[81,128]{1,0:T(8,128)S(1)} %get-tuple-element.116), channel_id=1, source_target_pairs={{0,24},{8,16},{16,8},{24,0},{1,25},{9,17},{17,9},{25,1},{2,26},{10... | collective-permute-start | bytes 124424 | tf_op jit(solution)/shard_map/halo_back/ppermute | solution.py:137
  36.7 0.0 collective-permute-done.6
  36.7 1.9 %collective-permute-done.5 = f32[81,128]{1,0:T(8,128)S(1)} collective-permute-done((f32[81,128]{1,0:T(8,128)S(1)}, f32[81,128]{1,0:T(8,128)S(1)}, u32[]{:S(2)}, u32[]{:S(2)}) %collective-permute-start.5) | collective-permute-done | bytes 41504 | tf_op jit(solution)/shard_map/halo_back/ppermute | solution.py:137
  38.7 1.0 %collective-permute-start.8 = (f32[81,128]{1,0:T(8,128)S(1)}, f32[81,128]{1,0:T(8,128)S(1)}, u32[]{:S(2)}, u32[]{:S(2)}) collective-permute-start(f32[81,128]{1,0:T(8,128)S(1)} %get-tuple-element.111), channel_id=1, source_target_pairs={{0,2},{2,0},{4,6},{6,4},{1,3},{3,1},{5,7},{7,5},{8,10},{10,8},{12,... | collective-permute-start | bytes 124424 | tf_op jit(solution)/shard_map/halo_back/ppermute | solution.py:136
  39.7 1.4 %collective-permute-start.7 = (f32[81,128]{1,0:T(8,128)S(1)}, f32[81,128]{1,0:T(8,128)S(1)}, u32[]{:S(2)}, u32[]{:S(2)}) collective-permute-start(f32[81,128]{1,0:T(8,128)S(1)} %get-tuple-element.112), channel_id=1, source_target_pairs={{0,6},{2,4},{4,2},{6,0},{1,7},{3,5},{5,3},{7,1},{8,14},{10,12},{12... | collective-permute-start | bytes 124424 | tf_op jit(solution)/shard_map/halo_back/ppermute | solution.py:137
  41.1 1.7 %collective-permute-done.8 = f32[81,128]{1,0:T(8,128)S(1)} collective-permute-done((f32[81,128]{1,0:T(8,128)S(1)}, f32[81,128]{1,0:T(8,128)S(1)}, u32[]{:S(2)}, u32[]{:S(2)}) %collective-permute-start.8) | collective-permute-done | bytes 41504 | tf_op jit(solution)/shard_map/halo_back/ppermute | solution.py:136
  42.8 2.7 %collective-permute-done.7 = f32[81,128]{1,0:T(8,128)S(1)} collective-permute-done((f32[81,128]{1,0:T(8,128)S(1)}, f32[81,128]{1,0:T(8,128)S(1)}, u32[]{:S(2)}, u32[]{:S(2)}) %collective-permute-start.7) | collective-permute-done | bytes 41504 | tf_op jit(solution)/shard_map/halo_back/ppermute | solution.py:137
  45.6 1.5 %collective-permute-start.9 = (f32[162,128]{1,0:T(8,128)S(1)}, f32[162,128]{1,0:T(8,128)S(1)}, u32[]{:S(2)}, u32[]{:S(2)}) collective-permute-start(f32[162,128]{1,0:T(8,128)S(1)} %halo_back.3), channel_id=1, source_target_pairs={{0,1},{1,0},{2,3},{3,2},{4,5},{5,4},{6,7},{7,6},{8,9},{9,8},{10,11... | collective-permute-start | bytes 248840 | tf_op jit(solution)/shard_map/halo_back/ppermute | solution.py:129
  47.1 1.1 %own_part.1 = (f32[1,128]{1,0:T(1,128)}, f32[128,128]{1,0:T(8,128)S(1)}, f32[3,128]{1,0:T(4,128)S(1)}) custom-call(f32[144,128]{1,0:T(8,128)S(1)} %get-tuple-element.97.refs_0_, f32[256,256]{1,0:T(8,128)S(1)} %get-tuple-element.98.refs_1_, f32[264,128]{1,0:T(8,128)S(1)} %add_bitcast_fusion.1.wide_ref.refs_3_.refs_2_, ...), custom_call_target="tpu_custom_call" | custom-call | tf_op jit(solution)/shard_map/own_part/pallas_call | solution.py:1028
  48.2 1.9 %collective-permute-done.9.refs_4_ = f32[162,128]{1,0:T(8,128)S(1)} collective-permute-done((f32[162,128]{1,0:T(8,128)S(1)}, f32[162,128]{1,0:T(8,128)S(1)}, u32[]{:S(2)}, u32[]{:S(2)}) %collective-permute-start.9) | collective-permute-done | bytes 82976 | tf_op jit(solution)/shard_map/halo_back/ppermute | solution.py:129
  50.1 1.0 %owner_sums.1 = (f32[3,128]{1,0:T(4,128)}, f32[128,128]{1,0:T(8,128)}) custom-call(f32[330,128]{1,0:T(8,128)S(1)} %get-tuple-element.57.refs_3_.refs_0_, f32[128,128]{1,0:T(8,128)S(1)} %get-tuple-element.104.refs_1_, f32[3,128]{1,0:T(4,128)S(1)} %get-tuple-element.105.refs_2_, f32[264,128]{1,0:T(8,128)S(1)} %add_bitcast_fusion.1.wide_ref.refs_3_.refs_2_, ...), custom_call_target="tpu_custom_call" | custom-call | tf_op jit(solution)/shard_map/owner_sums/pallas_call | solution.py:1040
  (23 shorter events, 0.2 us)
Async XLA Ops:
  0.6 0.8 %copy-start.6 = (f32[128,128]{1,0:T(8,128)S(1)}, f32[128,128]{1,0:T(8,128)}, u32[]{:S(2)}) copy-start(f32[128,128]{1,0:T(8,128)} %param.17) | copy-start | bytes 196612
  1.5 0.7 %copy-start.3 = (s32[1,12,8]{1,2,0:T(8,128)S(1)}, s32[1,12,8]{1,2,0:T(8,128)}, u32[]{:S(2)}) copy-start(s32[1,12,8]{1,2,0:T(8,128)} %param.19) | copy-start | bytes 1156
  1.5 0.7 %copy-start.5 = (s32[1,8,2]{1,2,0:T(2,128)S(1)}, s32[1,8,2]{1,2,0:T(2,128)}, u32[]{:S(2)}) copy-start(s32[1,8,2]{1,2,0:T(2,128)} %param.20) | copy-start | bytes 196
  1.5 0.7 %copy-start.4 = (s32[1,6,32]{2,0,1:T(1,128)S(1)}, s32[1,6,32]{2,0,1:T(1,128)}, u32[]{:S(2)}) copy-start(s32[1,6,32]{2,0,1:T(1,128)} %param.18) | copy-start | bytes 2308
  1.5 0.7 %copy-start.2 = (f32[3,128]{1,0:T(4,128)S(1)}, f32[3,128]{1,0:T(4,128)}, u32[]{:S(2)}) copy-start(f32[3,128]{1,0:T(4,128)} %refs_2_.1) | copy-start | bytes 4612
  2.2 3.7 %copy-start = (s32[6144]{0:T(1024)S(1)}, s32[6144]{0:T(1024)}, u32[]{:S(2)}) copy-start(s32[6144]{0:T(1024)} %param.21) | copy-start | bytes 73732
  2.2 3.7 %copy-start.1 = (s32[6144]{0:T(1024)S(1)}, s32[6144]{0:T(1024)}, u32[]{:S(2)}) copy-start(s32[6144]{0:T(1024)} %param.22) | copy-start | bytes 73732
  2.9 5.6 %collective-permute-start = (f32[162,128]{1,0:T(8,128)S(1)}, f32[162,128]{1,0:T(8,128)S(1)}, u32[]{:S(2)}, u32[]{:S(2)}) collective-permute-start(f32[162,128]{1,0:T(8,128)S(1)} %get-tuple-element.58), channel_id=1, source_target_pairs={{0,1},{1,0},{2,3},{3,2},{4,5},{5,4},{6,7},{7,6},{8,9},{9,8},{10,11... | collective-permute-start | bytes 248840 | tf_op jit(solution)/shard_map/halo_z/ppermute | solution.py:129
  8.5 4.2 %copy-start.7 = (bf16[256,128]{1,0:T(8,128)(2,1)S(1)}, bf16[256,128]{1,0:T(8,128)(2,1)}, u32[]{:S(2)}) copy-start(bf16[256,128]{1,0:T(8,128)(2,1)} %param.30) | copy-start | bytes 196612
  8.5 4.2 %copy-start.10 = (bf16[128,128]{1,0:T(8,128)(2,1)S(1)}, bf16[128,128]{1,0:T(8,128)(2,1)}, u32[]{:S(2)}) copy-start(bf16[128,128]{1,0:T(8,128)(2,1)} %param.29) | copy-start | bytes 98308
  8.5 4.2 %copy-start.11 = (bf16[128,128]{1,0:T(8,128)(2,1)S(1)}, bf16[128,128]{1,0:T(8,128)(2,1)}, u32[]{:S(2)}) copy-start(bf16[128,128]{1,0:T(8,128)(2,1)} %param.28) | copy-start | bytes 98308
  8.5 4.1 %copy-start.12 = (bf16[128,128]{1,0:T(8,128)(2,1)S(1)}, bf16[128,128]{1,0:T(8,128)(2,1)}, u32[]{:S(2)}) copy-start(bf16[128,128]{1,0:T(8,128)(2,1)} %param.27) | copy-start | bytes 98308
  8.5 6.2 %collective-permute-start.2 = (f32[81,128]{1,0:T(8,128)S(1)}, f32[81,128]{1,0:T(8,128)S(1)}, u32[]{:S(2)}, u32[]{:S(2)}) collective-permute-start(f32[81,128]{1,0:T(8,128)S(1)} %get-tuple-element.123), channel_id=1, source_target_pairs={{0,6},{2,4},{4,2},{6,0},{1,7},{3,5},{5,3},{7,1},{8,14},{10,12},{12... | collective-permute-start | bytes 124424 | tf_op jit(solution)/shard_map/halo_y/ppermute | solution.py:137
  12.6 4.0 %collective-permute-start.1 = (f32[81,128]{1,0:T(8,128)S(1)}, f32[81,128]{1,0:T(8,128)S(1)}, u32[]{:S(2)}, u32[]{:S(2)}) collective-permute-start(f32[81,128]{1,0:T(8,128)S(1)} %get-tuple-element.124), channel_id=1, source_target_pairs={{0,2},{2,0},{4,6},{6,4},{1,3},{3,1},{5,7},{7,5},{8,10},{10,8},{12,... | collective-permute-start | bytes 124424 | tf_op jit(solution)/shard_map/halo_y/ppermute | solution.py:136
  12.6 0.7 %copy-start.14 = (bf16[128]{0:T(256)(128)(2,1)S(1)}, bf16[128]{0:T(256)(128)(2,1)}, u32[]{:S(2)}) copy-start(bf16[128]{0:T(256)(128)(2,1)} %param.31) | copy-start | bytes 772
  13.3 0.8 %copy-start.8 = (f32[128,128]{1,0:T(8,128)S(1)}, f32[128,128]{1,0:T(8,128)}, u32[]{:S(2)}) copy-start(f32[128,128]{1,0:T(8,128)} %param.25) | copy-start | bytes 196612
  13.3 0.9 %copy-start.9 = (f32[128,128]{1,0:T(8,128)S(1)}, f32[128,128]{1,0:T(8,128)}, u32[]{:S(2)}) copy-start(f32[128,128]{1,0:T(8,128)} %param.24) | copy-start | bytes 196612
  13.3 0.9 %copy-start.13 = (f32[8,128]{1,0:T(8,128)S(1)}, f32[8,128]{1,0:T(8,128)}, u32[]{:S(2)}) copy-start(f32[8,128]{1,0:T(8,128)} %param.26) | copy-start | bytes 12292
  16.7 3.9 %collective-permute-start.4 = (f32[81,128]{1,0:T(8,128)S(1)}, f32[81,128]{1,0:T(8,128)S(1)}, u32[]{:S(2)}, u32[]{:S(2)}) collective-permute-start(f32[81,128]{1,0:T(8,128)S(1)} %get-tuple-element.119), channel_id=1, source_target_pairs={{0,24},{8,16},{16,8},{24,0},{1,25},{9,17},{17,9},{25,1},{2,26},{10... | collective-permute-start | bytes 124424 | tf_op jit(solution)/shard_map/halo_x/ppermute | solution.py:137
  16.8 3.9 %collective-permute-start.3 = (f32[81,128]{1,0:T(8,128)S(1)}, f32[81,128]{1,0:T(8,128)S(1)}, u32[]{:S(2)}, u32[]{:S(2)}) collective-permute-start(f32[81,128]{1,0:T(8,128)S(1)} %get-tuple-element.120), channel_id=1, source_target_pairs={{0,8},{8,0},{16,24},{24,16},{1,9},{9,1},{17,25},{25,17},{2,10},{10... | collective-permute-start | bytes 124424 | tf_op jit(solution)/shard_map/halo_x/ppermute | solution.py:136
  28.9 7.8 %collective-permute-start.6 = (f32[81,128]{1,0:T(8,128)S(1)}, f32[81,128]{1,0:T(8,128)S(1)}, u32[]{:S(2)}, u32[]{:S(2)}) collective-permute-start(f32[81,128]{1,0:T(8,128)S(1)} %get-tuple-element.115), channel_id=1, source_target_pairs={{0,8},{8,0},{16,24},{24,16},{1,9},{9,1},{17,25},{25,17},{2,10},{10... | collective-permute-start | bytes 124424 | tf_op jit(solution)/shard_map/halo_back/ppermute | solution.py:136
  29.1 9.5 %collective-permute-start.5 = (f32[81,128]{1,0:T(8,128)S(1)}, f32[81,128]{1,0:T(8,128)S(1)}, u32[]{:S(2)}, u32[]{:S(2)}) collective-permute-start(f32[81,128]{1,0:T(8,128)S(1)} %get-tuple-element.116), channel_id=1, source_target_pairs={{0,24},{8,16},{16,8},{24,0},{1,25},{9,17},{17,9},{25,1},{2,26},{10... | collective-permute-start | bytes 124424 | tf_op jit(solution)/shard_map/halo_back/ppermute | solution.py:137
  38.7 4.1 %collective-permute-start.8 = (f32[81,128]{1,0:T(8,128)S(1)}, f32[81,128]{1,0:T(8,128)S(1)}, u32[]{:S(2)}, u32[]{:S(2)}) collective-permute-start(f32[81,128]{1,0:T(8,128)S(1)} %get-tuple-element.111), channel_id=1, source_target_pairs={{0,2},{2,0},{4,6},{6,4},{1,3},{3,1},{5,7},{7,5},{8,10},{10,8},{12,... | collective-permute-start | bytes 124424 | tf_op jit(solution)/shard_map/halo_back/ppermute | solution.py:136
  39.7 5.8 %collective-permute-start.7 = (f32[81,128]{1,0:T(8,128)S(1)}, f32[81,128]{1,0:T(8,128)S(1)}, u32[]{:S(2)}, u32[]{:S(2)}) collective-permute-start(f32[81,128]{1,0:T(8,128)S(1)} %get-tuple-element.112), channel_id=1, source_target_pairs={{0,6},{2,4},{4,2},{6,0},{1,7},{3,5},{5,3},{7,1},{8,14},{10,12},{12... | collective-permute-start | bytes 124424 | tf_op jit(solution)/shard_map/halo_back/ppermute | solution.py:137
  45.6 4.6 %collective-permute-start.9 = (f32[162,128]{1,0:T(8,128)S(1)}, f32[162,128]{1,0:T(8,128)S(1)}, u32[]{:S(2)}, u32[]{:S(2)}) collective-permute-start(f32[162,128]{1,0:T(8,128)S(1)} %halo_back.3), channel_id=1, source_target_pairs={{0,1},{1,0},{2,3},{3,2},{4,5},{5,4},{6,7},{7,6},{8,9},{9,8},{10,11... | collective-permute-start | bytes 248840 | tf_op jit(solution)/shard_map/halo_back/ppermute | solution.py:129

commit v9 on v8

--- a/solution.py
+++ b/solution.py
@@ -630,11 +630,10 @@
         hots.append(jnp.concatenate([b_hi, b_lo], axis=0).astype(BF16))
         hots.append(jnp.concatenate([b_hi, jnp.zeros_like(b_hi)], axis=0).astype(BF16))
         mixed = dot_nn(table_ref[...], jnp.concatenate(hots, axis=0)).astype(BF16)
-        half = dot_nn(w1t_ref[...], mixed)
+        half = dot_nn(w1t_ref[...], mixed).astype(BF16)
         up = 1.0 + jnp.tanh(half)
         first = half * up
-        dsilu_ref[k, :, lanes] = (up + first * (2.0 - up)).astype(BF16)
-        first = first.astype(BF16)
+        dsilu_ref[k, :, lanes] = up + first * (2.0 - up)
         first_ref[k, :, lanes] = first
         both = dot_nn(wevt_ref[...], first)
         ew = (both[0:chans] * in_lanes(plane(6, k, s, n))).astype(BF16)
@@ -664,17 +663,18 @@
         value = val_ref[k, :, lanes].astype(F32)
         scalar = (value * total).astype(BF16)
         half = dot_nn(w2t_ref[...], jnp.concatenate([first_ref[k, :, lanes], scalar], axis=0))
+        half = half.astype(BF16)
         up = 1.0 + jnp.tanh(half)
         second = half * up
         wcol = jnp.concatenate([wcol_ref[...]] * (n * sub_rows), axis=1)
-        ee = jnp.sum(second * wcol, axis=0, keepdims=True)
+        ee = jnp.sum(second.astype(F32) * wcol, axis=0, keepdims=True)
         envv = in_lanes(plane(6, k, s, n))
         live = ee * in_lanes(plane(7, k, s, n))
         first_row = s * sub_rows
         for j in range(n * sub_rows):
             live_ref[k, pl.ds(first_row + j, 1), :] = live[:, j * LANES : (j + 1) * LANES]
         energy = ee * envv
-        dz2 = (envv * (up + second * (2.0 - up))).astype(BF16)
+        dz2 = envv.astype(BF16) * (up + second * (2.0 - up))
         dz2_ref[k, :, lanes] = dz2
         dscalar = dot_nn(w2_ref[...], dz2)
         dt = (value * dscalar).astype(BF16)

time: 51.5 us -> 50.8 us (0.986)
  starting transfers between devices: 20.5 us -> 13.6 us
  Pallas kernels: 13.9 us -> 19.8 us
    ppermute x4, starting transfers between devices: 13.2 us -> 6.66 us  [send(): lax.ppermute(jnp.where(even, messages[down], messages[up]), AXES[a], behind)]
    pallas_call x1, Pallas kernels: 8.22 us -> 14.1 us  [local(): pl.pallas_call(lambda *refs: main_kernel(plan, *refs), out_shape=[shape(o...]
where the time goes in v9:
time: 50.8 us; the launch traced here: 50.6 us
  Pallas kernels  19.8 us (39%)
  starting transfers between devices  13.6 us (27%)
  waiting for transfers between devices  13.2 us (26%)
  local copies, waits for them, and re-layouts  2.34 us (5%)
  between operations  1.56 us (3%)
    pallas_call x1, Pallas kernels, local(): pl.pallas_call(lambda *refs: main_kernel(plan, *refs), out_shape=[shape(o...  14.1 us
    ppermute x4, waiting for transfers between devices, send(): lax.ppermute(jnp.where(even, messages[down], messages[up]), AXES[a], behind)  7.2 us
    ppermute x4, starting transfers between devices, send(): lax.ppermute(jnp.where(even, messages[down], messages[up]), AXES[a], behind)  6.66 us
    ppermute x2, starting transfers between devices, send(): lax.ppermute(message, AXES[a], [(i, (i + step) % n) for i in range(n)])  4.6 us
    ppermute x4, waiting for transfers between devices, send(): lax.ppermute(jnp.where(even, messages[up], messages[down]), AXES[a], ahead)  4.1 us
    pallas_call x1, Pallas kernels, local(): pl.pallas_call(lambda *refs: sort_kernel(own, *refs), out_shape=[shape(n_...  2.55 us
    ppermute x4, starting transfers between devices, send(): lax.ppermute(jnp.where(even, messages[up], messages[down]), AXES[a], ahead)  2.36 us
    unnamed x30, local copies, waits for them, and re-layouts  2.34 us
  transfers between devices with their start and end apart: 10, of which 7 were waited for; matrix products, arithmetic and copies ran while one was open for 0% of the time, Pallas kernels for 8%

profile of v9, /device:TPU:0, one launch (start us, length us, event | category | flops | bytes accessed | tf_op | source)
XLA Modules:
  0.0 50.6 jit_solution(13817743822485555483)
XLA Ops:
  0.6 0.0 copy-start.6
  1.3 0.1 copy-done.6
  1.5 0.0 copy-start.4
  1.5 0.0 copy-start.2
  1.5 0.6 %copy-done.3 = s32[1,12,8]{1,2,0:T(8,128)S(1)} copy-done((s32[1,12,8]{1,2,0:T(8,128)S(1)}, s32[1,12,8]{1,2,0:T(8,128)}, u32[]{:S(2)}) %copy-start.3) | copy-done | bytes 408
  2.2 0.0 copy-done.5
  2.2 0.0 copy-done.4
  2.2 0.0 copy-done.2
  2.2 0.7 %prep.1 = (f32[162,128]{1,0:T(8,128)S(1)}, f32[168,128]{1,0:T(8,128)S(1)}, f32[330,128]{1,0:T(8,128)S(1)}) custom-call(f32[136,128]{1,0:T(8,128)S(1)} %add_bitcast_fusion.2.refs_0_.rows_ref, f32[3,128]{1,0:T(4,128)S(1)} %copy-done.2, s32[6,1,32]{2,1,0:T(1,128)S(1)} %bitcast.25, s32[1,8,12]{2,1,0:T(8,128)S(1)} %bitcast.24, s32[1,2,8]{2,1,0:T(2,128)S(1)} %bitcast.26), custom_call_target="tpu_custom_call" | custom-call | tf_op jit(solution)/shard_map/prep/pallas_call | solution.py:908
  2.9 3.0 %collective-permute-start = (f32[162,128]{1,0:T(8,128)S(1)}, f32[162,128]{1,0:T(8,128)S(1)}, u32[]{:S(2)}, u32[]{:S(2)}) collective-permute-start(f32[162,128]{1,0:T(8,128)S(1)} %get-tuple-element.58), channel_id=1, source_target_pairs={{0,1},{1,0},{2,3},{3,2},{4,5},{5,4},{6,7},{7,6},{8,9},{9,8},{10,11... | collective-permute-start | bytes 248840 | tf_op jit(solution)/shard_map/halo_z/ppermute | solution.py:129
  5.9 0.0 copy-done
  5.9 0.0 copy-done.1
  5.9 2.5 %group_edges.1 = (s32[2,24,128]{2,1,0:T(8,128)S(1)}, s32[2,128]{1,0:T(2,128)S(1)}) custom-call(f32[136,128]{1,0:T(8,128)S(1)} %add_bitcast_fusion.2.refs_0_.rows_ref, s32[48,128]{1,0:T(8,128)S(1)} %bitcast.22, s32[48,128]{1,0:T(8,128)S(1)} %bitcast.23), custom_call_target="tpu_custom_call" | custom-call | tf_op jit(solution)/shard_map/group_edges/pallas_call | solution.py:931
  8.4 0.0 collective-permute-done.refs_1_.refs_3_.refs_8_
  8.5 0.0 copy-start.7
  8.5 0.0 copy-start.10
  8.5 0.0 copy-start.11
  8.5 0.0 copy-start.12
  8.5 4.1 %collective-permute-start.2 = (f32[81,128]{1,0:T(8,128)S(1)}, f32[81,128]{1,0:T(8,128)S(1)}, u32[]{:S(2)}, u32[]{:S(2)}) collective-permute-start(f32[81,128]{1,0:T(8,128)S(1)} %get-tuple-element.123), channel_id=1, source_target_pairs={{0,6},{2,4},{4,2},{6,0},{1,7},{3,5},{5,3},{7,1},{8,14},{10,12},{12... | collective-permute-start | bytes 124424 | tf_op jit(solution)/shard_map/halo_y/ppermute | solution.py:137
  12.6 0.0 collective-permute-start.1
  12.6 0.0 copy-done.7
  12.6 0.0 copy-done.10
  12.6 0.0 copy-done.11
  12.7 0.0 copy-done.12
  12.7 0.6 %copy-done.14 = bf16[128]{0:T(256)(128)(2,1)S(1)} copy-done((bf16[128]{0:T(256)(128)(2,1)S(1)}, bf16[128]{0:T(256)(128)(2,1)}, u32[]{:S(2)}) %copy-start.14) | copy-done | bytes 280
  13.3 0.0 copy-start.13
  13.3 0.8 %copy-done.8 = f32[128,128]{1,0:T(8,128)S(1)} copy-done((f32[128,128]{1,0:T(8,128)S(1)}, f32[128,128]{1,0:T(8,128)}, u32[]{:S(2)}) %copy-start.8) | copy-done | bytes 65560
  14.1 0.0 copy-done.9
  14.2 0.3 weights.1
  14.5 0.3 collective-permute-done.2
  14.8 1.9 %collective-permute-done.1 = f32[81,128]{1,0:T(8,128)S(1)} collective-permute-done((f32[81,128]{1,0:T(8,128)S(1)}, f32[81,128]{1,0:T(8,128)S(1)}, u32[]{:S(2)}, u32[]{:S(2)}) %collective-permute-start.1) | collective-permute-done | bytes 41504 | tf_op jit(solution)/shard_map/halo_y/ppermute | solution.py:136
  16.7 0.1 collective-permute-start.4
  16.8 1.6 %collective-permute-start.3 = (f32[81,128]{1,0:T(8,128)S(1)}, f32[81,128]{1,0:T(8,128)S(1)}, u32[]{:S(2)}, u32[]{:S(2)}) collective-permute-start(f32[81,128]{1,0:T(8,128)S(1)} %get-tuple-element.120), channel_id=1, source_target_pairs={{0,8},{8,0},{16,24},{24,16},{1,9},{9,1},{17,25},{25,17},{2,10},{10... | collective-permute-start | bytes 124424 | tf_op jit(solution)/shard_map/halo_x/ppermute | solution.py:136
  18.4 2.2 %collective-permute-done.4 = f32[81,128]{1,0:T(8,128)S(1)} collective-permute-done((f32[81,128]{1,0:T(8,128)S(1)}, f32[81,128]{1,0:T(8,128)S(1)}, u32[]{:S(2)}, u32[]{:S(2)}) %collective-permute-start.4) | collective-permute-done | bytes 41504 | tf_op jit(solution)/shard_map/halo_x/ppermute | solution.py:137
  20.7 0.0 collective-permute-done.3
  20.7 14.1 %layer.1 = (f32[144,128]{1,0:T(8,128)S(1)}, f32[256,256]{1,0:T(8,128)S(1)}, f32[81,128]{1,0:T(8,128)S(1)}, f32[81,128]{1,0:T(8,128)S(1)}, f32[168,128]{1,0:T(8,128)S(1)}) custom-call(s32[2,128]{1,0:T(2,128)S(1)} %get-tuple-element.61.refs_0_, s32[2,24,128]{2,1,0:T(8,128)S(1)} %get-tuple-element.62.refs_1_, f32[3,128]{1,0:T(4,128)S(1)} %copy-done.2, ...), custom_call_target="tpu_custom_call" | custom-call | tf_op jit(solution)/shard_map/layer/pallas_call | solution.py:1010
  34.8 0.2 collective-permute-start.6
  34.9 1.1 %collective-permute-start.5 = (f32[81,128]{1,0:T(8,128)S(1)}, f32[81,128]{1,0:T(8,128)S(1)}, u32[]{:S(2)}, u32[]{:S(2)}) collective-permute-start(f32[81,128]{1,0:T(8,128)S(1)} %get-tuple-element.116), channel_id=1, source_target_pairs={{0,24},{8,16},{16,8},{24,0},{1,25},{9,17},{17,9},{25,1},{2,26},{10... | collective-permute-start | bytes 124424 | tf_op jit(solution)/shard_map/halo_back/ppermute | solution.py:137
  36.1 0.0 collective-permute-done.6
  36.1 2.3 %collective-permute-done.5 = f32[81,128]{1,0:T(8,128)S(1)} collective-permute-done((f32[81,128]{1,0:T(8,128)S(1)}, f32[81,128]{1,0:T(8,128)S(1)}, u32[]{:S(2)}, u32[]{:S(2)}) %collective-permute-start.5) | collective-permute-done | bytes 41504 | tf_op jit(solution)/shard_map/halo_back/ppermute | solution.py:137
  38.5 0.6 %collective-permute-start.8 = (f32[81,128]{1,0:T(8,128)S(1)}, f32[81,128]{1,0:T(8,128)S(1)}, u32[]{:S(2)}, u32[]{:S(2)}) collective-permute-start(f32[81,128]{1,0:T(8,128)S(1)} %get-tuple-element.111), channel_id=1, source_target_pairs={{0,2},{2,0},{4,6},{6,4},{1,3},{3,1},{5,7},{7,5},{8,10},{10,8},{12,... | collective-permute-start | bytes 124424 | tf_op jit(solution)/shard_map/halo_back/ppermute | solution.py:136
  39.0 1.4 %collective-permute-start.7 = (f32[81,128]{1,0:T(8,128)S(1)}, f32[81,128]{1,0:T(8,128)S(1)}, u32[]{:S(2)}, u32[]{:S(2)}) collective-permute-start(f32[81,128]{1,0:T(8,128)S(1)} %get-tuple-element.112), channel_id=1, source_target_pairs={{0,6},{2,4},{4,2},{6,0},{1,7},{3,5},{5,3},{7,1},{8,14},{10,12},{12... | collective-permute-start | bytes 124424 | tf_op jit(solution)/shard_map/halo_back/ppermute | solution.py:137
  40.4 2.2 %collective-permute-done.8 = f32[81,128]{1,0:T(8,128)S(1)} collective-permute-done((f32[81,128]{1,0:T(8,128)S(1)}, f32[81,128]{1,0:T(8,128)S(1)}, u32[]{:S(2)}, u32[]{:S(2)}) %collective-permute-start.8) | collective-permute-done | bytes 41504 | tf_op jit(solution)/shard_map/halo_back/ppermute | solution.py:136
  42.6 2.4 %collective-permute-done.7 = f32[81,128]{1,0:T(8,128)S(1)} collective-permute-done((f32[81,128]{1,0:T(8,128)S(1)}, f32[81,128]{1,0:T(8,128)S(1)}, u32[]{:S(2)}, u32[]{:S(2)}) %collective-permute-start.7) | collective-permute-done | bytes 41504 | tf_op jit(solution)/shard_map/halo_back/ppermute | solution.py:137
  45.0 1.6 %collective-permute-start.9 = (f32[162,128]{1,0:T(8,128)S(1)}, f32[162,128]{1,0:T(8,128)S(1)}, u32[]{:S(2)}, u32[]{:S(2)}) collective-permute-start(f32[162,128]{1,0:T(8,128)S(1)} %halo_back.3), channel_id=1, source_target_pairs={{0,1},{1,0},{2,3},{3,2},{4,5},{5,4},{6,7},{7,6},{8,9},{9,8},{10,11... | collective-permute-start | bytes 248840 | tf_op jit(solution)/shard_map/halo_back/ppermute | solution.py:129
  46.6 1.1 %own_part.1 = (f32[1,128]{1,0:T(1,128)}, f32[128,128]{1,0:T(8,128)S(1)}, f32[3,128]{1,0:T(4,128)S(1)}) custom-call(f32[144,128]{1,0:T(8,128)S(1)} %get-tuple-element.97.refs_0_, f32[256,256]{1,0:T(8,128)S(1)} %get-tuple-element.98.refs_1_, f32[264,128]{1,0:T(8,128)S(1)} %add_bitcast_fusion.1.wide_ref.refs_3_.refs_2_, ...), custom_call_target="tpu_custom_call" | custom-call | tf_op jit(solution)/shard_map/own_part/pallas_call | solution.py:1028
  47.6 1.9 %collective-permute-done.9.refs_4_ = f32[162,128]{1,0:T(8,128)S(1)} collective-permute-done((f32[162,128]{1,0:T(8,128)S(1)}, f32[162,128]{1,0:T(8,128)S(1)}, u32[]{:S(2)}, u32[]{:S(2)}) %collective-permute-start.9) | collective-permute-done | bytes 82976 | tf_op jit(solution)/shard_map/halo_back/ppermute | solution.py:129
  49.5 1.0 %owner_sums.1 = (f32[3,128]{1,0:T(4,128)}, f32[128,128]{1,0:T(8,128)}) custom-call(f32[330,128]{1,0:T(8,128)S(1)} %get-tuple-element.57.refs_3_.refs_0_, f32[128,128]{1,0:T(8,128)S(1)} %get-tuple-element.104.refs_1_, f32[3,128]{1,0:T(4,128)S(1)} %get-tuple-element.105.refs_2_, f32[264,128]{1,0:T(8,128)S(1)} %add_bitcast_fusion.1.wide_ref.refs_3_.refs_2_, ...), custom_call_target="tpu_custom_call" | custom-call | tf_op jit(solution)/shard_map/owner_sums/pallas_call | solution.py:1040
  (23 shorter events, 0.2 us)
Async XLA Ops:
  0.6 0.8 %copy-start.6 = (f32[128,128]{1,0:T(8,128)S(1)}, f32[128,128]{1,0:T(8,128)}, u32[]{:S(2)}) copy-start(f32[128,128]{1,0:T(8,128)} %param.17) | copy-start | bytes 196612
  1.5 0.7 %copy-start.3 = (s32[1,12,8]{1,2,0:T(8,128)S(1)}, s32[1,12,8]{1,2,0:T(8,128)}, u32[]{:S(2)}) copy-start(s32[1,12,8]{1,2,0:T(8,128)} %param.19) | copy-start | bytes 1156
  1.5 0.7 %copy-start.5 = (s32[1,8,2]{1,2,0:T(2,128)S(1)}, s32[1,8,2]{1,2,0:T(2,128)}, u32[]{:S(2)}) copy-start(s32[1,8,2]{1,2,0:T(2,128)} %param.20) | copy-start | bytes 196
  1.5 0.7 %copy-start.4 = (s32[1,6,32]{2,0,1:T(1,128)S(1)}, s32[1,6,32]{2,0,1:T(1,128)}, u32[]{:S(2)}) copy-start(s32[1,6,32]{2,0,1:T(1,128)} %param.18) | copy-start | bytes 2308
  1.5 0.7 %copy-start.2 = (f32[3,128]{1,0:T(4,128)S(1)}, f32[3,128]{1,0:T(4,128)}, u32[]{:S(2)}) copy-start(f32[3,128]{1,0:T(4,128)} %refs_2_.1) | copy-start | bytes 4612
  2.2 3.7 %copy-start = (s32[6144]{0:T(1024)S(1)}, s32[6144]{0:T(1024)}, u32[]{:S(2)}) copy-start(s32[6144]{0:T(1024)} %param.21) | copy-start | bytes 73732
  2.2 3.7 %copy-start.1 = (s32[6144]{0:T(1024)S(1)}, s32[6144]{0:T(1024)}, u32[]{:S(2)}) copy-start(s32[6144]{0:T(1024)} %param.22) | copy-start | bytes 73732
  2.9 5.6 %collective-permute-start = (f32[162,128]{1,0:T(8,128)S(1)}, f32[162,128]{1,0:T(8,128)S(1)}, u32[]{:S(2)}, u32[]{:S(2)}) collective-permute-start(f32[162,128]{1,0:T(8,128)S(1)} %get-tuple-element.58), channel_id=1, source_target_pairs={{0,1},{1,0},{2,3},{3,2},{4,5},{5,4},{6,7},{7,6},{8,9},{9,8},{10,11... | collective-permute-start | bytes 248840 | tf_op jit(solution)/shard_map/halo_z/ppermute | solution.py:129
  8.5 4.2 %copy-start.7 = (bf16[256,128]{1,0:T(8,128)(2,1)S(1)}, bf16[256,128]{1,0:T(8,128)(2,1)}, u32[]{:S(2)}) copy-start(bf16[256,128]{1,0:T(8,128)(2,1)} %param.30) | copy-start | bytes 196612
  8.5 4.2 %copy-start.10 = (bf16[128,128]{1,0:T(8,128)(2,1)S(1)}, bf16[128,128]{1,0:T(8,128)(2,1)}, u32[]{:S(2)}) copy-start(bf16[128,128]{1,0:T(8,128)(2,1)} %param.29) | copy-start | bytes 98308
  8.5 4.2 %copy-start.11 = (bf16[128,128]{1,0:T(8,128)(2,1)S(1)}, bf16[128,128]{1,0:T(8,128)(2,1)}, u32[]{:S(2)}) copy-start(bf16[128,128]{1,0:T(8,128)(2,1)} %param.28) | copy-start | bytes 98308
  8.5 4.1 %copy-start.12 = (bf16[128,128]{1,0:T(8,128)(2,1)S(1)}, bf16[128,128]{1,0:T(8,128)(2,1)}, u32[]{:S(2)}) copy-start(bf16[128,128]{1,0:T(8,128)(2,1)} %param.27) | copy-start | bytes 98308
  8.5 6.2 %collective-permute-start.2 = (f32[81,128]{1,0:T(8,128)S(1)}, f32[81,128]{1,0:T(8,128)S(1)}, u32[]{:S(2)}, u32[]{:S(2)}) collective-permute-start(f32[81,128]{1,0:T(8,128)S(1)} %get-tuple-element.123), channel_id=1, source_target_pairs={{0,6},{2,4},{4,2},{6,0},{1,7},{3,5},{5,3},{7,1},{8,14},{10,12},{12... | collective-permute-start | bytes 124424 | tf_op jit(solution)/shard_map/halo_y/ppermute | solution.py:137
  12.6 4.0 %collective-permute-start.1 = (f32[81,128]{1,0:T(8,128)S(1)}, f32[81,128]{1,0:T(8,128)S(1)}, u32[]{:S(2)}, u32[]{:S(2)}) collective-permute-start(f32[81,128]{1,0:T(8,128)S(1)} %get-tuple-element.124), channel_id=1, source_target_pairs={{0,2},{2,0},{4,6},{6,4},{1,3},{3,1},{5,7},{7,5},{8,10},{10,8},{12,... | collective-permute-start | bytes 124424 | tf_op jit(solution)/shard_map/halo_y/ppermute | solution.py:136
  12.6 0.7 %copy-start.14 = (bf16[128]{0:T(256)(128)(2,1)S(1)}, bf16[128]{0:T(256)(128)(2,1)}, u32[]{:S(2)}) copy-start(bf16[128]{0:T(256)(128)(2,1)} %param.31) | copy-start | bytes 772
  13.3 0.8 %copy-start.8 = (f32[128,128]{1,0:T(8,128)S(1)}, f32[128,128]{1,0:T(8,128)}, u32[]{:S(2)}) copy-start(f32[128,128]{1,0:T(8,128)} %param.25) | copy-start | bytes 196612
  13.3 0.9 %copy-start.9 = (f32[128,128]{1,0:T(8,128)S(1)}, f32[128,128]{1,0:T(8,128)}, u32[]{:S(2)}) copy-start(f32[128,128]{1,0:T(8,128)} %param.24) | copy-start | bytes 196612
  13.3 0.9 %copy-start.13 = (f32[8,128]{1,0:T(8,128)S(1)}, f32[8,128]{1,0:T(8,128)}, u32[]{:S(2)}) copy-start(f32[8,128]{1,0:T(8,128)} %param.26) | copy-start | bytes 12292
  16.7 3.9 %collective-permute-start.4 = (f32[81,128]{1,0:T(8,128)S(1)}, f32[81,128]{1,0:T(8,128)S(1)}, u32[]{:S(2)}, u32[]{:S(2)}) collective-permute-start(f32[81,128]{1,0:T(8,128)S(1)} %get-tuple-element.119), channel_id=1, source_target_pairs={{0,24},{8,16},{16,8},{24,0},{1,25},{9,17},{17,9},{25,1},{2,26},{10... | collective-permute-start | bytes 124424 | tf_op jit(solution)/shard_map/halo_x/ppermute | solution.py:137
  16.8 3.9 %collective-permute-start.3 = (f32[81,128]{1,0:T(8,128)S(1)}, f32[81,128]{1,0:T(8,128)S(1)}, u32[]{:S(2)}, u32[]{:S(2)}) collective-permute-start(f32[81,128]{1,0:T(8,128)S(1)} %get-tuple-element.120), channel_id=1, source_target_pairs={{0,8},{8,0},{16,24},{24,16},{1,9},{9,1},{17,25},{25,17},{2,10},{10... | collective-permute-start | bytes 124424 | tf_op jit(solution)/shard_map/halo_x/ppermute | solution.py:136
  34.8 1.3 %collective-permute-start.6 = (f32[81,128]{1,0:T(8,128)S(1)}, f32[81,128]{1,0:T(8,128)S(1)}, u32[]{:S(2)}, u32[]{:S(2)}) collective-permute-start(f32[81,128]{1,0:T(8,128)S(1)} %get-tuple-element.115), channel_id=1, source_target_pairs={{0,8},{8,0},{16,24},{24,16},{1,9},{9,1},{17,25},{25,17},{2,10},{10... | collective-permute-start | bytes 124424 | tf_op jit(solution)/shard_map/halo_back/ppermute | solution.py:136
  34.9 3.5 %collective-permute-start.5 = (f32[81,128]{1,0:T(8,128)S(1)}, f32[81,128]{1,0:T(8,128)S(1)}, u32[]{:S(2)}, u32[]{:S(2)}) collective-permute-start(f32[81,128]{1,0:T(8,128)S(1)} %get-tuple-element.116), channel_id=1, source_target_pairs={{0,24},{8,16},{16,8},{24,0},{1,25},{9,17},{17,9},{25,1},{2,26},{10... | collective-permute-start | bytes 124424 | tf_op jit(solution)/shard_map/halo_back/ppermute | solution.py:137
  38.5 4.1 %collective-permute-start.8 = (f32[81,128]{1,0:T(8,128)S(1)}, f32[81,128]{1,0:T(8,128)S(1)}, u32[]{:S(2)}, u32[]{:S(2)}) collective-permute-start(f32[81,128]{1,0:T(8,128)S(1)} %get-tuple-element.111), channel_id=1, source_target_pairs={{0,2},{2,0},{4,6},{6,4},{1,3},{3,1},{5,7},{7,5},{8,10},{10,8},{12,... | collective-permute-start | bytes 124424 | tf_op jit(solution)/shard_map/halo_back/ppermute | solution.py:136
  39.0 5.9 %collective-permute-start.7 = (f32[81,128]{1,0:T(8,128)S(1)}, f32[81,128]{1,0:T(8,128)S(1)}, u32[]{:S(2)}, u32[]{:S(2)}) collective-permute-start(f32[81,128]{1,0:T(8,128)S(1)} %get-tuple-element.112), channel_id=1, source_target_pairs={{0,6},{2,4},{4,2},{6,0},{1,7},{3,5},{5,3},{7,1},{8,14},{10,12},{12... | collective-permute-start | bytes 124424 | tf_op jit(solution)/shard_map/halo_back/ppermute | solution.py:137
  45.0 4.6 %collective-permute-start.9 = (f32[162,128]{1,0:T(8,128)S(1)}, f32[162,128]{1,0:T(8,128)S(1)}, u32[]{:S(2)}, u32[]{:S(2)}) collective-permute-start(f32[162,128]{1,0:T(8,128)S(1)} %halo_back.3), channel_id=1, source_target_pairs={{0,1},{1,0},{2,3},{3,2},{4,5},{5,4},{6,7},{7,6},{8,9},{9,8},{10,11... | collective-permute-start | bytes 248840 | tf_op jit(solution)/shard_map/halo_back/ppermute | solution.py:129
